TPU v7x, 32 devices: a whole 2x2x4 slice. The times are simulated.
32 devices in a mesh: paths: 2 (over x), hi: 16 (over z, y, core).
Axes of the slice: x: 2, y: 2, z: 4, core: 2. Of those that a mesh axis runs over, the one named last changes fastest.
Arguments:
- amplitudes: float32 [2, 2097152], P(None, ('paths', 'hi')), parts along dimension 1, may hold values from -6 to 6
- gate_matrices: bfloat16 [6, 2, 128, 128], replicated, may hold values from -0.375 to 0.375
- phase_qubits: int32 [12, 8, 2], P('paths'), parts along dimension 0, may hold values from 0 to 19
- phase_angles: float32 [12, 8], P('paths'), parts along dimension 0, may hold values from -3.140625 to 3.140625
- cut_qubits: int32 [12, 2], P('paths'), parts along dimension 0, may hold values from 0 to 19
- cut_angle: float32 [12], P('paths'), parts along dimension 0, may hold values from 0.6 to 0.97
- path_index: int32 [12], P('paths'), parts along dimension 0, may hold values from 0 to 1
Outputs:
- final_state: float32 [2, 2097152], P(None, ('paths', 'hi')), parts along dimension 1
There are 2 independent parts, one for each index of `paths`. A program takes and returns all parts, laid end to end along the dimension named above; an argument that names none is the same for every part. Nothing has to cross between parts.
All inputs are finite; a program needn't handle non-finite values.
Results may differ from a plain program's by a relative error of at most 0.0003.
Values sent between devices are 32-bit elements; how exact they have to be, the bound alone decides.
No kernel may reach another device: no remote copies, remote signals or barrier semaphores. Data moves between devices by JAX's collectives and lax.ppermute only.
A program may use at most 64 MiB of HBM per device.

v0:
```python
import functools

import jax
import jax.numpy as jnp
import numpy as np
from jax import lax
from jax.experimental import pallas as pl
from jax.experimental.pallas import tpu as pltpu
from jax.sharding import PartitionSpec as P

LANE_BITS = 7
GATE_BITS = 6


def fitted(function, degree):
    nodes = np.cos(np.pi * (np.arange(64) + 0.5) / 64) * 0.125 + 0.125
    series = np.polynomial.chebyshev.Chebyshev.fit(nodes, function(np.sqrt(nodes)), degree, domain=[0, 0.25])
    return [float(c) for c in series.convert(kind=np.polynomial.Polynomial).coef]


COS_TERMS = fitted(lambda v: np.cos(2 * np.pi * v), 7)
SIN_TERMS = fitted(lambda v: np.sin(2 * np.pi * v) / v, 6)


def horner(terms, w):
    total = jnp.full_like(w, terms[-1])
    for term in terms[-2::-1]:
        total = total * w + term
    return total


def turn(angle):
    part = angle - jnp.round(angle)
    square = part * part
    return horner(COS_TERMS, square), part * horner(SIN_TERMS, square)


class Plan:
    def __init__(self, global_count, local_bits, layers):
        self.global_count, self.local_bits, self.layers = global_count, local_bits, layers
        self.top = top = local_bits - global_count
        place = {}
        for label in range(local_bits + global_count):
            if label < top:
                place[label] = label
            elif label < local_bits:
                place[label] = label + global_count
            else:
                place[label] = label - global_count
        held = list(range(local_bits + global_count))
        self.targets = []
        for layer in range(layers):
            if layer < global_count:
                low, high = 7 + layer, local_bits + layer
                held[low], held[high] = held[high], held[low]
                target = low
            else:
                if layer == global_count:
                    held = held[:top] + held[local_bits:] + held[top:local_bits]
                target = local_bits - 2 * global_count + layer
            self.targets.append(place[held[target]])
        assert all(LANE_BITS <= bit < local_bits for bit in self.targets)
        ends = [place[label] for label in held]
        self.extra = sum(ends[local_bits + k] != local_bits + k for k in range(global_count))
        swapped = ends[:]
        for k in range(self.extra):
            low, high = local_bits - self.extra + k, local_bits + k
            assert ends[low] == high
            swapped[low], swapped[high] = ends[high], ends[low]
        assert swapped[local_bits:] == list(range(local_bits, local_bits + global_count))
        assert swapped[:LANE_BITS] == list(range(LANE_BITS))
        self.wanted = swapped[LANE_BITS:local_bits]
        self.orders, self.steps = [], []
        order = list(range(LANE_BITS, local_bits))
        for layer, target in enumerate(self.targets):
            step = 0
            if target in order[:3]:
                def lasts(at):
                    triple = order[at:at + 3]
                    if triple == self.wanted[:3] and not set(triple) & set(self.targets[layer:]):
                        return layers + 1
                    return next((k for k, bit in enumerate(self.targets[layer:]) if bit in triple), layers)
                step = max(range(1, len(order) - 2), key=lasts)
                triple = order[step:step + 3]
                assert target not in triple
                if triple == self.wanted[:3]:
                    order = self.wanted
                else:
                    order = triple + [bit for bit in order if bit not in triple]
            self.steps.append(step)
            self.orders.append(order)

    def locate(self, qubit, layer):
        low, count = 7, min(layer + 1, self.global_count)
        size, high = self.global_count, self.local_bits
        if layer >= size:
            qubit = jnp.where(qubit >= high, qubit - size, jnp.where(qubit >= self.top, qubit + size, qubit))
        up = (qubit >= low) & (qubit < low + count)
        down = (qubit >= high) & (qubit < high + count)
        label = jnp.where(up, qubit + (high - low), jnp.where(down, qubit - (high - low), qubit))
        return jnp.where(label >= high, label - size, jnp.where(label >= self.top, label + size, label))


def tables_kernel(plan, rows, gates, pair_qubits, pair_angles, cut_qubits, cut_angle, path_index,
                  weights, cosines, sines):
    device_part = lax.axis_index("hi") << plan.local_bits
    lane = lax.broadcasted_iota(jnp.int32, (128, 128), 1)
    for layer in range(plan.layers):
        turned = [gates[layer, part].astype(jnp.float32).T for part in range(2)]
        for from_part in range(2):
            for to_part in range(2):
                block = turned[from_part ^ to_part]
                if (from_part, to_part) == (1, 0):
                    block = -block
                for to_bit in range(2):
                    kept = jnp.where((lane >= 64) == (to_bit == 1), block, 0.0)
                    moved = pltpu.roll(kept, 64, 1)
                    first, second = (kept, moved) if to_bit == 0 else (moved, kept)
                    for from_bit in range(2):
                        part = slice(64 * from_bit, 64 * from_bit + 64)
                        both = jnp.concatenate([first[part], second[part]], axis=0)
                        at_row, at_col = 256 * from_part + 128 * from_bit, 256 * to_part + 128 * to_bit
                        weights[layer, at_row:at_row + 128, at_col:at_col + 128] = both.astype(jnp.bfloat16)

    block_rows = 64
    block_bits = block_rows.bit_length() - 1
    row = lax.broadcasted_iota(jnp.int32, (block_rows, 128), 0)
    lanes = lax.broadcasted_iota(jnp.int32, (block_rows, 128), 1)
    for layer in range(plan.layers):
        order = plan.orders[layer]
        base = lanes + device_part
        for bit in range(block_bits):
            base = base + (((row >> bit) & 1) << order[bit])
        masks, turns = [], []
        for pair in range(pair_qubits.shape[1]):
            first = plan.locate(pair_qubits[layer, pair, 0], layer)
            second = plan.locate(pair_qubits[layer, pair, 1], layer)
            one = jnp.int32(1)
            masks.append((one << first) | (one << second))
            turns.append(pair_angles[layer, pair] * np.float32(0.5 / np.pi))
        if layer == 0:
            size = jnp.ones((8, 128), jnp.float32)
            cut_masks, cut_turns = [], []
            for cut in range(cut_qubits.shape[0]):
                first = plan.locate(cut_qubits[cut, 0], layer)
                second = plan.locate(cut_qubits[cut, 1], layer)
                one = jnp.int32(1)
                cut_masks.append((one << first) | (one << second))
                chosen = path_index[cut] == 0
                cosine, sine = turn(jnp.full((8, 128), cut_angle[cut] * np.float32(0.5 / np.pi)))
                size = size * jnp.where(chosen, cosine, sine)
                cut_turns.append(jnp.where(chosen, 0.0, 0.25))
            size = jnp.broadcast_to(size[:1], (block_rows, 128))

        @pl.loop(0, rows // block_rows)
        def _(block):
            offset = jnp.int32(0)
            for bit in range(block_bits, len(order)):
                offset = offset + (((block >> (bit - block_bits)) & 1) << order[bit])
            index = base + offset
            angle = jnp.zeros((block_rows, 128), jnp.float32)
            for mask, amount in zip(masks, turns):
                angle = angle + jnp.where((index & mask) == mask, amount, 0.0)
            if layer == 0:
                for mask, amount in zip(cut_masks, cut_turns):
                    both = index & mask
                    angle = angle + jnp.where((both == 0) | (both == mask), -amount, amount)
            cosine, sine = turn(angle)
            if layer == 0:
                cosine, sine = cosine * size, sine * size
            at = pl.ds(pl.multiple_of(block * block_rows, block_rows), block_rows)
            cosines[layer, at, :] = cosine
            sines[layer, at, :] = sine


def offset_of(number, bits, order):
    return sum(((number >> k) & 1) << order.index(bit) for k, bit in enumerate(bits))


def layers_kernel(plan, rows, state, weights, cosines, sines, out, held):
    order = list(range(LANE_BITS, plan.local_bits))
    for layer in range(plan.layers):
        new_order, step, target = plan.orders[layer], plan.steps[layer], plan.targets[layer]
        rest = [bit for bit in new_order if bit != target]
        pieces = []
        for part in range(2):
            for side in range(2):
                tiles = []
                for tile in range(rows // 16):
                    at = offset_of(tile, rest[3:], order) + side * (1 << order.index(target))
                    if layer == 0:
                        tiles.append(state[pl.ds(2 * at + part, 8, 2 << step), :])
                    elif step:
                        tiles.append(held[(layer - 1) % 2, part, pl.ds(at, 8, 1 << step), :])
                    else:
                        tiles.append(held[(layer - 1) % 2, part, pl.ds(at, 8), :])
                pieces.append(jnp.concatenate(tiles, axis=0))
        joined = jnp.concatenate(pieces, axis=1)
        large = joined.astype(jnp.bfloat16)
        small = (joined - large.astype(jnp.float32)).astype(jnp.bfloat16)
        both = jnp.dot(jnp.concatenate([large, small], axis=0), weights[layer],
                       preferred_element_type=jnp.float32)
        result = both[:rows // 2] + both[rows // 2:]
        for side in range(2):
            for tile in range(rows // 16):
                at = offset_of(tile, rest[3:], new_order) + side * (1 << new_order.index(target))
                real = result[8 * tile:8 * tile + 8, 128 * side:128 * side + 128]
                imag = result[8 * tile:8 * tile + 8, 256 + 128 * side:384 + 128 * side]
                cosine, sine = cosines[layer, at:at + 8, :], sines[layer, at:at + 8, :]
                new_real, new_imag = cosine * real - sine * imag, sine * real + cosine * imag
                if layer == plan.layers - 1:
                    out[pl.ds(2 * at, 8, 2), :] = new_real
                    out[pl.ds(2 * at + 1, 8, 2), :] = new_imag
                else:
                    held[layer % 2, 0, at:at + 8, :] = new_real
                    held[layer % 2, 1, at:at + 8, :] = new_imag
        order = new_order


def shards(
    amplitudes, gate_matrices, phase_qubits, phase_angles, cut_qubits, cut_angle, path_index
):
    devices = lax.axis_size("hi")
    global_count = devices.bit_length() - 1
    amp_count = amplitudes.shape[1]
    rows = amp_count >> LANE_BITS
    layers = gate_matrices.shape[0]
    plan = Plan(global_count, amp_count.bit_length() - 1, layers)

    sent = amplitudes.reshape(2, rows, 128).transpose(1, 0, 2).reshape(devices, -1, 128)
    came = lax.all_to_all(sent, "hi", split_axis=0, concat_axis=0, tiled=True).reshape(2 * rows, 128)

    vmem, smem = pl.BlockSpec(memory_space=pltpu.VMEM), pl.BlockSpec(memory_space=pltpu.SMEM)
    table = jax.ShapeDtypeStruct((layers, rows, 128), jnp.float32)
    weights, cosines, sines = pl.pallas_call(
        functools.partial(tables_kernel, plan, rows),
        out_shape=(jax.ShapeDtypeStruct((layers, 512, 512), jnp.bfloat16), table, table),
        in_specs=[vmem] + [smem] * 5,
        out_specs=[vmem] * 3,
        cost_estimate=pl.CostEstimate(flops=100 * layers * amp_count, bytes_accessed=4 * layers * amp_count, transcendentals=0),
        compiler_params=pltpu.CompilerParams(vmem_limit_bytes=40 << 20),
        name="tables",
    )(gate_matrices, phase_qubits, phase_angles, cut_qubits, cut_angle, path_index)

    result = pl.pallas_call(
        functools.partial(layers_kernel, plan, rows),
        out_shape=jax.ShapeDtypeStruct((2 * rows, 128), jnp.float32),
        in_specs=[vmem] * 4,
        out_specs=vmem,
        scratch_shapes=[pltpu.VMEM((2, 2, rows, 128), jnp.float32)],
        compiler_params=pltpu.CompilerParams(vmem_limit_bytes=40 << 20),
        name="layers",
    )(came, weights, cosines, sines)

    if plan.orders[-1] != plan.wanted:
        bits = len(plan.wanted)
        shaped = result.reshape((2,) * bits + (2, 128))
        axes = [bits - 1 - plan.orders[-1].index(plan.wanted[bits - 1 - axis]) for axis in range(bits)]
        result = shaped.transpose(axes + [bits, bits + 1]).reshape(2 * rows, 128)
    if plan.extra:
        size = 1 << plan.extra
        groups = [list(range(first, first + size)) for first in range(0, devices, size)]
        result = lax.all_to_all(
            result.reshape(size, -1, 128), "hi", split_axis=0, concat_axis=0,
            axis_index_groups=groups, tiled=True,
        )
    return result.reshape(rows, 2, 128).transpose(1, 0, 2).reshape(2, amp_count)


def solution(mesh):
    placed = (
        P(None, ("paths", "hi")),
        P(),
        P("paths", None, None),
        P("paths", None),
        P("paths", None),
        P("paths"),
        P("paths"),
    )
    return jax.shard_map(
        shards, mesh=mesh, in_specs=placed, out_specs=P(None, ("paths", "hi")), check_vma=False
    )
```

profile of v0, /device:TPU:0, one launch (start us, length us, event | category | flops | bytes accessed | tf_op | source)
XLA Modules:
  0.0 31.4 jit_solution(1710001912303221554)
XLA Ops:
  0.0 0.0 copy-start.10
  0.0 0.0 copy-start.9
  0.0 0.0 copy-start.8
  0.0 1.1 %copy.14 = f32[1,2,512,128]{3,2,1,0:T(8,128)S(1)} copy(f32[1,2,512,128]{3,1,2,0:T(2,128)} %bitcast.15) | data formatting | bytes 1048576
  1.2 1.2 %copy.8 = f32[512,2,128]{2,1,0:T(2,128)} copy(f32[512,2,128]{2,0,1:T(8,128)S(1)} %bitcast.14) | data formatting | bytes 1048576 | tf_op jit(solution)/shard_map/transpose | solution.py:230
  2.4 7.4 %all-to-all-start = ((f32[16,64,128]{2,1,0:T(8,128)}), f32[16,64,128]{2,1,0:T(8,128)}, u32[]{:S(2)}, u32[]{:S(2)}) async-start(f32[16,64,128]{2,1,0:T(8,128)} %bitcast.1), calls=%async_computation | async-start | bytes 1048576 | tf_op jit(solution)/shard_map/all_to_all | solution.py:231
  9.8 0.0 copy-done.10
  9.8 0.1 copy.10.cut_qubits
  9.9 0.0 copy-done.9
  9.9 0.7 %copy.9.pair_qubits = s32[6,8,2]{2,1,0:T(8,128)} copy(s32[6,8,2]{1,2,0:T(2,128)S(1)} %copy-done.9) | data formatting | bytes 768 | tf_op args[2]
  10.6 0.0 copy-done.4
  10.6 0.0 copy-done.6
  10.6 0.0 copy-done.7
  10.6 0.0 copy-done.8
  10.6 0.0 copy-start.5
  10.7 0.7 %copy-done.5 = s32[6,8,2]{2,1,0:T(8,128)S(1)} copy-done((s32[6,8,2]{2,1,0:T(8,128)S(1)}, s32[6,8,2]{2,1,0:T(8,128)}, u32[]{:S(2)}) %copy-start.5) | copy-done | bytes 408
  11.4 6.4 %tables.1 = (bf16[6,512,512]{2,1,0:T(8,128)(2,1)S(1)}, f32[6,512,128]{2,1,0:T(8,128)S(1)}, f32[6,512,128]{2,1,0:T(8,128)S(1)}) custom-call(bf16[6,2,128,128]{3,2,1,0:T(8,128)(2,1)S(1)} %copy-done.4, s32[6,8,2]{2,1,0:T(8,128)S(1)} %copy-done.5, f32[6,8]{1,0:T(8,128)S(1)} %copy-done.6, s32[6,2]{1,0:T(8,128)S(1)} %copy.10.cut_qubits, f32[6]{0:T(128)S(1)} %copy-done.7, ...), custom_call_target="tpu_custom_call" | custom-call | flops 39321600 | bytes 1572864 | tf_op jit(solution)/shard_map/tables/pallas_call | solution.py:235
  17.8 0.0 copy-start
  17.8 1.2 %copy-done = f32[6,512,128]{2,1,0:T(8,128)} copy-done((f32[6,512,128]{2,1,0:T(8,128)}, f32[6,512,128]{2,1,0:T(8,128)S(1)}, u32[]{:S(2)}) %copy-start) | copy-done | bytes 1572888
  19.0 1.1 %copy-done.2 = f32[6,512,128]{2,1,0:T(8,128)} copy-done((f32[6,512,128]{2,1,0:T(8,128)}, f32[6,512,128]{2,1,0:T(8,128)S(1)}, u32[]{:S(2)}) %copy-start.2) | copy-done | bytes 1572888
  20.1 4.2 %all-to-all-done = f32[16,64,128]{2,1,0:T(8,128)} async-done(((f32[16,64,128]{2,1,0:T(8,128)}), f32[16,64,128]{2,1,0:T(8,128)}, u32[]{:S(2)}, u32[]{:S(2)}) %all-to-all-start) | async-done | bytes 524320 | tf_op jit(solution)/shard_map/all_to_all | solution.py:231
  24.3 1.4 %copy-done.1 = f32[6,512,128]{2,1,0:T(8,128)S(1)} copy-done((f32[6,512,128]{2,1,0:T(8,128)S(1)}, f32[6,512,128]{2,1,0:T(8,128)}, u32[]{:S(2)}) %copy-start.1) | copy-done | bytes 1572888
  25.7 1.4 %copy-done.3 = f32[6,512,128]{2,1,0:T(8,128)S(1)} copy-done((f32[6,512,128]{2,1,0:T(8,128)S(1)}, f32[6,512,128]{2,1,0:T(8,128)}, u32[]{:S(2)}) %copy-start.3) | copy-done | bytes 1572888
  27.2 4.3 %layers.1 = f32[1024,128]{1,0:T(8,128)} custom-call(f32[1024,128]{1,0:T(8,128)} %bitcast.2.state, bf16[6,512,512]{2,1,0:T(8,128)(2,1)S(1)} %get-tuple-element.8.weights, f32[6,512,128]{2,1,0:T(8,128)S(1)} %copy-done.1, f32[6,512,128]{2,1,0:T(8,128)S(1)} %copy-done.3), custom_call_target="tpu_custom_call" | custom-call | tf_op jit(solution)/shard_map/layers/pallas_call | solution.py:245
  (6 shorter events, 0.0 us)
Async XLA Ops:
  0.0 9.8 %copy-start.10 = (s32[6,2]{0,1:T(2,128)S(1)}, s32[6,2]{0,1:T(2,128)}, u32[]{:S(2)}) copy-start(s32[6,2]{0,1:T(2,128)} %param.11) | copy-start | bytes 148
  0.0 9.9 %copy-start.9 = (s32[6,8,2]{1,2,0:T(2,128)S(1)}, s32[6,8,2]{1,2,0:T(2,128)}, u32[]{:S(2)}) copy-start(s32[6,8,2]{1,2,0:T(2,128)} %param.9) | copy-start | bytes 1156
  0.0 10.6 %copy-start.4 = (bf16[6,2,128,128]{3,2,1,0:T(8,128)(2,1)S(1)}, bf16[6,2,128,128]{3,2,1,0:T(8,128)(2,1)}, u32[]{:S(2)}) copy-start(bf16[6,2,128,128]{3,2,1,0:T(8,128)(2,1)} %gates.1) | copy-start | bytes 1179652
  0.0 10.6 %copy-start.6 = (f32[6,8]{1,0:T(8,128)S(1)}, f32[6,8]{1,0:T(8,128)}, u32[]{:S(2)}) copy-start(f32[6,8]{1,0:T(8,128)} %pair_angles.1) | copy-start | bytes 580
  0.0 10.6 %copy-start.7 = (f32[6]{0:T(128)S(1)}, f32[6]{0:T(128)}, u32[]{:S(2)}) copy-start(f32[6]{0:T(128)} %cut_angle.1) | copy-start | bytes 76
  0.0 10.6 %copy-start.8 = (s32[6]{0:T(128)S(1)}, s32[6]{0:T(128)}, u32[]{:S(2)}) copy-start(s32[6]{0:T(128)} %path_index.1) | copy-start | bytes 76
  2.4 22.0 %all-to-all-start = ((f32[16,64,128]{2,1,0:T(8,128)}), f32[16,64,128]{2,1,0:T(8,128)}, u32[]{:S(2)}, u32[]{:S(2)}) async-start(f32[16,64,128]{2,1,0:T(8,128)} %bitcast.1), calls=%async_computation | async-start | bytes 1048576 | tf_op jit(solution)/shard_map/all_to_all | solution.py:231
  10.6 0.7 %copy-start.5 = (s32[6,8,2]{2,1,0:T(8,128)S(1)}, s32[6,8,2]{2,1,0:T(8,128)}, u32[]{:S(2)}) copy-start(s32[6,8,2]{2,1,0:T(8,128)} %copy.9.pair_qubits) | copy-start | bytes 1156
  17.8 1.2 %copy-start = (f32[6,512,128]{2,1,0:T(8,128)}, f32[6,512,128]{2,1,0:T(8,128)S(1)}, u32[]{:S(2)}) copy-start(f32[6,512,128]{2,1,0:T(8,128)S(1)} %get-tuple-element.9.cosines) | copy-start | bytes 4718596
  19.0 1.1 %copy-start.2 = (f32[6,512,128]{2,1,0:T(8,128)}, f32[6,512,128]{2,1,0:T(8,128)S(1)}, u32[]{:S(2)}) copy-start(f32[6,512,128]{2,1,0:T(8,128)S(1)} %get-tuple-element.10.sines) | copy-start | bytes 4718596
  24.3 1.4 %copy-start.1 = (f32[6,512,128]{2,1,0:T(8,128)S(1)}, f32[6,512,128]{2,1,0:T(8,128)}, u32[]{:S(2)}) copy-start(f32[6,512,128]{2,1,0:T(8,128)} %copy-done) | copy-start | bytes 4718596
  25.7 1.4 %copy-start.3 = (f32[6,512,128]{2,1,0:T(8,128)S(1)}, f32[6,512,128]{2,1,0:T(8,128)}, u32[]{:S(2)}) copy-start(f32[6,512,128]{2,1,0:T(8,128)} %copy-done.2) | copy-start | bytes 4718596
where the time goes:
time: 31.8 us; the launch traced here: 31.4 us
  Pallas kernels  10.7 us (34%)
  local copies, waits for them, and re-layouts  9 us (28%)
  starting transfers between devices  7.45 us (23%)
  waiting for transfers between devices  4.2 us (13%)
    unnamed x25, local copies, waits for them, and re-layouts  7.8 us
    all_to_all x1, starting transfers between devices, shards(): lax.all_to_all(sent, 'hi', split_axis=0, concat_axis=0, tiled=True)  7.45 us
    pallas_call x1, Pallas kernels, shards(): pl.pallas_call(functools.partial(tables_kernel, plan, rows), out_shape=(j...  6.43 us
    pallas_call x1, Pallas kernels, shards(): pl.pallas_call(functools.partial(layers_kernel, plan, rows), out_shape=ja...  4.27 us
    all_to_all x1, waiting for transfers between devices, shards(): lax.all_to_all(sent, 'hi', split_axis=0, concat_axis=0, tiled=True)  4.2 us
    transpose x1, local copies, waits for them, and re-layouts, shards(): amplitudes.reshape(2, rows, 128).transpose(1, 0, 2)  1.2 us
  transfers between devices with their start and end apart: 1, of which 1 were waited for; matrix products, arithmetic and copies ran while one was open for 3% of the time, Pallas kernels for 20%

commit v1 on v0

--- a/solution.py
+++ b/solution.py
@@ -5,6 +5,7 @@
 import numpy as np
 from jax import lax
 from jax.experimental import pallas as pl
+from jax.experimental.layout import Layout, with_layout_constraint
 from jax.experimental.pallas import tpu as pltpu
 from jax.sharding import PartitionSpec as P
 
@@ -132,18 +133,18 @@
         for bit in range(block_bits):
             base = base + (((row >> bit) & 1) << order[bit])
         masks, turns = [], []
-        for pair in range(pair_qubits.shape[1]):
-            first = plan.locate(pair_qubits[layer, pair, 0], layer)
-            second = plan.locate(pair_qubits[layer, pair, 1], layer)
+        for pair in range(pair_qubits.shape[2]):
+            first = plan.locate(pair_qubits[layer, 0, pair], layer)
+            second = plan.locate(pair_qubits[layer, 1, pair], layer)
             one = jnp.int32(1)
             masks.append((one << first) | (one << second))
             turns.append(pair_angles[layer, pair] * np.float32(0.5 / np.pi))
         if layer == 0:
             size = jnp.ones((8, 128), jnp.float32)
             cut_masks, cut_turns = [], []
-            for cut in range(cut_qubits.shape[0]):
-                first = plan.locate(cut_qubits[cut, 0], layer)
-                second = plan.locate(cut_qubits[cut, 1], layer)
+            for cut in range(cut_qubits.shape[1]):
+                first = plan.locate(cut_qubits[0, cut], layer)
+                second = plan.locate(cut_qubits[1, cut], layer)
                 one = jnp.int32(1)
                 cut_masks.append((one << first) | (one << second))
                 chosen = path_index[cut] == 0
@@ -177,7 +178,15 @@
     return sum(((number >> k) & 1) << order.index(bit) for k, bit in enumerate(bits))
 
 
-def layers_kernel(plan, rows, state, weights, cosines, sines, out, held):
+def layers_kernel(plan, rows, count, *refs):
+    pieces, (weights, cosines, sines, out, held, state) = refs[:count], refs[count:]
+    if count == 1:
+        state = pieces[0]
+    else:
+        size = pieces[0].shape[0]
+        for number, piece in enumerate(pieces):
+            place = lax.axis_index("hi") ^ number
+            state[pl.ds(pl.multiple_of(place * size, size), size), :] = piece[...]
     order = list(range(LANE_BITS, plan.local_bits))
     for layer in range(plan.layers):
         new_order, step, target = plan.orders[layer], plan.steps[layer], plan.targets[layer]
@@ -227,8 +236,16 @@
     layers = gate_matrices.shape[0]
     plan = Plan(global_count, amp_count.bit_length() - 1, layers)
 
-    sent = amplitudes.reshape(2, rows, 128).transpose(1, 0, 2).reshape(devices, -1, 128)
-    came = lax.all_to_all(sent, "hi", split_axis=0, concat_axis=0, tiled=True).reshape(2 * rows, 128)
+    shaped = with_layout_constraint(amplitudes.reshape(2, rows, 128), Layout(major_to_minor=(1, 0, 2)))
+    sent = shaped.transpose(1, 0, 2).reshape(devices, -1, 128)
+    if devices <= 32:
+        place = lax.axis_index("hi")
+        pieces = [lax.dynamic_index_in_dim(sent, place ^ k, keepdims=False) for k in range(devices)]
+        for k in range(devices - 1, 0, -1):
+            pieces[k] = lax.ppermute(pieces[k], "hi", [(i, i ^ k) for i in range(devices)])
+    else:
+        came = lax.all_to_all(sent, "hi", split_axis=0, concat_axis=0, tiled=True)
+        pieces = [came.reshape(2 * rows, 128)]
 
     vmem, smem = pl.BlockSpec(memory_space=pltpu.VMEM), pl.BlockSpec(memory_space=pltpu.SMEM)
     table = jax.ShapeDtypeStruct((layers, rows, 128), jnp.float32)
@@ -238,19 +255,19 @@
         in_specs=[vmem] + [smem] * 5,
         out_specs=[vmem] * 3,
         cost_estimate=pl.CostEstimate(flops=100 * layers * amp_count, bytes_accessed=4 * layers * amp_count, transcendentals=0),
-        compiler_params=pltpu.CompilerParams(vmem_limit_bytes=40 << 20),
+        compiler_params=pltpu.CompilerParams(vmem_limit_bytes=24 << 20),
         name="tables",
-    )(gate_matrices, phase_qubits, phase_angles, cut_qubits, cut_angle, path_index)
+    )(gate_matrices, phase_qubits.transpose(0, 2, 1), phase_angles, cut_qubits.T, cut_angle, path_index)
 
     result = pl.pallas_call(
-        functools.partial(layers_kernel, plan, rows),
+        functools.partial(layers_kernel, plan, rows, len(pieces)),
         out_shape=jax.ShapeDtypeStruct((2 * rows, 128), jnp.float32),
-        in_specs=[vmem] * 4,
+        in_specs=[vmem] * (len(pieces) + 3),
         out_specs=vmem,
-        scratch_shapes=[pltpu.VMEM((2, 2, rows, 128), jnp.float32)],
-        compiler_params=pltpu.CompilerParams(vmem_limit_bytes=40 << 20),
+        scratch_shapes=[pltpu.VMEM((2, 2, rows, 128), jnp.float32), pltpu.VMEM((2 * rows, 128), jnp.float32)],
+        compiler_params=pltpu.CompilerParams(vmem_limit_bytes=24 << 20),
         name="layers",
-    )(came, weights, cosines, sines)
+    )(*pieces, weights, cosines, sines)
 
     if plan.orders[-1] != plan.wanted:
         bits = len(plan.wanted)

time: 31.8 us -> 38.1 us (1.20)
  starting transfers between devices: 7.45 us -> 22.1 us
  local copies, waits for them, and re-layouts: 9 us -> 5.4 us
  waiting for transfers between devices: 4.2 us -> 0.81 us
  Pallas kernels: 10.7 us -> 9.33 us
    ppermute x0 -> x15, starting transfers between devices: none -> 22.1 us  [shards(): lax.ppermute(pieces[k], 'hi', [(i, i ^ k) for i in range(devices)])]
    all_to_all x1 -> x0, starting transfers between devices: 7.45 us -> none  [shards(): lax.all_to_all(sent, 'hi', split_axis=0, concat_axis=0, tiled=True)]
    all_to_all x1 -> x0, waiting for transfers between devices: 4.2 us -> none  [shards(): lax.all_to_all(sent, 'hi', split_axis=0, concat_axis=0, tiled=True)]
    unnamed x25 -> x12, local copies, waits for them, and re-layouts: 7.8 us -> 4.36 us
    transpose x1 -> x0, local copies, waits for them, and re-layouts: 1.2 us -> none  [shards(): amplitudes.reshape(2, rows, 128).transpose(1, 0, 2)]
    squeeze x0 -> x1, local copies, waits for them, and re-layouts: none -> 1.04 us  [shards(): lax.dynamic_index_in_dim(sent, place ^ k, keepdims=False)]
    pallas_call x1, Pallas kernels: 4.27 us -> 3.26 us  [shards(): pl.pallas_call(functools.partial(layers_kernel, plan, rows, len(pieces)),...]
    ppermute x0 -> x15, waiting for transfers between devices: none -> 0.81 us  [shards(): lax.ppermute(pieces[k], 'hi', [(i, i ^ k) for i in range(devices)])]
  transfers between devices with their start and end apart: 1 -> 15, of which waited for: 1 -> 1; matrix products, arithmetic and copies ran while one was open for 3% -> 0% of each run, Pallas kernels for 20% -> 16%
where the time goes in v1:
time: 38.1 us; the launch traced here: 37.7 us
  starting transfers between devices  22.1 us (58%)
  Pallas kernels  9.33 us (24%)
  local copies, waits for them, and re-layouts  5.4 us (14%)
  waiting for transfers between devices  0.81 us (2%)
    ppermute x15, starting transfers between devices, shards(): lax.ppermute(pieces[k], 'hi', [(i, i ^ k) for i in range(devices)])  22.1 us
    pallas_call x1, Pallas kernels, shards(): pl.pallas_call(functools.partial(tables_kernel, plan, rows), out_shape=(j...  6.08 us
    unnamed x12, local copies, waits for them, and re-layouts  4.36 us
    pallas_call x1, Pallas kernels, shards(): pl.pallas_call(functools.partial(layers_kernel, plan, rows, len(pieces)),...  3.26 us
    squeeze x1, local copies, waits for them, and re-layouts, shards(): lax.dynamic_index_in_dim(sent, place ^ k, keepdims=False)  1.04 us
    ppermute x15, waiting for transfers between devices, shards(): lax.ppermute(pieces[k], 'hi', [(i, i ^ k) for i in range(devices)])  0.81 us
  transfers between devices with their start and end apart: 15, of which 1 were waited for; matrix products, arithmetic and copies ran while one was open for 0% of the time, Pallas kernels for 16%

profile of v1, /device:TPU:0, one launch (start us, length us, event | category | flops | bytes accessed | tf_op | source)
XLA Modules:
  0.0 37.7 jit_solution(1111110240292477399)
XLA Ops:
  0.0 1.0 %dynamic-slice_bitcast_fusion = (f32[64,128]{1,0:T(8,128)S(1)}, f32[64,128]{1,0:T(8,128)S(1)}, f32[64,128]{1,0:T(8,128)S(1)}, f32[64,128]{1,0:T(8,128)S(1)}, f32...) fusion(f32[16,64,128]{2,1,0:T(8,128)} %bitcast.46, ...), kind=kLoop, calls=%fused_computation | loop fusion | bytes 1048640 | tf_op jit(solution)/shard_map/jit(dynamic_index_in_dim)/squeeze | solution.py:243
  1.0 5.5 %collective-permute-start.14 = (f32[64,128]{1,0:T(8,128)S(1)}, f32[64,128]{1,0:T(8,128)S(1)}, u32[]{:S(2)}, u32[]{:S(2)}) collective-permute-start(f32[64,128]{1,0:T(8,128)S(1)} %get-tuple-element.11), channel_id=1, source_target_pairs={{0,15},{1,14},{2,13},{3,12},{4,11},{5,10},{6,9},{7,8},{8,7},{9,6},... | collective-permute-start | bytes 98312 | tf_op jit(solution)/shard_map/ppermute | solution.py:245
  6.6 0.6 %collective-permute-start.13 = (f32[64,128]{1,0:T(8,128)S(1)}, f32[64,128]{1,0:T(8,128)S(1)}, u32[]{:S(2)}, u32[]{:S(2)}) collective-permute-start(f32[64,128]{1,0:T(8,128)S(1)} %get-tuple-element.12), channel_id=1, source_target_pairs={{0,14},{1,15},{2,12},{3,13},{4,10},{5,11},{6,8},{7,9},{8,6},{9,7},... | collective-permute-start | bytes 98312 | tf_op jit(solution)/shard_map/ppermute | solution.py:245
  7.2 3.2 %collective-permute-start.12 = (f32[64,128]{1,0:T(8,128)S(1)}, f32[64,128]{1,0:T(8,128)S(1)}, u32[]{:S(2)}, u32[]{:S(2)}) collective-permute-start(f32[64,128]{1,0:T(8,128)S(1)} %get-tuple-element.13), channel_id=1, source_target_pairs={{0,13},{1,12},{2,15},{3,14},{4,9},{5,8},{6,11},{7,10},{8,5},{9,4},... | collective-permute-start | bytes 98312 | tf_op jit(solution)/shard_map/ppermute | solution.py:245
  10.4 0.3 collective-permute-start.11
  10.7 3.6 %collective-permute-start.9 = (f32[64,128]{1,0:T(8,128)S(1)}, f32[64,128]{1,0:T(8,128)S(1)}, u32[]{:S(2)}, u32[]{:S(2)}) collective-permute-start(f32[64,128]{1,0:T(8,128)S(1)} %get-tuple-element.16), channel_id=1, source_target_pairs={{0,10},{1,11},{2,8},{3,9},{4,14},{5,15},{6,12},{7,13},{8,2},{9,3},... | collective-permute-start | bytes 98312 | tf_op jit(solution)/shard_map/ppermute | solution.py:245
  14.3 0.0 collective-permute-done.13.refs_14_
  14.3 2.6 %collective-permute-start.7 = (f32[64,128]{1,0:T(8,128)S(1)}, f32[64,128]{1,0:T(8,128)S(1)}, u32[]{:S(2)}, u32[]{:S(2)}) collective-permute-start(f32[64,128]{1,0:T(8,128)S(1)} %get-tuple-element.18), channel_id=1, source_target_pairs={{0,8},{1,9},{2,10},{3,11},{4,12},{5,13},{6,14},{7,15},{8,0},{9,1},... | collective-permute-start | bytes 98312 | tf_op jit(solution)/shard_map/ppermute | solution.py:245
  16.9 1.9 %collective-permute-start.6 = (f32[64,128]{1,0:T(8,128)S(1)}, f32[64,128]{1,0:T(8,128)S(1)}, u32[]{:S(2)}, u32[]{:S(2)}) collective-permute-start(f32[64,128]{1,0:T(8,128)S(1)} %get-tuple-element.19), channel_id=1, source_target_pairs={{0,7},{1,6},{2,5},{3,4},{4,3},{5,2},{6,1},{7,0},{8,15},{9,14},{10,... | collective-permute-start | bytes 98312 | tf_op jit(solution)/shard_map/ppermute | solution.py:245
  18.8 0.8 %collective-permute-start.5 = (f32[64,128]{1,0:T(8,128)S(1)}, f32[64,128]{1,0:T(8,128)S(1)}, u32[]{:S(2)}, u32[]{:S(2)}) collective-permute-start(f32[64,128]{1,0:T(8,128)S(1)} %get-tuple-element.20), channel_id=1, source_target_pairs={{0,6},{1,7},{2,4},{3,5},{4,2},{5,3},{6,0},{7,1},{8,14},{9,15},{10,... | collective-permute-start | bytes 98312 | tf_op jit(solution)/shard_map/ppermute | solution.py:245
  19.6 1.2 %collective-permute-start.4 = (f32[64,128]{1,0:T(8,128)S(1)}, f32[64,128]{1,0:T(8,128)S(1)}, u32[]{:S(2)}, u32[]{:S(2)}) collective-permute-start(f32[64,128]{1,0:T(8,128)S(1)} %get-tuple-element.21), channel_id=1, source_target_pairs={{0,5},{1,4},{2,7},{3,6},{4,1},{5,0},{6,3},{7,2},{8,13},{9,12},{10,... | collective-permute-start | bytes 98312 | tf_op jit(solution)/shard_map/ppermute | solution.py:245
  20.8 0.5 %collective-permute-start.3 = (f32[64,128]{1,0:T(8,128)S(1)}, f32[64,128]{1,0:T(8,128)S(1)}, u32[]{:S(2)}, u32[]{:S(2)}) collective-permute-start(f32[64,128]{1,0:T(8,128)S(1)} %get-tuple-element.22), channel_id=1, source_target_pairs={{0,4},{1,5},{2,6},{3,7},{4,0},{5,1},{6,2},{7,3},{8,12},{9,13},{10,... | collective-permute-start | bytes 98312 | tf_op jit(solution)/shard_map/ppermute | solution.py:245
  21.3 0.9 %collective-permute-start.2 = (f32[64,128]{1,0:T(8,128)S(1)}, f32[64,128]{1,0:T(8,128)S(1)}, u32[]{:S(2)}, u32[]{:S(2)}) collective-permute-start(f32[64,128]{1,0:T(8,128)S(1)} %get-tuple-element.23), channel_id=1, source_target_pairs={{0,3},{1,2},{2,1},{3,0},{4,7},{5,6},{6,5},{7,4},{8,11},{9,10},{10,... | collective-permute-start | bytes 98312 | tf_op jit(solution)/shard_map/ppermute | solution.py:245
  22.3 0.0 collective-permute-done.6.refs_7_
  22.3 0.9 %collective-permute-start.1 = (f32[64,128]{1,0:T(8,128)S(1)}, f32[64,128]{1,0:T(8,128)S(1)}, u32[]{:S(2)}, u32[]{:S(2)}) collective-permute-start(f32[64,128]{1,0:T(8,128)S(1)} %get-tuple-element.24), channel_id=1, source_target_pairs={{0,2},{1,3},{2,0},{3,1},{4,6},{5,7},{6,4},{7,5},{8,10},{9,11},{10,... | collective-permute-start | bytes 98312 | tf_op jit(solution)/shard_map/ppermute | solution.py:245
  23.1 0.8 %collective-permute-done.5.refs_6_ = f32[64,128]{1,0:T(8,128)S(1)} collective-permute-done((f32[64,128]{1,0:T(8,128)S(1)}, f32[64,128]{1,0:T(8,128)S(1)}, u32[]{:S(2)}, u32[]{:S(2)}) %collective-permute-start.5) | collective-permute-done | bytes 32800 | tf_op jit(solution)/shard_map/ppermute | solution.py:245
  23.9 1.0 %copy-done = bf16[6,2,128,128]{3,2,1,0:T(8,128)(2,1)S(1)} copy-done((bf16[6,2,128,128]{3,2,1,0:T(8,128)(2,1)S(1)}, bf16[6,2,128,128]{3,2,1,0:T(8,128)(2,1)}, u32[]{:S(2)}) %copy-start) | copy-done | bytes 393240
  24.9 0.7 %copy-done.1 = s32[6,8,2]{1,2,0:T(2,128)S(1)} copy-done((s32[6,8,2]{1,2,0:T(2,128)S(1)}, s32[6,8,2]{1,2,0:T(2,128)}, u32[]{:S(2)}) %copy-start.1) | copy-done | bytes 408
  25.6 0.7 %copy-done.2 = f32[6,8]{1,0:T(8,128)S(1)} copy-done((f32[6,8]{1,0:T(8,128)S(1)}, f32[6,8]{1,0:T(8,128)}, u32[]{:S(2)}) %copy-start.2) | copy-done | bytes 216
  26.3 0.7 %copy-done.3 = s32[6,2]{0,1:T(2,128)S(1)} copy-done((s32[6,2]{0,1:T(2,128)S(1)}, s32[6,2]{0,1:T(2,128)}, u32[]{:S(2)}) %copy-start.3) | copy-done | bytes 72
  27.0 0.7 %copy-done.4 = f32[6]{0:T(128)S(1)} copy-done((f32[6]{0:T(128)S(1)}, f32[6]{0:T(128)}, u32[]{:S(2)}) %copy-start.4) | copy-done | bytes 48
  27.6 0.7 %copy-done.5 = s32[6]{0:T(128)S(1)} copy-done((s32[6]{0:T(128)S(1)}, s32[6]{0:T(128)}, u32[]{:S(2)}) %copy-start.5) | copy-done | bytes 48
  28.3 6.1 %tables.1 = (bf16[6,512,512]{2,1,0:T(8,128)(2,1)S(1)}, f32[6,512,128]{2,1,0:T(8,128)S(1)}, f32[6,512,128]{2,1,0:T(8,128)S(1)}) custom-call(bf16[6,2,128,128]{3,2,1,0:T(8,128)(2,1)S(1)} %copy-done, s32[6,2,8]{2,1,0:T(2,128)S(1)} %bitcast.44, f32[6,8]{1,0:T(8,128)S(1)} %copy-done.2, s32[2,6]{1,0:T(2,128)S(1)} %bitcast.45, f32[6]{0:T(128)S(1)} %copy-done.4, ...), custom_call_target="tpu_custom_call" | custom-call | flops 39321600 | bytes 1572864 | tf_op jit(solution)/shard_map/tables/pallas_call | solution.py:252
  34.4 3.3 %layers.1 = f32[1024,128]{1,0:T(8,128)} custom-call(f32[64,128]{1,0:T(8,128)S(1)} %get-tuple-element.26.refs_0_, f32[64,128]{1,0:T(8,128)S(1)} %collective-permute-done.refs_1_, f32[64,128]{1,0:T(8,128)S(1)} %collective-permute-done.1.refs_2_, f32[64,128]{1,0:T(8,128)S(1)} %collective-permute-done.2.refs_3_, f32[64,128]{1,0:T(8,128)S(1)} %collective-permute-done.3.refs_4_, ...), custom_call_target="tpu_custom_call" | custom-call | tf_op jit(solution)/shard_map/layers/pallas_call | solution.py:262
  (21 shorter events, 0.0 us)
Async XLA Ops:
  1.0 9.6 %collective-permute-start.14 = (f32[64,128]{1,0:T(8,128)S(1)}, f32[64,128]{1,0:T(8,128)S(1)}, u32[]{:S(2)}, u32[]{:S(2)}) collective-permute-start(f32[64,128]{1,0:T(8,128)S(1)} %get-tuple-element.11), channel_id=1, source_target_pairs={{0,15},{1,14},{2,13},{3,12},{4,11},{5,10},{6,9},{7,8},{8,7},{9,6},... | collective-permute-start | bytes 98312 | tf_op jit(solution)/shard_map/ppermute | solution.py:245
  6.6 7.7 %collective-permute-start.13 = (f32[64,128]{1,0:T(8,128)S(1)}, f32[64,128]{1,0:T(8,128)S(1)}, u32[]{:S(2)}, u32[]{:S(2)}) collective-permute-start(f32[64,128]{1,0:T(8,128)S(1)} %get-tuple-element.12), channel_id=1, source_target_pairs={{0,14},{1,15},{2,12},{3,13},{4,10},{5,11},{6,8},{7,9},{8,6},{9,7},... | collective-permute-start | bytes 98312 | tf_op jit(solution)/shard_map/ppermute | solution.py:245
  7.2 7.1 %collective-permute-start.12 = (f32[64,128]{1,0:T(8,128)S(1)}, f32[64,128]{1,0:T(8,128)S(1)}, u32[]{:S(2)}, u32[]{:S(2)}) collective-permute-start(f32[64,128]{1,0:T(8,128)S(1)} %get-tuple-element.13), channel_id=1, source_target_pairs={{0,13},{1,12},{2,15},{3,14},{4,9},{5,8},{6,11},{7,10},{8,5},{9,4},... | collective-permute-start | bytes 98312 | tf_op jit(solution)/shard_map/ppermute | solution.py:245
  10.4 6.5 %collective-permute-start.11 = (f32[64,128]{1,0:T(8,128)S(1)}, f32[64,128]{1,0:T(8,128)S(1)}, u32[]{:S(2)}, u32[]{:S(2)}) collective-permute-start(f32[64,128]{1,0:T(8,128)S(1)} %get-tuple-element.14), channel_id=1, source_target_pairs={{0,12},{1,13},{2,14},{3,15},{4,8},{5,9},{6,10},{7,11},{8,4},{9,5},... | collective-permute-start | bytes 98312 | tf_op jit(solution)/shard_map/ppermute | solution.py:245
  10.7 8.1 %collective-permute-start.10 = (f32[64,128]{1,0:T(8,128)S(1)}, f32[64,128]{1,0:T(8,128)S(1)}, u32[]{:S(2)}, u32[]{:S(2)}) collective-permute-start(f32[64,128]{1,0:T(8,128)S(1)} %get-tuple-element.15), channel_id=1, source_target_pairs={{0,11},{1,10},{2,9},{3,8},{4,15},{5,14},{6,13},{7,12},{8,3},{9,2},... | collective-permute-start | bytes 98312 | tf_op jit(solution)/shard_map/ppermute | solution.py:245
  10.7 8.9 %collective-permute-start.9 = (f32[64,128]{1,0:T(8,128)S(1)}, f32[64,128]{1,0:T(8,128)S(1)}, u32[]{:S(2)}, u32[]{:S(2)}) collective-permute-start(f32[64,128]{1,0:T(8,128)S(1)} %get-tuple-element.16), channel_id=1, source_target_pairs={{0,10},{1,11},{2,8},{3,9},{4,14},{5,15},{6,12},{7,13},{8,2},{9,3},... | collective-permute-start | bytes 98312 | tf_op jit(solution)/shard_map/ppermute | solution.py:245
  14.3 6.5 %collective-permute-start.8 = (f32[64,128]{1,0:T(8,128)S(1)}, f32[64,128]{1,0:T(8,128)S(1)}, u32[]{:S(2)}, u32[]{:S(2)}) collective-permute-start(f32[64,128]{1,0:T(8,128)S(1)} %get-tuple-element.17), channel_id=1, source_target_pairs={{0,9},{1,8},{2,11},{3,10},{4,13},{5,12},{6,15},{7,14},{8,1},{9,0},... | collective-permute-start | bytes 98312 | tf_op jit(solution)/shard_map/ppermute | solution.py:245
  14.3 7.0 %collective-permute-start.7 = (f32[64,128]{1,0:T(8,128)S(1)}, f32[64,128]{1,0:T(8,128)S(1)}, u32[]{:S(2)}, u32[]{:S(2)}) collective-permute-start(f32[64,128]{1,0:T(8,128)S(1)} %get-tuple-element.18), channel_id=1, source_target_pairs={{0,8},{1,9},{2,10},{3,11},{4,12},{5,13},{6,14},{7,15},{8,0},{9,1},... | collective-permute-start | bytes 98312 | tf_op jit(solution)/shard_map/ppermute | solution.py:245
  16.9 5.4 %collective-permute-start.6 = (f32[64,128]{1,0:T(8,128)S(1)}, f32[64,128]{1,0:T(8,128)S(1)}, u32[]{:S(2)}, u32[]{:S(2)}) collective-permute-start(f32[64,128]{1,0:T(8,128)S(1)} %get-tuple-element.19), channel_id=1, source_target_pairs={{0,7},{1,6},{2,5},{3,4},{4,3},{5,2},{6,1},{7,0},{8,15},{9,14},{10,... | collective-permute-start | bytes 98312 | tf_op jit(solution)/shard_map/ppermute | solution.py:245
  18.8 5.1 %collective-permute-start.5 = (f32[64,128]{1,0:T(8,128)S(1)}, f32[64,128]{1,0:T(8,128)S(1)}, u32[]{:S(2)}, u32[]{:S(2)}) collective-permute-start(f32[64,128]{1,0:T(8,128)S(1)} %get-tuple-element.20), channel_id=1, source_target_pairs={{0,6},{1,7},{2,4},{3,5},{4,2},{5,3},{6,0},{7,1},{8,14},{9,15},{10,... | collective-permute-start | bytes 98312 | tf_op jit(solution)/shard_map/ppermute | solution.py:245
  19.6 14.8 %collective-permute-start.4 = (f32[64,128]{1,0:T(8,128)S(1)}, f32[64,128]{1,0:T(8,128)S(1)}, u32[]{:S(2)}, u32[]{:S(2)}) collective-permute-start(f32[64,128]{1,0:T(8,128)S(1)} %get-tuple-element.21), channel_id=1, source_target_pairs={{0,5},{1,4},{2,7},{3,6},{4,1},{5,0},{6,3},{7,2},{8,13},{9,12},{10,... | collective-permute-start | bytes 98312 | tf_op jit(solution)/shard_map/ppermute | solution.py:245
  20.8 13.6 %collective-permute-start.3 = (f32[64,128]{1,0:T(8,128)S(1)}, f32[64,128]{1,0:T(8,128)S(1)}, u32[]{:S(2)}, u32[]{:S(2)}) collective-permute-start(f32[64,128]{1,0:T(8,128)S(1)} %get-tuple-element.22), channel_id=1, source_target_pairs={{0,4},{1,5},{2,6},{3,7},{4,0},{5,1},{6,2},{7,3},{8,12},{9,13},{10,... | collective-permute-start | bytes 98312 | tf_op jit(solution)/shard_map/ppermute | solution.py:245
  21.3 13.1 %collective-permute-start.2 = (f32[64,128]{1,0:T(8,128)S(1)}, f32[64,128]{1,0:T(8,128)S(1)}, u32[]{:S(2)}, u32[]{:S(2)}) collective-permute-start(f32[64,128]{1,0:T(8,128)S(1)} %get-tuple-element.23), channel_id=1, source_target_pairs={{0,3},{1,2},{2,1},{3,0},{4,7},{5,6},{6,5},{7,4},{8,11},{9,10},{10,... | collective-permute-start | bytes 98312 | tf_op jit(solution)/shard_map/ppermute | solution.py:245
  22.3 12.1 %collective-permute-start.1 = (f32[64,128]{1,0:T(8,128)S(1)}, f32[64,128]{1,0:T(8,128)S(1)}, u32[]{:S(2)}, u32[]{:S(2)}) collective-permute-start(f32[64,128]{1,0:T(8,128)S(1)} %get-tuple-element.24), channel_id=1, source_target_pairs={{0,2},{1,3},{2,0},{3,1},{4,6},{5,7},{6,4},{7,5},{8,10},{9,11},{10,... | collective-permute-start | bytes 98312 | tf_op jit(solution)/shard_map/ppermute | solution.py:245
  23.9 10.5 %collective-permute-start = (f32[64,128]{1,0:T(8,128)S(1)}, f32[64,128]{1,0:T(8,128)S(1)}, u32[]{:S(2)}, u32[]{:S(2)}) collective-permute-start(f32[64,128]{1,0:T(8,128)S(1)} %get-tuple-element.25), channel_id=1, source_target_pairs={{0,1},{1,0},{2,3},{3,2},{4,5},{5,4},{6,7},{7,6},{8,9},{9,8},{10,11... | collective-permute-start | bytes 98312 | tf_op jit(solution)/shard_map/ppermute | solution.py:245
  23.9 1.0 %copy-start = (bf16[6,2,128,128]{3,2,1,0:T(8,128)(2,1)S(1)}, bf16[6,2,128,128]{3,2,1,0:T(8,128)(2,1)}, u32[]{:S(2)}) copy-start(bf16[6,2,128,128]{3,2,1,0:T(8,128)(2,1)} %gates.1) | copy-start | bytes 1179652
  24.9 0.7 %copy-start.1 = (s32[6,8,2]{1,2,0:T(2,128)S(1)}, s32[6,8,2]{1,2,0:T(2,128)}, u32[]{:S(2)}) copy-start(s32[6,8,2]{1,2,0:T(2,128)} %param.9) | copy-start | bytes 1156
  25.6 0.7 %copy-start.2 = (f32[6,8]{1,0:T(8,128)S(1)}, f32[6,8]{1,0:T(8,128)}, u32[]{:S(2)}) copy-start(f32[6,8]{1,0:T(8,128)} %pair_angles.1) | copy-start | bytes 580
  26.3 0.7 %copy-start.3 = (s32[6,2]{0,1:T(2,128)S(1)}, s32[6,2]{0,1:T(2,128)}, u32[]{:S(2)}) copy-start(s32[6,2]{0,1:T(2,128)} %param.11) | copy-start | bytes 148
  27.0 0.7 %copy-start.4 = (f32[6]{0:T(128)S(1)}, f32[6]{0:T(128)}, u32[]{:S(2)}) copy-start(f32[6]{0:T(128)} %cut_angle.1) | copy-start | bytes 76
  27.6 0.7 %copy-start.5 = (s32[6]{0:T(128)S(1)}, s32[6]{0:T(128)}, u32[]{:S(2)}) copy-start(s32[6]{0:T(128)} %path_index.1) | copy-start | bytes 76

commit v2 on v1

v2 whole, which is shorter than its diff:
```python
import functools

import jax
import jax.numpy as jnp
import numpy as np
from jax import lax
from jax.experimental import pallas as pl
from jax.experimental.layout import Layout, with_layout_constraint
from jax.experimental.pallas import tpu as pltpu
from jax.sharding import PartitionSpec as P

LANE_BITS = 7
GATE_BITS = 6


def fitted(function, degree):
    nodes = np.cos(np.pi * (np.arange(64) + 0.5) / 64) * 0.125 + 0.125
    series = np.polynomial.chebyshev.Chebyshev.fit(nodes, function(np.sqrt(nodes)), degree, domain=[0, 0.25])
    return [float(c) for c in series.convert(kind=np.polynomial.Polynomial).coef]


COS_TERMS = fitted(lambda v: np.cos(2 * np.pi * v), 7)
SIN_TERMS = fitted(lambda v: np.sin(2 * np.pi * v) / v, 6)


def horner(terms, w):
    total = jnp.full_like(w, terms[-1])
    for term in terms[-2::-1]:
        total = total * w + term
    return total


def turn(angle):
    part = angle - jnp.round(angle)
    square = part * part
    return horner(COS_TERMS, square), part * horner(SIN_TERMS, square)


class Plan:
    def __init__(self, global_count, local_bits, layers):
        self.global_count, self.local_bits, self.layers = global_count, local_bits, layers
        self.top = top = local_bits - global_count
        place = {}
        for label in range(local_bits + global_count):
            if label < top:
                place[label] = label
            elif label < local_bits:
                place[label] = label + global_count
            else:
                place[label] = label - global_count
        held = list(range(local_bits + global_count))
        self.targets = []
        for layer in range(layers):
            if layer < global_count:
                low, high = 7 + layer, local_bits + layer
                held[low], held[high] = held[high], held[low]
                target = low
            else:
                if layer == global_count:
                    held = held[:top] + held[local_bits:] + held[top:local_bits]
                target = local_bits - 2 * global_count + layer
            self.targets.append(place[held[target]])
        assert all(LANE_BITS <= bit < local_bits for bit in self.targets)
        ends = [place[label] for label in held]
        self.extra = sum(ends[local_bits + k] != local_bits + k for k in range(global_count))
        swapped = ends[:]
        for k in range(self.extra):
            low, high = local_bits - self.extra + k, local_bits + k
            assert ends[low] == high
            swapped[low], swapped[high] = ends[high], ends[low]
        assert swapped[local_bits:] == list(range(local_bits, local_bits + global_count))
        assert swapped[:LANE_BITS] == list(range(LANE_BITS))
        self.wanted = swapped[LANE_BITS:local_bits]
        self.orders, self.steps, self.slots = [], [], []
        order, lane_top = list(range(LANE_BITS, local_bits)), GATE_BITS
        for layer, target in enumerate(self.targets + [GATE_BITS]):
            step = 0
            if target in order[:3]:
                step = max(range(1, len(order) - 2), key=lambda at: self.lasts(order[at:at + 3], layer))
                triple = order[step:step + 3]
                assert target not in triple
                order = triple + [bit for bit in order if bit not in triple]
            slot = order.index(target)
            order = order[:slot] + [lane_top] + order[slot + 1:]
            lane_top = target
            self.steps.append(step)
            self.slots.append(slot)
            self.orders.append(order)
        at = [self.wanted.index(bit) for bit in order[:3]]
        self.direct = at == list(range(at[0], at[0] + 3))

    def lasts(self, triple, layer):
        uses = self.targets[layer:] + [GATE_BITS]
        count = next((k for k, bit in enumerate(uses) if bit in triple), len(uses))
        at = [self.wanted.index(bit) for bit in triple if bit in self.wanted]
        if count == len(uses) and at == list(range(at[0], at[0] + 3)):
            count += 1
        return count

    def locate(self, qubit, layer):
        low, count = 7, min(layer + 1, self.global_count)
        size, high = self.global_count, self.local_bits
        if layer >= size:
            qubit = jnp.where(qubit >= high, qubit - size, jnp.where(qubit >= self.top, qubit + size, qubit))
        up = (qubit >= low) & (qubit < low + count)
        down = (qubit >= high) & (qubit < high + count)
        label = jnp.where(up, qubit + (high - low), jnp.where(down, qubit - (high - low), qubit))
        return jnp.where(label >= high, label - size, jnp.where(label >= self.top, label + size, label))


def tables_kernel(plan, rows, gates, pair_qubits, pair_angles, cut_qubits, cut_angle, path_index,
                  weights, phases, weights_here, phases_here, done):
    device_part = lax.axis_index("hi") << plan.local_bits
    copies = []
    for layer in range(plan.layers):
        real, imag = [gates[layer, part].astype(jnp.float32).T for part in range(2)]
        joined = jnp.concatenate(
            [jnp.concatenate([real, imag], axis=1), jnp.concatenate([-imag, real], axis=1)], axis=0
        )
        weights_here[layer] = joined.astype(jnp.bfloat16)
    copies.append(pltpu.make_async_copy(weights_here, weights, done.at[plan.layers]))
    copies[-1].start()

    block_rows = 64
    block_bits = block_rows.bit_length() - 1
    row = lax.broadcasted_iota(jnp.int32, (block_rows, 128), 0)
    lane = lax.broadcasted_iota(jnp.int32, (block_rows, 128), 1)
    for layer in range(plan.layers):
        order = plan.orders[layer]
        base = (lane & 63) + ((lane >> 6) << plan.targets[layer]) + device_part
        for bit in range(block_bits):
            base = base + (((row >> bit) & 1) << order[bit])
        masks, turns = [], []
        one = jnp.int32(1)
        for pair in range(pair_qubits.shape[2]):
            first = plan.locate(pair_qubits[layer, 0, pair], layer)
            second = plan.locate(pair_qubits[layer, 1, pair], layer)
            masks.append((one << first) | (one << second))
            turns.append(pair_angles[layer, pair] * np.float32(0.5 / np.pi))
        if layer == 0:
            size = jnp.ones((8, 128), jnp.float32)
            cut_masks, cut_turns = [], []
            for cut in range(cut_qubits.shape[1]):
                first = plan.locate(cut_qubits[0, cut], layer)
                second = plan.locate(cut_qubits[1, cut], layer)
                cut_masks.append((one << first) | (one << second))
                chosen = path_index[cut] == 0
                cosine, sine = turn(jnp.full((8, 128), cut_angle[cut] * np.float32(0.5 / np.pi)))
                size = size * jnp.where(chosen, cosine, sine)
                cut_turns.append(jnp.where(chosen, 0.0, 0.25))
            size = jnp.broadcast_to(size[:1], (block_rows, 128))

        @pl.loop(0, rows // block_rows)
        def _(block):
            offset = jnp.int32(0)
            for bit in range(block_bits, len(order)):
                offset = offset + (((block >> (bit - block_bits)) & 1) << order[bit])
            index = base + offset
            angle = jnp.zeros((block_rows, 128), jnp.float32)
            for mask, amount in zip(masks, turns):
                angle = angle + jnp.where((index & mask) == mask, amount, 0.0)
            if layer == 0:
                for mask, amount in zip(cut_masks, cut_turns):
                    both = index & mask
                    angle = angle + jnp.where((both == 0) | (both == mask), -amount, amount)
            cosine, sine = turn(angle)
            if layer == 0:
                cosine, sine = cosine * size, sine * size
            at = pl.ds(pl.multiple_of(block * block_rows, block_rows), block_rows)
            phases_here[layer, 0, at, :] = cosine
            phases_here[layer, 1, at, :] = sine

        copies.append(pltpu.make_async_copy(phases_here.at[layer], phases.at[layer], done.at[layer]))
        copies[-1].start()
    for copy in copies:
        copy.wait()


def offset_of(number, bits, order):
    return sum(((number >> k) & 1) << order.index(bit) for k, bit in enumerate(bits))


def trade(low, high):
    lane = lax.broadcasted_iota(jnp.int32, low.shape, 1)
    return (jnp.where(lane < 64, low, pltpu.roll(high, 64, 1)),
            jnp.where(lane < 64, pltpu.roll(low, 64, 1), high))


def layers_kernel(plan, rows, state, weights, phases, out, state_here, weights_here, phases_here, held, done):
    layers = plan.layers
    copies = [pltpu.make_async_copy(state, state_here, done.at[0])]
    for layer in range(layers):
        copies.append(pltpu.make_async_copy(weights.at[layer], weights_here.at[layer], done.at[1 + 2 * layer]))
        copies.append(pltpu.make_async_copy(phases.at[layer], phases_here.at[layer], done.at[2 + 2 * layer]))
    for copy in copies:
        copy.start()
    copies[0].wait()

    tiles = rows // 8
    old_order = list(range(LANE_BITS, plan.local_bits))
    for layer in range(layers + 1):
        order, step, slot = plan.orders[layer], plan.steps[layer], plan.slots[layer]
        lane_top = plan.targets[layer - 1] if layer else GATE_BITS
        target = (plan.targets + [GATE_BITS])[layer]
        read_order = [target if bit == lane_top else bit for bit in order]
        values = [[None] * tiles, [None] * tiles]
        for tile in range(tiles):
            pair = tile | 1 << (slot - 3)
            if pair == tile:
                continue
            for part in range(2):
                loaded = []
                for number in (tile, pair):
                    at = offset_of(number, read_order[3:], old_order)
                    if layer == 0:
                        loaded.append(state_here[pl.ds(2 * at + part, 8, 2 << step), :])
                    elif step:
                        loaded.append(held[(layer - 1) % 2, part, pl.ds(at, 8, 1 << step), :])
                    else:
                        loaded.append(held[(layer - 1) % 2, part, pl.ds(at, 8), :])
                values[part][tile], values[part][pair] = trade(*loaded)
        old_order = order
        if layer == layers:
            break
        joined = jnp.concatenate([jnp.concatenate(values[part], axis=0) for part in range(2)], axis=1)
        large = joined.astype(jnp.bfloat16)
        small = (joined - large.astype(jnp.float32)).astype(jnp.bfloat16)
        copies[1 + 2 * layer].wait()
        weight = weights_here[layer]
        result = jnp.dot(jnp.concatenate([large, small], axis=1), jnp.concatenate([weight, weight], axis=0),
                         preferred_element_type=jnp.float32)
        real, imag = result[:, :128], result[:, 128:]
        copies[2 + 2 * layer].wait()
        cosine, sine = phases_here[layer, 0], phases_here[layer, 1]
        held[layer % 2, 0] = cosine * real - sine * imag
        held[layer % 2, 1] = sine * real + cosine * imag

    for tile in range(tiles):
        for part in range(2):
            if plan.direct:
                at = offset_of(tile, old_order[3:], plan.wanted)
                stride = 2 << plan.wanted.index(old_order[0])
                out[pl.ds(2 * at + part, 8, stride), :] = values[part][tile]
            else:
                out[pl.ds(16 * tile + part, 8, 2), :] = values[part][tile]


def shards(
    amplitudes, gate_matrices, phase_qubits, phase_angles, cut_qubits, cut_angle, path_index
):
    devices = lax.axis_size("hi")
    global_count = devices.bit_length() - 1
    amp_count = amplitudes.shape[1]
    rows = amp_count >> LANE_BITS
    layers = gate_matrices.shape[0]
    plan = Plan(global_count, amp_count.bit_length() - 1, layers)

    shaped = with_layout_constraint(amplitudes.reshape(2, rows, 128), Layout(major_to_minor=(1, 0, 2)))
    sent = shaped.transpose(1, 0, 2).reshape(devices, -1, 128)
    came = lax.all_to_all(sent, "hi", split_axis=0, concat_axis=0, tiled=True).reshape(2 * rows, 128)

    vmem, smem = pl.BlockSpec(memory_space=pltpu.VMEM), pl.BlockSpec(memory_space=pltpu.SMEM)
    hbm = pl.BlockSpec(memory_space=pltpu.HBM)
    weights_shape, phases_shape = (layers, 256, 256), (layers, 2, rows, 128)
    here = [pltpu.VMEM(weights_shape, jnp.bfloat16), pltpu.VMEM(phases_shape, jnp.float32)]
    weights, phases = pl.pallas_call(
        functools.partial(tables_kernel, plan, rows),
        out_shape=(
            jax.ShapeDtypeStruct(weights_shape, jnp.bfloat16),
            jax.ShapeDtypeStruct(phases_shape, jnp.float32),
        ),
        in_specs=[vmem] + [smem] * 5,
        out_specs=[hbm] * 2,
        scratch_shapes=here + [pltpu.SemaphoreType.DMA((layers + 1,))],
        cost_estimate=pl.CostEstimate(flops=100 * layers * amp_count, bytes_accessed=8 * layers * amp_count, transcendentals=0),
        compiler_params=pltpu.CompilerParams(vmem_limit_bytes=24 << 20),
        name="tables",
    )(gate_matrices, phase_qubits.transpose(0, 2, 1), phase_angles, cut_qubits.T, cut_angle, path_index)

    result = pl.pallas_call(
        functools.partial(layers_kernel, plan, rows),
        out_shape=jax.ShapeDtypeStruct((2 * rows, 128), jnp.float32),
        in_specs=[hbm] * 3,
        out_specs=vmem,
        scratch_shapes=[pltpu.VMEM((2 * rows, 128), jnp.float32)] + here
        + [pltpu.VMEM((2, 2, rows, 128), jnp.float32), pltpu.SemaphoreType.DMA((2 * layers + 1,))],
        compiler_params=pltpu.CompilerParams(vmem_limit_bytes=24 << 20),
        name="layers",
    )(came, weights, phases)

    if not plan.direct:
        bits = len(plan.wanted)
        shaped = result.reshape((2,) * bits + (2, 128))
        axes = [bits - 1 - plan.orders[-1].index(plan.wanted[bits - 1 - axis]) for axis in range(bits)]
        result = shaped.transpose(axes + [bits, bits + 1]).reshape(2 * rows, 128)
    if plan.extra:
        size = 1 << plan.extra
        groups = [list(range(first, first + size)) for first in range(0, devices, size)]
        result = lax.all_to_all(
            result.reshape(size, -1, 128), "hi", split_axis=0, concat_axis=0,
            axis_index_groups=groups, tiled=True,
        )
    return result.reshape(rows, 2, 128).transpose(1, 0, 2).reshape(2, amp_count)


def solution(mesh):
    placed = (
        P(None, ("paths", "hi")),
        P(),
        P("paths", None, None),
        P("paths", None),
        P("paths", None),
        P("paths"),
        P("paths"),
    )
    return jax.shard_map(
        shards, mesh=mesh, in_specs=placed, out_specs=P(None, ("paths", "hi")), check_vma=False
    )
```

time: 38.1 us -> 29.9 us (0.78)
  starting transfers between devices: 22.1 us -> 7.43 us
  Pallas kernels: 9.33 us -> 12.7 us
  waiting for transfers between devices: 0.81 us -> 2.93 us
  local copies, waits for them, and re-layouts: 5.4 us -> 6.36 us
    ppermute x15 -> x0, starting transfers between devices: 22.1 us -> none  [shards(): lax.ppermute(pieces[k], 'hi', [(i, i ^ k) for i in range(devices)])]
    all_to_all x0 -> x1, starting transfers between devices: none -> 7.43 us  [shards(): lax.all_to_all(sent, 'hi', split_axis=0, concat_axis=0, tiled=True)]
    pallas_call x1, Pallas kernels: 3.26 us -> 6.37 us  [shards(): pl.pallas_call(functools.partial(layers_kernel, plan, rows), out_shape=ja...]
    all_to_all x0 -> x1, waiting for transfers between devices: none -> 2.93 us  [shards(): lax.all_to_all(sent, 'hi', split_axis=0, concat_axis=0, tiled=True)]
    unnamed x12 -> x16, local copies, waits for them, and re-layouts: 4.36 us -> 6.36 us
    squeeze x1 -> x0, local copies, waits for them, and re-layouts: 1.04 us -> none  [shards(): lax.dynamic_index_in_dim(sent, place ^ k, keepdims=False)]
    ppermute x15 -> x0, waiting for transfers between devices: 0.81 us -> none  [shards(): lax.ppermute(pieces[k], 'hi', [(i, i ^ k) for i in range(devices)])]
  transfers between devices with their start and end apart: 15 -> 1, of which waited for: 1 -> 1; matrix products, arithmetic and copies ran while one was open for 0% -> 0% of each run, Pallas kernels for 16% -> 21%
where the time goes in v2:
time: 29.9 us; the launch traced here: 29.5 us
  Pallas kernels  12.7 us (42%)
  starting transfers between devices  7.43 us (25%)
  local copies, waits for them, and re-layouts  6.36 us (21%)
  waiting for transfers between devices  2.93 us (10%)
    all_to_all x1, starting transfers between devices, shards(): lax.all_to_all(sent, 'hi', split_axis=0, concat_axis=0, tiled=True)  7.43 us
    pallas_call x1, Pallas kernels, shards(): pl.pallas_call(functools.partial(layers_kernel, plan, rows), out_shape=ja...  6.37 us
    unnamed x16, local copies, waits for them, and re-layouts  6.36 us
    pallas_call x1, Pallas kernels, shards(): pl.pallas_call(functools.partial(tables_kernel, plan, rows), out_shape=(j...  6.33 us
    all_to_all x1, waiting for transfers between devices, shards(): lax.all_to_all(sent, 'hi', split_axis=0, concat_axis=0, tiled=True)  2.93 us
  transfers between devices with their start and end apart: 1, of which 1 were waited for; matrix products, arithmetic and copies ran while one was open for 0% of the time, Pallas kernels for 21%

profile of v2, /device:TPU:0, one launch (start us, length us, event | category | flops | bytes accessed | tf_op | source)
XLA Modules:
  0.0 29.5 jit_solution(12720423946563480893)
XLA Ops:
  0.0 7.4 %all-to-all-start = ((f32[16,64,128]{2,1,0:T(8,128)}), f32[16,64,128]{2,1,0:T(8,128)}, u32[]{:S(2)}, u32[]{:S(2)}) async-start(f32[16,64,128]{2,1,0:T(8,128)} %bitcast.15), calls=%async_computation | async-start | bytes 1048576 | tf_op jit(solution)/shard_map/all_to_all | solution.py:260
  7.4 0.0 copy-start.2
  7.5 1.0 %copy-done.2 = bf16[6,2,128,128]{3,2,1,0:T(8,128)(2,1)S(1)} copy-done((bf16[6,2,128,128]{3,2,1,0:T(8,128)(2,1)S(1)}, bf16[6,2,128,128]{3,2,1,0:T(8,128)(2,1)}, u32[]{:S(2)}) %copy-start.2) | copy-done | bytes 393240
  8.4 0.0 copy-start.3
  8.4 0.7 %copy-done.3 = s32[6,8,2]{1,2,0:T(2,128)S(1)} copy-done((s32[6,8,2]{1,2,0:T(2,128)S(1)}, s32[6,8,2]{1,2,0:T(2,128)}, u32[]{:S(2)}) %copy-start.3) | copy-done | bytes 408
  9.1 0.0 copy-start.4
  9.1 0.7 %copy-done.4 = f32[6,8]{1,0:T(8,128)S(1)} copy-done((f32[6,8]{1,0:T(8,128)S(1)}, f32[6,8]{1,0:T(8,128)}, u32[]{:S(2)}) %copy-start.4) | copy-done | bytes 216
  9.8 0.0 copy-start.5
  9.8 0.7 %copy-done.5 = s32[6,2]{0,1:T(2,128)S(1)} copy-done((s32[6,2]{0,1:T(2,128)S(1)}, s32[6,2]{0,1:T(2,128)}, u32[]{:S(2)}) %copy-start.5) | copy-done | bytes 72
  10.5 0.0 copy-start.6
  10.5 0.7 %copy-done.6 = f32[6]{0:T(128)S(1)} copy-done((f32[6]{0:T(128)S(1)}, f32[6]{0:T(128)}, u32[]{:S(2)}) %copy-start.6) | copy-done | bytes 48
  11.2 0.0 copy-start.7
  11.2 0.7 %copy-done.7 = s32[6]{0:T(128)S(1)} copy-done((s32[6]{0:T(128)S(1)}, s32[6]{0:T(128)}, u32[]{:S(2)}) %copy-start.7) | copy-done | bytes 48
  11.8 6.3 %tables.1 = (bf16[6,256,256]{2,1,0:T(8,128)(2,1)S(1)}, f32[6,2,512,128]{3,2,1,0:T(8,128)S(1)}) custom-call(bf16[6,2,128,128]{3,2,1,0:T(8,128)(2,1)S(1)} %copy-done.2, s32[6,2,8]{2,1,0:T(2,128)S(1)} %bitcast.13, f32[6,8]{1,0:T(8,128)S(1)} %copy-done.4, s32[2,6]{1,0:T(2,128)S(1)} %bitcast.14, f32[6]{0:T(128)S(1)} %copy-done.6, s32[6]{0:T(128)S(1)} %copy-done.7), custom_call_target="tpu_custom_call" | custom-call | flops 39321600 | bytes 3145728 | tf_op jit(solution)/shard_map/tables/pallas_call | solution.py:266
  18.2 0.0 copy-start
  18.2 0.9 %copy-done = bf16[6,256,256]{2,1,0:T(8,128)(2,1)} copy-done((bf16[6,256,256]{2,1,0:T(8,128)(2,1)}, bf16[6,256,256]{2,1,0:T(8,128)(2,1)S(1)}, u32[]{:S(2)}) %copy-start) | copy-done | bytes 786456
  19.0 2.9 %all-to-all-done = f32[16,64,128]{2,1,0:T(8,128)} async-done(((f32[16,64,128]{2,1,0:T(8,128)}), f32[16,64,128]{2,1,0:T(8,128)}, u32[]{:S(2)}, u32[]{:S(2)}) %all-to-all-start) | async-done | bytes 524320 | tf_op jit(solution)/shard_map/all_to_all | solution.py:260
  22.0 0.0 copy-start.1
  22.0 1.1 %copy-done.1 = bf16[6,256,256]{2,1,0:T(8,128)(2,1)S(1)} copy-done((bf16[6,256,256]{2,1,0:T(8,128)(2,1)S(1)}, bf16[6,256,256]{2,1,0:T(8,128)(2,1)}, u32[]{:S(2)}) %copy-start.1) | copy-done | bytes 786456
  23.1 6.4 %layers.1 = f32[1024,128]{1,0:T(8,128)} custom-call(f32[1024,128]{1,0:T(8,128)} %bitcast.3.state, bf16[6,256,256]{2,1,0:T(8,128)(2,1)S(1)} %copy-done.1, f32[6,2,512,128]{3,2,1,0:T(8,128)S(1)} %get-tuple-element.8.phases), custom_call_target="tpu_custom_call" | custom-call | tf_op jit(solution)/shard_map/layers/pallas_call | solution.py:280
Async XLA Ops:
  0.0 22.0 %all-to-all-start = ((f32[16,64,128]{2,1,0:T(8,128)}), f32[16,64,128]{2,1,0:T(8,128)}, u32[]{:S(2)}, u32[]{:S(2)}) async-start(f32[16,64,128]{2,1,0:T(8,128)} %bitcast.15), calls=%async_computation | async-start | bytes 1048576 | tf_op jit(solution)/shard_map/all_to_all | solution.py:260
  7.4 1.0 %copy-start.2 = (bf16[6,2,128,128]{3,2,1,0:T(8,128)(2,1)S(1)}, bf16[6,2,128,128]{3,2,1,0:T(8,128)(2,1)}, u32[]{:S(2)}) copy-start(bf16[6,2,128,128]{3,2,1,0:T(8,128)(2,1)} %gates.1) | copy-start | bytes 1179652
  8.4 0.7 %copy-start.3 = (s32[6,8,2]{1,2,0:T(2,128)S(1)}, s32[6,8,2]{1,2,0:T(2,128)}, u32[]{:S(2)}) copy-start(s32[6,8,2]{1,2,0:T(2,128)} %param.9) | copy-start | bytes 1156
  9.1 0.7 %copy-start.4 = (f32[6,8]{1,0:T(8,128)S(1)}, f32[6,8]{1,0:T(8,128)}, u32[]{:S(2)}) copy-start(f32[6,8]{1,0:T(8,128)} %pair_angles.1) | copy-start | bytes 580
  9.8 0.7 %copy-start.5 = (s32[6,2]{0,1:T(2,128)S(1)}, s32[6,2]{0,1:T(2,128)}, u32[]{:S(2)}) copy-start(s32[6,2]{0,1:T(2,128)} %param.11) | copy-start | bytes 148
  10.5 0.7 %copy-start.6 = (f32[6]{0:T(128)S(1)}, f32[6]{0:T(128)}, u32[]{:S(2)}) copy-start(f32[6]{0:T(128)} %cut_angle.1) | copy-start | bytes 76
  11.2 0.7 %copy-start.7 = (s32[6]{0:T(128)S(1)}, s32[6]{0:T(128)}, u32[]{:S(2)}) copy-start(s32[6]{0:T(128)} %path_index.1) | copy-start | bytes 76
  18.2 0.9 %copy-start = (bf16[6,256,256]{2,1,0:T(8,128)(2,1)}, bf16[6,256,256]{2,1,0:T(8,128)(2,1)S(1)}, u32[]{:S(2)}) copy-start(bf16[6,256,256]{2,1,0:T(8,128)(2,1)S(1)} %get-tuple-element.7.weights) | copy-start | bytes 2359300
  22.0 1.1 %copy-start.1 = (bf16[6,256,256]{2,1,0:T(8,128)(2,1)S(1)}, bf16[6,256,256]{2,1,0:T(8,128)(2,1)}, u32[]{:S(2)}) copy-start(bf16[6,256,256]{2,1,0:T(8,128)(2,1)} %copy-done) | copy-start | bytes 2359300

commit v3 on v2

--- a/solution.py
+++ b/solution.py
@@ -273,7 +273,7 @@
         out_specs=[hbm] * 2,
         scratch_shapes=here + [pltpu.SemaphoreType.DMA((layers + 1,))],
         cost_estimate=pl.CostEstimate(flops=100 * layers * amp_count, bytes_accessed=8 * layers * amp_count, transcendentals=0),
-        compiler_params=pltpu.CompilerParams(vmem_limit_bytes=24 << 20),
+        compiler_params=pltpu.CompilerParams(vmem_limit_bytes=60 << 20),
         name="tables",
     )(gate_matrices, phase_qubits.transpose(0, 2, 1), phase_angles, cut_qubits.T, cut_angle, path_index)
 
@@ -284,7 +284,7 @@
         out_specs=vmem,
         scratch_shapes=[pltpu.VMEM((2 * rows, 128), jnp.float32)] + here
         + [pltpu.VMEM((2, 2, rows, 128), jnp.float32), pltpu.SemaphoreType.DMA((2 * layers + 1,))],
-        compiler_params=pltpu.CompilerParams(vmem_limit_bytes=24 << 20),
+        compiler_params=pltpu.CompilerParams(vmem_limit_bytes=60 << 20),
         name="layers",
     )(came, weights, phases)
 

time: 29.9 us -> 29.1 us (0.973)
  local copies, waits for them, and re-layouts: 6.36 us -> 0.8 us
  waiting for transfers between devices: 2.93 us -> 7.4 us
  Pallas kernels: 12.7 us -> 13.3 us
    unnamed x16 -> x2, local copies, waits for them, and re-layouts: 6.36 us -> 0.8 us
    all_to_all x1, waiting for transfers between devices: 2.93 us -> 7.4 us  [shards(): lax.all_to_all(sent, 'hi', split_axis=0, concat_axis=0, tiled=True)]
    pallas_call x1, Pallas kernels: 6.33 us -> 7.06 us  [shards(): pl.pallas_call(functools.partial(tables_kernel, plan, rows), out_shape=(j...]
  transfers between devices with their start and end apart: 1 -> 1, of which waited for: 1 -> 1; matrix products, arithmetic and copies ran while one was open for 0% -> 0% of each run, Pallas kernels for 21% -> 24%
where the time goes in v3:
time: 29.1 us; the launch traced here: 28.9 us
  Pallas kernels  13.3 us (46%)
  waiting for transfers between devices  7.4 us (25%)
  starting transfers between devices  7.38 us (25%)
  local copies, waits for them, and re-layouts  0.8 us (3%)
    all_to_all x1, waiting for transfers between devices, shards(): lax.all_to_all(sent, 'hi', split_axis=0, concat_axis=0, tiled=True)  7.4 us
    all_to_all x1, starting transfers between devices, shards(): lax.all_to_all(sent, 'hi', split_axis=0, concat_axis=0, tiled=True)  7.38 us
    pallas_call x1, Pallas kernels, shards(): pl.pallas_call(functools.partial(tables_kernel, plan, rows), out_shape=(j...  7.06 us
    pallas_call x1, Pallas kernels, shards(): pl.pallas_call(functools.partial(layers_kernel, plan, rows), out_shape=ja...  6.21 us
    unnamed x2, local copies, waits for them, and re-layouts  0.8 us
  transfers between devices with their start and end apart: 1, of which 1 were waited for; matrix products, arithmetic and copies ran while one was open for 0% of the time, Pallas kernels for 24%

profile of v3, /device:TPU:0, one launch (start us, length us, event | category | flops | bytes accessed | tf_op | source)
XLA Modules:
  0.0 28.9 jit_solution(9310492649686028122)
XLA Ops:
  0.0 7.4 %all-to-all-start = ((f32[16,64,128]{2,1,0:T(8,128)}), f32[16,64,128]{2,1,0:T(8,128)S(1)}, u32[]{:S(2)}, u32[]{:S(2)}) async-start(f32[16,64,128]{2,1,0:T(8,128)} %bitcast.14), calls=%async_computation | async-start | bytes 1048576 | tf_op jit(solution)/shard_map/all_to_all | solution.py:260
  7.4 7.1 %tables.1 = (bf16[6,256,256]{2,1,0:T(8,128)(2,1)}, f32[6,2,512,128]{3,2,1,0:T(8,128)}) custom-call(bf16[6,2,128,128]{3,2,1,0:T(8,128)(2,1)} %gates.1, s32[6,2,8]{2,1,0:T(2,128)} %bitcast.15, f32[6,8]{1,0:T(8,128)} %pair_angles.1, s32[2,6]{1,0:T(2,128)} %bitcast.16, f32[6]{0:T(128)} %cut_angle.1, s32[6]{0:T(128)} %path_index.1), custom_call_target="tpu_custom_call" | custom-call | flops 39321600 | bytes 3145728 | tf_op jit(solution)/shard_map/tables/pallas_call | solution.py:266
  14.5 7.4 %all-to-all-done = f32[16,64,128]{2,1,0:T(8,128)S(1)} async-done(((f32[16,64,128]{2,1,0:T(8,128)}), f32[16,64,128]{2,1,0:T(8,128)S(1)}, u32[]{:S(2)}, u32[]{:S(2)}) %all-to-all-start) | async-done | bytes 524320 | tf_op jit(solution)/shard_map/all_to_all | solution.py:260
  21.9 0.0 copy-start
  21.9 0.8 %copy-done = f32[16,64,128]{2,1,0:T(8,128)} copy-done((f32[16,64,128]{2,1,0:T(8,128)}, f32[16,64,128]{2,1,0:T(8,128)S(1)}, u32[]{:S(2)}) %copy-start) | copy-done | bytes 524312
  22.7 6.2 %layers.1 = f32[1024,128]{1,0:T(8,128)} custom-call(f32[1024,128]{1,0:T(8,128)} %bitcast.13, bf16[6,256,256]{2,1,0:T(8,128)(2,1)} %get-tuple-element.7.weights, f32[6,2,512,128]{3,2,1,0:T(8,128)} %get-tuple-element.8.phases), custom_call_target="tpu_custom_call" | custom-call | tf_op jit(solution)/shard_map/layers/pallas_call | solution.py:280
Async XLA Ops:
  0.0 21.9 %all-to-all-start = ((f32[16,64,128]{2,1,0:T(8,128)}), f32[16,64,128]{2,1,0:T(8,128)S(1)}, u32[]{:S(2)}, u32[]{:S(2)}) async-start(f32[16,64,128]{2,1,0:T(8,128)} %bitcast.14), calls=%async_computation | async-start | bytes 1048576 | tf_op jit(solution)/shard_map/all_to_all | solution.py:260
  21.9 0.8 %copy-start = (f32[16,64,128]{2,1,0:T(8,128)}, f32[16,64,128]{2,1,0:T(8,128)S(1)}, u32[]{:S(2)}) copy-start(f32[16,64,128]{2,1,0:T(8,128)S(1)} %all-to-all-done) | copy-start | bytes 1572868

commit v4 on v0

--- a/solution.py
+++ b/solution.py
@@ -5,6 +5,7 @@
 import numpy as np
 from jax import lax
 from jax.experimental import pallas as pl
+from jax.experimental.layout import Layout, with_layout_constraint
 from jax.experimental.pallas import tpu as pltpu
 from jax.sharding import PartitionSpec as P
 
@@ -74,21 +75,22 @@
         order = list(range(LANE_BITS, local_bits))
         for layer, target in enumerate(self.targets):
             step = 0
-            if target in order[:3]:
-                def lasts(at):
-                    triple = order[at:at + 3]
-                    if triple == self.wanted[:3] and not set(triple) & set(self.targets[layer:]):
-                        return layers + 1
-                    return next((k for k, bit in enumerate(self.targets[layer:]) if bit in triple), layers)
-                step = max(range(1, len(order) - 2), key=lasts)
+            if target in order[:4]:
+                step = max(range(1, len(order) - 2), key=lambda at: self.lasts(order[at:at + 3], layer))
                 triple = order[step:step + 3]
-                assert target not in triple
-                if triple == self.wanted[:3]:
+                if triple == self.wanted[:3] and not set(self.wanted[:4]) & set(self.targets[layer:]):
                     order = self.wanted
                 else:
-                    order = triple + [bit for bit in order if bit not in triple]
+                    rest = sorted((bit for bit in order if bit not in triple), key=lambda bit: -self.lasts([bit], layer))
+                    order = triple + rest
+                assert target not in order[:4]
             self.steps.append(step)
             self.orders.append(order)
+
+    def lasts(self, bits, layer):
+        uses = self.targets[layer:]
+        count = next((k for k, bit in enumerate(uses) if bit in bits), len(uses))
+        return count + (count == len(uses) and bits == self.wanted[:3])
 
     def locate(self, qubit, layer):
         low, count = 7, min(layer + 1, self.global_count)
@@ -102,8 +104,9 @@
 
 
 def tables_kernel(plan, rows, gates, pair_qubits, pair_angles, cut_qubits, cut_angle, path_index,
-                  weights, cosines, sines):
+                  weights, phases, weights_here, phases_here, done):
     device_part = lax.axis_index("hi") << plan.local_bits
+    copies = []
     lane = lax.broadcasted_iota(jnp.int32, (128, 128), 1)
     for layer in range(plan.layers):
         turned = [gates[layer, part].astype(jnp.float32).T for part in range(2)]
@@ -120,31 +123,32 @@
                         part = slice(64 * from_bit, 64 * from_bit + 64)
                         both = jnp.concatenate([first[part], second[part]], axis=0)
                         at_row, at_col = 256 * from_part + 128 * from_bit, 256 * to_part + 128 * to_bit
-                        weights[layer, at_row:at_row + 128, at_col:at_col + 128] = both.astype(jnp.bfloat16)
+                        weights_here[layer, at_row:at_row + 128, at_col:at_col + 128] = both.astype(jnp.bfloat16)
+        copies.append(pltpu.make_async_copy(weights_here.at[layer], weights.at[layer], done.at[layer]))
+        copies[-1].start()
 
     block_rows = 64
     block_bits = block_rows.bit_length() - 1
     row = lax.broadcasted_iota(jnp.int32, (block_rows, 128), 0)
-    lanes = lax.broadcasted_iota(jnp.int32, (block_rows, 128), 1)
+    lane = lax.broadcasted_iota(jnp.int32, (block_rows, 128), 1)
     for layer in range(plan.layers):
         order = plan.orders[layer]
-        base = lanes + device_part
+        base = lane + device_part
         for bit in range(block_bits):
             base = base + (((row >> bit) & 1) << order[bit])
         masks, turns = [], []
-        for pair in range(pair_qubits.shape[1]):
-            first = plan.locate(pair_qubits[layer, pair, 0], layer)
-            second = plan.locate(pair_qubits[layer, pair, 1], layer)
-            one = jnp.int32(1)
+        one = jnp.int32(1)
+        for pair in range(pair_qubits.shape[2]):
+            first = plan.locate(pair_qubits[layer, 0, pair], layer)
+            second = plan.locate(pair_qubits[layer, 1, pair], layer)
             masks.append((one << first) | (one << second))
             turns.append(pair_angles[layer, pair] * np.float32(0.5 / np.pi))
         if layer == 0:
             size = jnp.ones((8, 128), jnp.float32)
             cut_masks, cut_turns = [], []
-            for cut in range(cut_qubits.shape[0]):
-                first = plan.locate(cut_qubits[cut, 0], layer)
-                second = plan.locate(cut_qubits[cut, 1], layer)
-                one = jnp.int32(1)
+            for cut in range(cut_qubits.shape[1]):
+                first = plan.locate(cut_qubits[0, cut], layer)
+                second = plan.locate(cut_qubits[1, cut], layer)
                 cut_masks.append((one << first) | (one << second))
                 chosen = path_index[cut] == 0
                 cosine, sine = turn(jnp.full((8, 128), cut_angle[cut] * np.float32(0.5 / np.pi)))
@@ -169,52 +173,79 @@
             if layer == 0:
                 cosine, sine = cosine * size, sine * size
             at = pl.ds(pl.multiple_of(block * block_rows, block_rows), block_rows)
-            cosines[layer, at, :] = cosine
-            sines[layer, at, :] = sine
+            phases_here[layer, 0, at, :] = cosine
+            phases_here[layer, 1, at, :] = sine
+
+        copies.append(pltpu.make_async_copy(phases_here.at[layer], phases.at[layer], done.at[plan.layers + layer]))
+        copies[-1].start()
+    for copy in copies:
+        copy.wait()
 
 
 def offset_of(number, bits, order):
     return sum(((number >> k) & 1) << order.index(bit) for k, bit in enumerate(bits))
 
 
-def layers_kernel(plan, rows, state, weights, cosines, sines, out, held):
-    order = list(range(LANE_BITS, plan.local_bits))
-    for layer in range(plan.layers):
-        new_order, step, target = plan.orders[layer], plan.steps[layer], plan.targets[layer]
-        rest = [bit for bit in new_order if bit != target]
+def split(values):
+    large = values.astype(jnp.bfloat16)
+    return large, (values - large.astype(jnp.float32)).astype(jnp.bfloat16)
+
+
+def layers_kernel(plan, rows, state, weights, phases, out, weights_here, phases_here, held, parts, done):
+    layers = plan.layers
+    copies = []
+    for layer in range(layers):
+        copies.append(pltpu.make_async_copy(weights.at[layer], weights_here.at[layer], done.at[2 * layer]))
+        copies.append(pltpu.make_async_copy(phases.at[layer], phases_here.at[layer], done.at[2 * layer + 1]))
+    for copy in copies:
+        copy.start()
+
+    old_order = list(range(LANE_BITS, plan.local_bits))
+    for layer in range(layers):
+        order, step, target = plan.orders[layer], plan.steps[layer], plan.targets[layer]
+        rest = [bit for bit in order if bit != target]
         pieces = []
         for part in range(2):
             for side in range(2):
-                tiles = []
-                for tile in range(rows // 16):
-                    at = offset_of(tile, rest[3:], order) + side * (1 << order.index(target))
-                    if layer == 0:
-                        tiles.append(state[pl.ds(2 * at + part, 8, 2 << step), :])
-                    elif step:
-                        tiles.append(held[(layer - 1) % 2, part, pl.ds(at, 8, 1 << step), :])
+                if layer == 0 or step:
+                    tiles = []
+                    for tile in range(rows // 16):
+                        at = offset_of(tile, rest[3:], old_order) + (side << old_order.index(target))
+                        if layer == 0:
+                            tiles.append(state[pl.ds(2 * at + part, 8, 2 << step), :])
+                        else:
+                            tiles.append(held[part, pl.ds(at, 8, 1 << step), :])
+                    pieces.append(split(jnp.concatenate(tiles, axis=0)))
+                else:
+                    starts = [offset_of(tile, rest[4:], order) + (side << order.index(target))
+                              for tile in range(rows // 32)]
+                    pieces.append([
+                        jnp.concatenate([parts[layer % 2, size, part, at:at + 16, :] for at in starts], axis=0)
+                        for size in range(2)
+                    ])
+        joined = jnp.concatenate(
+            [jnp.concatenate([piece[size] for piece in pieces], axis=1) for size in range(2)], axis=0
+        )
+        copies[2 * layer].wait()
+        both = jnp.dot(joined, weights_here[layer], preferred_element_type=jnp.float32)
+        result = both[:rows // 2] + both[rows // 2:]
+        copies[2 * layer + 1].wait()
+        for side in range(2):
+            for tile in range(rows // 32):
+                at = offset_of(tile, rest[4:], order) + (side << order.index(target))
+                real = result[16 * tile:16 * tile + 16, 128 * side:128 * side + 128]
+                imag = result[16 * tile:16 * tile + 16, 256 + 128 * side:384 + 128 * side]
+                cosine, sine = phases_here[layer, 0, at:at + 16, :], phases_here[layer, 1, at:at + 16, :]
+                for part, value in enumerate((cosine * real - sine * imag, sine * real + cosine * imag)):
+                    if layer == layers - 1:
+                        out[pl.ds(2 * at + part, 16, 2), :] = value
+                    elif plan.steps[layer + 1]:
+                        held[part, at:at + 16, :] = value
                     else:
-                        tiles.append(held[(layer - 1) % 2, part, pl.ds(at, 8), :])
-                pieces.append(jnp.concatenate(tiles, axis=0))
-        joined = jnp.concatenate(pieces, axis=1)
-        large = joined.astype(jnp.bfloat16)
-        small = (joined - large.astype(jnp.float32)).astype(jnp.bfloat16)
-        both = jnp.dot(jnp.concatenate([large, small], axis=0), weights[layer],
-                       preferred_element_type=jnp.float32)
-        result = both[:rows // 2] + both[rows // 2:]
-        for side in range(2):
-            for tile in range(rows // 16):
-                at = offset_of(tile, rest[3:], new_order) + side * (1 << new_order.index(target))
-                real = result[8 * tile:8 * tile + 8, 128 * side:128 * side + 128]
-                imag = result[8 * tile:8 * tile + 8, 256 + 128 * side:384 + 128 * side]
-                cosine, sine = cosines[layer, at:at + 8, :], sines[layer, at:at + 8, :]
-                new_real, new_imag = cosine * real - sine * imag, sine * real + cosine * imag
-                if layer == plan.layers - 1:
-                    out[pl.ds(2 * at, 8, 2), :] = new_real
-                    out[pl.ds(2 * at + 1, 8, 2), :] = new_imag
-                else:
-                    held[layer % 2, 0, at:at + 8, :] = new_real
-                    held[layer % 2, 1, at:at + 8, :] = new_imag
-        order = new_order
+                        large, small = split(value)
+                        parts[(layer + 1) % 2, 0, part, at:at + 16, :] = large
+                        parts[(layer + 1) % 2, 1, part, at:at + 16, :] = small
+        old_order = order
 
 
 def shards(
@@ -227,30 +258,41 @@
     layers = gate_matrices.shape[0]
     plan = Plan(global_count, amp_count.bit_length() - 1, layers)
 
-    sent = amplitudes.reshape(2, rows, 128).transpose(1, 0, 2).reshape(devices, -1, 128)
+    shaped = with_layout_constraint(amplitudes.reshape(2, rows, 128), Layout(major_to_minor=(1, 0, 2)))
+    sent = shaped.transpose(1, 0, 2).reshape(devices, -1, 128)
     came = lax.all_to_all(sent, "hi", split_axis=0, concat_axis=0, tiled=True).reshape(2 * rows, 128)
 
     vmem, smem = pl.BlockSpec(memory_space=pltpu.VMEM), pl.BlockSpec(memory_space=pltpu.SMEM)
-    table = jax.ShapeDtypeStruct((layers, rows, 128), jnp.float32)
-    weights, cosines, sines = pl.pallas_call(
+    hbm = pl.BlockSpec(memory_space=pltpu.HBM)
+    weights_shape, phases_shape = (layers, 512, 512), (layers, 2, rows, 128)
+    here = [pltpu.VMEM(weights_shape, jnp.bfloat16), pltpu.VMEM(phases_shape, jnp.float32)]
+    weights, phases = pl.pallas_call(
         functools.partial(tables_kernel, plan, rows),
-        out_shape=(jax.ShapeDtypeStruct((layers, 512, 512), jnp.bfloat16), table, table),
+        out_shape=(
+            jax.ShapeDtypeStruct(weights_shape, jnp.bfloat16),
+            jax.ShapeDtypeStruct(phases_shape, jnp.float32),
+        ),
         in_specs=[vmem] + [smem] * 5,
-        out_specs=[vmem] * 3,
-        cost_estimate=pl.CostEstimate(flops=100 * layers * amp_count, bytes_accessed=4 * layers * amp_count, transcendentals=0),
-        compiler_params=pltpu.CompilerParams(vmem_limit_bytes=40 << 20),
+        out_specs=[hbm] * 2,
+        scratch_shapes=here + [pltpu.SemaphoreType.DMA((2 * layers,))],
+        cost_estimate=pl.CostEstimate(flops=100 * layers * amp_count, bytes_accessed=8 * layers * amp_count, transcendentals=0),
+        compiler_params=pltpu.CompilerParams(vmem_limit_bytes=60 << 20),
         name="tables",
-    )(gate_matrices, phase_qubits, phase_angles, cut_qubits, cut_angle, path_index)
+    )(gate_matrices, phase_qubits.transpose(0, 2, 1), phase_angles, cut_qubits.T, cut_angle, path_index)
 
     result = pl.pallas_call(
         functools.partial(layers_kernel, plan, rows),
         out_shape=jax.ShapeDtypeStruct((2 * rows, 128), jnp.float32),
-        in_specs=[vmem] * 4,
+        in_specs=[vmem, hbm, hbm],
         out_specs=vmem,
-        scratch_shapes=[pltpu.VMEM((2, 2, rows, 128), jnp.float32)],
-        compiler_params=pltpu.CompilerParams(vmem_limit_bytes=40 << 20),
+        scratch_shapes=here + [
+            pltpu.VMEM((2, rows, 128), jnp.float32),
+            pltpu.VMEM((2, 2, 2, rows, 128), jnp.bfloat16),
+            pltpu.SemaphoreType.DMA((2 * layers,)),
+        ],
+        compiler_params=pltpu.CompilerParams(vmem_limit_bytes=58 << 20),
         name="layers",
-    )(came, weights, cosines, sines)
+    )(came, weights, phases)
 
     if plan.orders[-1] != plan.wanted:
         bits = len(plan.wanted)

time: 31.8 us -> 29.5 us (0.928)
  local copies, waits for them, and re-layouts: 9 us -> 0.8 us
  Pallas kernels: 10.7 us -> 14.2 us
  waiting for transfers between devices: 4.2 us -> 6.82 us
    unnamed x25 -> x2, local copies, waits for them, and re-layouts: 7.8 us -> 0.8 us
    all_to_all x1, waiting for transfers between devices: 4.2 us -> 6.82 us  [shards(): lax.all_to_all(sent, 'hi', split_axis=0, concat_axis=0, tiled=True)]
    pallas_call x1, Pallas kernels: 4.27 us -> 6.59 us  [shards(): pl.pallas_call(functools.partial(layers_kernel, plan, rows), out_shape=ja...]
    pallas_call x1, Pallas kernels: 6.43 us -> 7.64 us  [shards(): pl.pallas_call(functools.partial(tables_kernel, plan, rows), out_shape=(j...]
    transpose x1 -> x0, local copies, waits for them, and re-layouts: 1.2 us -> none  [shards(): amplitudes.reshape(2, rows, 128).transpose(1, 0, 2)]
  transfers between devices with their start and end apart: 1 -> 1, of which waited for: 1 -> 1; matrix products, arithmetic and copies ran while one was open for 3% -> 0% of each run, Pallas kernels for 20% -> 26%
where the time goes in v4:
time: 29.5 us; the launch traced here: 29.2 us
  Pallas kernels  14.2 us (48%)
  starting transfers between devices  7.38 us (25%)
  waiting for transfers between devices  6.82 us (23%)
  local copies, waits for them, and re-layouts  0.8 us (3%)
    pallas_call x1, Pallas kernels, shards(): pl.pallas_call(functools.partial(tables_kernel, plan, rows), out_shape=(j...  7.64 us
    all_to_all x1, starting transfers between devices, shards(): lax.all_to_all(sent, 'hi', split_axis=0, concat_axis=0, tiled=True)  7.38 us
    all_to_all x1, waiting for transfers between devices, shards(): lax.all_to_all(sent, 'hi', split_axis=0, concat_axis=0, tiled=True)  6.82 us
    pallas_call x1, Pallas kernels, shards(): pl.pallas_call(functools.partial(layers_kernel, plan, rows), out_shape=ja...  6.59 us
    unnamed x2, local copies, waits for them, and re-layouts  0.8 us
  transfers between devices with their start and end apart: 1, of which 1 were waited for; matrix products, arithmetic and copies ran while one was open for 0% of the time, Pallas kernels for 26%

profile of v4, /device:TPU:0, one launch (start us, length us, event | category | flops | bytes accessed | tf_op | source)
XLA Modules:
  0.0 29.2 jit_solution(10484619641165862697)
XLA Ops:
  0.0 7.4 %all-to-all-start = ((f32[16,64,128]{2,1,0:T(8,128)}), f32[16,64,128]{2,1,0:T(8,128)S(1)}, u32[]{:S(2)}, u32[]{:S(2)}) async-start(f32[16,64,128]{2,1,0:T(8,128)} %bitcast.14), calls=%async_computation | async-start | bytes 1048576 | tf_op jit(solution)/shard_map/all_to_all | solution.py:263
  7.4 7.6 %tables.1 = (bf16[6,512,512]{2,1,0:T(8,128)(2,1)}, f32[6,2,512,128]{3,2,1,0:T(8,128)}) custom-call(bf16[6,2,128,128]{3,2,1,0:T(8,128)(2,1)} %gates.1, s32[6,2,8]{2,1,0:T(2,128)} %bitcast.15, f32[6,8]{1,0:T(8,128)} %pair_angles.1, s32[2,6]{1,0:T(2,128)} %bitcast.16, f32[6]{0:T(128)} %cut_angle.1, s32[6]{0:T(128)} %path_index.1), custom_call_target="tpu_custom_call" | custom-call | flops 39321600 | bytes 3145728 | tf_op jit(solution)/shard_map/tables/pallas_call | solution.py:269
  15.0 6.8 %all-to-all-done = f32[16,64,128]{2,1,0:T(8,128)S(1)} async-done(((f32[16,64,128]{2,1,0:T(8,128)}), f32[16,64,128]{2,1,0:T(8,128)S(1)}, u32[]{:S(2)}, u32[]{:S(2)}) %all-to-all-start) | async-done | bytes 524320 | tf_op jit(solution)/shard_map/all_to_all | solution.py:263
  21.9 0.0 copy-start
  21.9 0.8 %copy-done = f32[16,64,128]{2,1,0:T(8,128)} copy-done((f32[16,64,128]{2,1,0:T(8,128)}, f32[16,64,128]{2,1,0:T(8,128)S(1)}, u32[]{:S(2)}) %copy-start) | copy-done | bytes 524312
  22.7 6.6 %layers.1 = f32[1024,128]{1,0:T(8,128)} custom-call(f32[1024,128]{1,0:T(8,128)} %bitcast.13, bf16[6,512,512]{2,1,0:T(8,128)(2,1)} %get-tuple-element.7.weights, f32[6,2,512,128]{3,2,1,0:T(8,128)} %get-tuple-element.8.phases), custom_call_target="tpu_custom_call" | custom-call | tf_op jit(solution)/shard_map/layers/pallas_call | solution.py:283
Async XLA Ops:
  0.0 21.9 %all-to-all-start = ((f32[16,64,128]{2,1,0:T(8,128)}), f32[16,64,128]{2,1,0:T(8,128)S(1)}, u32[]{:S(2)}, u32[]{:S(2)}) async-start(f32[16,64,128]{2,1,0:T(8,128)} %bitcast.14), calls=%async_computation | async-start | bytes 1048576 | tf_op jit(solution)/shard_map/all_to_all | solution.py:263
  21.9 0.8 %copy-start = (f32[16,64,128]{2,1,0:T(8,128)}, f32[16,64,128]{2,1,0:T(8,128)S(1)}, u32[]{:S(2)}) copy-start(f32[16,64,128]{2,1,0:T(8,128)S(1)} %all-to-all-done) | copy-start | bytes 1572868

commit v5 on v4

--- a/solution.py
+++ b/solution.py
@@ -11,6 +11,7 @@
 
 LANE_BITS = 7
 GATE_BITS = 6
+STEPS = 32767.0
 
 
 def fitted(function, degree):
@@ -104,28 +105,27 @@
 
 
 def tables_kernel(plan, rows, gates, pair_qubits, pair_angles, cut_qubits, cut_angle, path_index,
-                  weights, phases, weights_here, phases_here, done):
+                  near, far, phases, sizes, far_here, done):
     device_part = lax.axis_index("hi") << plan.local_bits
-    copies = []
     lane = lax.broadcasted_iota(jnp.int32, (128, 128), 1)
-    for layer in range(plan.layers):
-        turned = [gates[layer, part].astype(jnp.float32).T for part in range(2)]
-        for from_part in range(2):
-            for to_part in range(2):
-                block = turned[from_part ^ to_part]
-                if (from_part, to_part) == (1, 0):
-                    block = -block
-                for to_bit in range(2):
-                    kept = jnp.where((lane >= 64) == (to_bit == 1), block, 0.0)
-                    moved = pltpu.roll(kept, 64, 1)
-                    first, second = (kept, moved) if to_bit == 0 else (moved, kept)
-                    for from_bit in range(2):
-                        part = slice(64 * from_bit, 64 * from_bit + 64)
-                        both = jnp.concatenate([first[part], second[part]], axis=0)
-                        at_row, at_col = 256 * from_part + 128 * from_bit, 256 * to_part + 128 * to_bit
-                        weights_here[layer, at_row:at_row + 128, at_col:at_col + 128] = both.astype(jnp.bfloat16)
-        copies.append(pltpu.make_async_copy(weights_here.at[layer], weights.at[layer], done.at[layer]))
-        copies[-1].start()
+    for layer in range(plan.layers - 1, -1, -1):
+        for kind in range(2):
+            turned = gates[layer, kind].astype(jnp.float32).T
+            for to_bit in range(2):
+                kept = jnp.where((lane >= 64) == (to_bit == 1), turned, 0.0)
+                moved = pltpu.roll(kept, 64, 1)
+                first, second = (kept, moved) if to_bit == 0 else (moved, kept)
+                for from_bit in range(2):
+                    part = slice(64 * from_bit, 64 * from_bit + 64)
+                    both = jnp.concatenate([first[part], second[part]], axis=0).astype(jnp.bfloat16)
+                    at_row, at_col = slice(128 * from_bit, 128 * from_bit + 128), slice(128 * to_bit, 128 * to_bit + 128)
+                    if layer == plan.layers - 1:
+                        far_here[kind, at_row, at_col] = both
+                    else:
+                        near[layer, kind, at_row, at_col] = both
+        if layer == plan.layers - 1:
+            copy = pltpu.make_async_copy(far_here, far, done)
+            copy.start()
 
     block_rows = 64
     block_bits = block_rows.bit_length() - 1
@@ -154,7 +154,7 @@
                 cosine, sine = turn(jnp.full((8, 128), cut_angle[cut] * np.float32(0.5 / np.pi)))
                 size = size * jnp.where(chosen, cosine, sine)
                 cut_turns.append(jnp.where(chosen, 0.0, 0.25))
-            size = jnp.broadcast_to(size[:1], (block_rows, 128))
+            sizes[...] = size
 
         @pl.loop(0, rows // block_rows)
         def _(block):
@@ -170,16 +170,12 @@
                     both = index & mask
                     angle = angle + jnp.where((both == 0) | (both == mask), -amount, amount)
             cosine, sine = turn(angle)
-            if layer == 0:
-                cosine, sine = cosine * size, sine * size
             at = pl.ds(pl.multiple_of(block * block_rows, block_rows), block_rows)
-            phases_here[layer, 0, at, :] = cosine
-            phases_here[layer, 1, at, :] = sine
-
-        copies.append(pltpu.make_async_copy(phases_here.at[layer], phases.at[layer], done.at[plan.layers + layer]))
-        copies[-1].start()
-    for copy in copies:
-        copy.wait()
+            cosine = jnp.round(cosine * STEPS).astype(jnp.int32)
+            sine = jnp.round(sine * STEPS).astype(jnp.int32)
+            phases[layer, at, :] = (cosine << 16) | (sine & 0xFFFF)
+
+    copy.wait()
 
 
 def offset_of(number, bits, order):
@@ -191,14 +187,10 @@
     return large, (values - large.astype(jnp.float32)).astype(jnp.bfloat16)
 
 
-def layers_kernel(plan, rows, state, weights, phases, out, weights_here, phases_here, held, parts, done):
+def layers_kernel(plan, rows, state, near, far, phases, sizes, out, far_here, held, parts, done):
     layers = plan.layers
-    copies = []
-    for layer in range(layers):
-        copies.append(pltpu.make_async_copy(weights.at[layer], weights_here.at[layer], done.at[2 * layer]))
-        copies.append(pltpu.make_async_copy(phases.at[layer], phases_here.at[layer], done.at[2 * layer + 1]))
-    for copy in copies:
-        copy.start()
+    copy = pltpu.make_async_copy(far, far_here, done)
+    copy.start()
 
     old_order = list(range(LANE_BITS, plan.local_bits))
     for layer in range(layers):
@@ -226,16 +218,28 @@
         joined = jnp.concatenate(
             [jnp.concatenate([piece[size] for piece in pieces], axis=1) for size in range(2)], axis=0
         )
-        copies[2 * layer].wait()
-        both = jnp.dot(joined, weights_here[layer], preferred_element_type=jnp.float32)
+        if layer == layers - 1:
+            copy.wait()
+            weights = far_here
+        else:
+            weights = near.at[layer]
+        real, imag = weights[0], weights[1]
+        weight = jnp.concatenate(
+            [jnp.concatenate([real, imag], axis=1), jnp.concatenate([-imag, real], axis=1)], axis=0
+        )
+        both = jnp.dot(joined, weight, preferred_element_type=jnp.float32)
         result = both[:rows // 2] + both[rows // 2:]
-        copies[2 * layer + 1].wait()
+        unit = jnp.full((16, 128), 1 / STEPS, jnp.float32)
+        if layer == 0:
+            unit = unit * sizes[0:1, :]
         for side in range(2):
             for tile in range(rows // 32):
                 at = offset_of(tile, rest[4:], order) + (side << order.index(target))
                 real = result[16 * tile:16 * tile + 16, 128 * side:128 * side + 128]
                 imag = result[16 * tile:16 * tile + 16, 256 + 128 * side:384 + 128 * side]
-                cosine, sine = phases_here[layer, 0, at:at + 16, :], phases_here[layer, 1, at:at + 16, :]
+                word = phases[layer, at:at + 16, :]
+                cosine = (word >> 16).astype(jnp.float32) * unit
+                sine = ((word << 16) >> 16).astype(jnp.float32) * unit
                 for part, value in enumerate((cosine * real - sine * imag, sine * real + cosine * imag)):
                     if layer == layers - 1:
                         out[pl.ds(2 * at + part, 16, 2), :] = value
@@ -264,35 +268,37 @@
 
     vmem, smem = pl.BlockSpec(memory_space=pltpu.VMEM), pl.BlockSpec(memory_space=pltpu.SMEM)
     hbm = pl.BlockSpec(memory_space=pltpu.HBM)
-    weights_shape, phases_shape = (layers, 512, 512), (layers, 2, rows, 128)
-    here = [pltpu.VMEM(weights_shape, jnp.bfloat16), pltpu.VMEM(phases_shape, jnp.float32)]
-    weights, phases = pl.pallas_call(
+    weights_shape = (2, 256, 256)
+    near, far, phases, sizes = pl.pallas_call(
         functools.partial(tables_kernel, plan, rows),
         out_shape=(
+            jax.ShapeDtypeStruct((layers - 1,) + weights_shape, jnp.bfloat16),
             jax.ShapeDtypeStruct(weights_shape, jnp.bfloat16),
-            jax.ShapeDtypeStruct(phases_shape, jnp.float32),
+            jax.ShapeDtypeStruct((layers, rows, 128), jnp.int32),
+            jax.ShapeDtypeStruct((8, 128), jnp.float32),
         ),
         in_specs=[vmem] + [smem] * 5,
-        out_specs=[hbm] * 2,
-        scratch_shapes=here + [pltpu.SemaphoreType.DMA((2 * layers,))],
-        cost_estimate=pl.CostEstimate(flops=100 * layers * amp_count, bytes_accessed=8 * layers * amp_count, transcendentals=0),
-        compiler_params=pltpu.CompilerParams(vmem_limit_bytes=60 << 20),
+        out_specs=[vmem, hbm, vmem, vmem],
+        scratch_shapes=[pltpu.VMEM(weights_shape, jnp.bfloat16), pltpu.SemaphoreType.DMA],
+        cost_estimate=pl.CostEstimate(flops=100 * layers * amp_count, bytes_accessed=4 * layers * amp_count, transcendentals=0),
+        compiler_params=pltpu.CompilerParams(vmem_limit_bytes=24 << 20),
         name="tables",
     )(gate_matrices, phase_qubits.transpose(0, 2, 1), phase_angles, cut_qubits.T, cut_angle, path_index)
 
     result = pl.pallas_call(
         functools.partial(layers_kernel, plan, rows),
         out_shape=jax.ShapeDtypeStruct((2 * rows, 128), jnp.float32),
-        in_specs=[vmem, hbm, hbm],
+        in_specs=[vmem, vmem, hbm, vmem, vmem],
         out_specs=vmem,
-        scratch_shapes=here + [
+        scratch_shapes=[
+            pltpu.VMEM(weights_shape, jnp.bfloat16),
             pltpu.VMEM((2, rows, 128), jnp.float32),
             pltpu.VMEM((2, 2, 2, rows, 128), jnp.bfloat16),
-            pltpu.SemaphoreType.DMA((2 * layers,)),
+            pltpu.SemaphoreType.DMA,
         ],
-        compiler_params=pltpu.CompilerParams(vmem_limit_bytes=58 << 20),
+        compiler_params=pltpu.CompilerParams(vmem_limit_bytes=24 << 20),
         name="layers",
-    )(came, weights, phases)
+    )(came, near, far, phases, sizes)
 
     if plan.orders[-1] != plan.wanted:
         bits = len(plan.wanted)

time: 29.5 us -> 27 us (0.915)
  local copies, waits for them, and re-layouts: 0.8 us -> 6 us
  waiting for transfers between devices: 6.82 us -> 2.62 us
  Pallas kernels: 14.2 us -> 10.5 us
    unnamed x2 -> x16, local copies, waits for them, and re-layouts: 0.8 us -> 6 us
    all_to_all x1, waiting for transfers between devices: 6.82 us -> 2.62 us  [shards(): lax.all_to_all(sent, 'hi', split_axis=0, concat_axis=0, tiled=True)]
    pallas_call x1, Pallas kernels: 6.59 us -> 3.78 us  [shards(): pl.pallas_call(functools.partial(layers_kernel, plan, rows), out_shape=ja...]
    pallas_call x1, Pallas kernels: 7.64 us -> 6.76 us  [shards(): pl.pallas_call(functools.partial(tables_kernel, plan, rows), out_shape=(j...]
  transfers between devices with their start and end apart: 1 -> 1, of which waited for: 1 -> 1; matrix products, arithmetic and copies ran while one was open for 0% -> 0% of each run, Pallas kernels for 26% -> 25%
where the time goes in v5:
time: 27 us; the launch traced here: 26.6 us
  Pallas kernels  10.5 us (39%)
  starting transfers between devices  7.38 us (27%)
  local copies, waits for them, and re-layouts  6 us (22%)
  waiting for transfers between devices  2.62 us (10%)
    all_to_all x1, starting transfers between devices, shards(): lax.all_to_all(sent, 'hi', split_axis=0, concat_axis=0, tiled=True)  7.38 us
    pallas_call x1, Pallas kernels, shards(): pl.pallas_call(functools.partial(tables_kernel, plan, rows), out_shape=(j...  6.76 us
    unnamed x16, local copies, waits for them, and re-layouts  6 us
    pallas_call x1, Pallas kernels, shards(): pl.pallas_call(functools.partial(layers_kernel, plan, rows), out_shape=ja...  3.78 us
    all_to_all x1, waiting for transfers between devices, shards(): lax.all_to_all(sent, 'hi', split_axis=0, concat_axis=0, tiled=True)  2.62 us
  transfers between devices with their start and end apart: 1, of which 1 were waited for; matrix products, arithmetic and copies ran while one was open for 0% of the time, Pallas kernels for 25%

profile of v5, /device:TPU:0, one launch (start us, length us, event | category | flops | bytes accessed | tf_op | source)
XLA Modules:
  0.0 26.6 jit_solution(11105910979301816705)
XLA Ops:
  0.0 7.4 %all-to-all-start = ((f32[16,64,128]{2,1,0:T(8,128)}), f32[16,64,128]{2,1,0:T(8,128)S(1)}, u32[]{:S(2)}, u32[]{:S(2)}) async-start(f32[16,64,128]{2,1,0:T(8,128)} %bitcast.16), calls=%async_computation | async-start | bytes 1048576 | tf_op jit(solution)/shard_map/all_to_all | solution.py:267
  7.4 0.0 copy-start
  7.4 1.0 %copy-done = bf16[6,2,128,128]{3,2,1,0:T(8,128)(2,1)S(1)} copy-done((bf16[6,2,128,128]{3,2,1,0:T(8,128)(2,1)S(1)}, bf16[6,2,128,128]{3,2,1,0:T(8,128)(2,1)}, u32[]{:S(2)}) %copy-start) | copy-done | bytes 393240
  8.4 0.0 copy-start.3
  8.4 0.7 %copy-done.3 = s32[6,8,2]{1,2,0:T(2,128)S(1)} copy-done((s32[6,8,2]{1,2,0:T(2,128)S(1)}, s32[6,8,2]{1,2,0:T(2,128)}, u32[]{:S(2)}) %copy-start.3) | copy-done | bytes 408
  9.1 0.0 copy-start.4
  9.1 0.7 %copy-done.4 = f32[6,8]{1,0:T(8,128)S(1)} copy-done((f32[6,8]{1,0:T(8,128)S(1)}, f32[6,8]{1,0:T(8,128)}, u32[]{:S(2)}) %copy-start.4) | copy-done | bytes 216
  9.8 0.0 copy-start.5
  9.8 0.7 %copy-done.5 = s32[6,2]{0,1:T(2,128)S(1)} copy-done((s32[6,2]{0,1:T(2,128)S(1)}, s32[6,2]{0,1:T(2,128)}, u32[]{:S(2)}) %copy-start.5) | copy-done | bytes 72
  10.5 0.0 copy-start.6
  10.5 0.7 %copy-done.6 = f32[6]{0:T(128)S(1)} copy-done((f32[6]{0:T(128)S(1)}, f32[6]{0:T(128)}, u32[]{:S(2)}) %copy-start.6) | copy-done | bytes 48
  11.1 0.0 copy-start.7
  11.1 0.7 %copy-done.7 = s32[6]{0:T(128)S(1)} copy-done((s32[6]{0:T(128)S(1)}, s32[6]{0:T(128)}, u32[]{:S(2)}) %copy-start.7) | copy-done | bytes 48
  11.8 6.8 %tables.1 = (bf16[5,2,256,256]{3,2,1,0:T(8,128)(2,1)S(1)}, bf16[2,256,256]{2,1,0:T(8,128)(2,1)S(1)}, s32[6,512,128]{2,1,0:T(8,128)S(1)}, f32[8,128]{1,0:T(8,128)S(1)}) custom-call(bf16[6,2,128,128]{3,2,1,0:T(8,128)(2,1)S(1)} %copy-done, s32[6,2,8]{2,1,0:T(2,128)S(1)} %bitcast.14, f32[6,8]{1,0:T(8,128)S(1)} %copy-done.4, s32[2,6]{1,0:T(2,128)S(1)} %bitcast.15, ...), custom_call_target="tpu_custom_call" | custom-call | flops 39321600 | bytes 1572864 | tf_op jit(solution)/shard_map/tables/pallas_call | solution.py:272
  18.5 0.0 copy-start.1
  18.5 0.7 %copy-done.1 = bf16[2,256,256]{2,1,0:T(8,128)(2,1)} copy-done((bf16[2,256,256]{2,1,0:T(8,128)(2,1)}, bf16[2,256,256]{2,1,0:T(8,128)(2,1)S(1)}, u32[]{:S(2)}) %copy-start.1) | copy-done | bytes 262168
  19.2 2.6 %all-to-all-done = f32[16,64,128]{2,1,0:T(8,128)S(1)} async-done(((f32[16,64,128]{2,1,0:T(8,128)}), f32[16,64,128]{2,1,0:T(8,128)S(1)}, u32[]{:S(2)}, u32[]{:S(2)}) %all-to-all-start) | async-done | bytes 524320 | tf_op jit(solution)/shard_map/all_to_all | solution.py:267
  21.9 0.0 copy-start.2
  21.9 0.9 %copy-done.2 = bf16[2,256,256]{2,1,0:T(8,128)(2,1)S(1)} copy-done((bf16[2,256,256]{2,1,0:T(8,128)(2,1)S(1)}, bf16[2,256,256]{2,1,0:T(8,128)(2,1)}, u32[]{:S(2)}) %copy-start.2) | copy-done | bytes 262168
  22.8 3.8 %layers.1 = f32[1024,128]{1,0:T(8,128)} custom-call(f32[1024,128]{1,0:T(8,128)S(1)} %bitcast.13, bf16[5,2,256,256]{3,2,1,0:T(8,128)(2,1)S(1)} %get-tuple-element.9.near, bf16[2,256,256]{2,1,0:T(8,128)(2,1)S(1)} %copy-done.2, s32[6,512,128]{2,1,0:T(8,128)S(1)} %get-tuple-element.11.phases, f32[8,128]{1,0:T(8,128)S(1)} %get-tuple-element.12.sizes), custom_call_target="tpu_custom_call" | custom-call | tf_op jit(solution)/shard_map/layers/pallas_call | solution.py:288
Async XLA Ops:
  0.0 21.9 %all-to-all-start = ((f32[16,64,128]{2,1,0:T(8,128)}), f32[16,64,128]{2,1,0:T(8,128)S(1)}, u32[]{:S(2)}, u32[]{:S(2)}) async-start(f32[16,64,128]{2,1,0:T(8,128)} %bitcast.16), calls=%async_computation | async-start | bytes 1048576 | tf_op jit(solution)/shard_map/all_to_all | solution.py:267
  7.4 1.0 %copy-start = (bf16[6,2,128,128]{3,2,1,0:T(8,128)(2,1)S(1)}, bf16[6,2,128,128]{3,2,1,0:T(8,128)(2,1)}, u32[]{:S(2)}) copy-start(bf16[6,2,128,128]{3,2,1,0:T(8,128)(2,1)} %gates.1) | copy-start | bytes 1179652
  8.4 0.7 %copy-start.3 = (s32[6,8,2]{1,2,0:T(2,128)S(1)}, s32[6,8,2]{1,2,0:T(2,128)}, u32[]{:S(2)}) copy-start(s32[6,8,2]{1,2,0:T(2,128)} %param.9) | copy-start | bytes 1156
  9.1 0.7 %copy-start.4 = (f32[6,8]{1,0:T(8,128)S(1)}, f32[6,8]{1,0:T(8,128)}, u32[]{:S(2)}) copy-start(f32[6,8]{1,0:T(8,128)} %pair_angles.1) | copy-start | bytes 580
  9.8 0.7 %copy-start.5 = (s32[6,2]{0,1:T(2,128)S(1)}, s32[6,2]{0,1:T(2,128)}, u32[]{:S(2)}) copy-start(s32[6,2]{0,1:T(2,128)} %param.11) | copy-start | bytes 148
  10.5 0.7 %copy-start.6 = (f32[6]{0:T(128)S(1)}, f32[6]{0:T(128)}, u32[]{:S(2)}) copy-start(f32[6]{0:T(128)} %cut_angle.1) | copy-start | bytes 76
  11.1 0.7 %copy-start.7 = (s32[6]{0:T(128)S(1)}, s32[6]{0:T(128)}, u32[]{:S(2)}) copy-start(s32[6]{0:T(128)} %path_index.1) | copy-start | bytes 76
  18.5 0.7 %copy-start.1 = (bf16[2,256,256]{2,1,0:T(8,128)(2,1)}, bf16[2,256,256]{2,1,0:T(8,128)(2,1)S(1)}, u32[]{:S(2)}) copy-start(bf16[2,256,256]{2,1,0:T(8,128)(2,1)S(1)} %get-tuple-element.10.far) | copy-start | bytes 786436
  21.9 1.0 %copy-start.2 = (bf16[2,256,256]{2,1,0:T(8,128)(2,1)S(1)}, bf16[2,256,256]{2,1,0:T(8,128)(2,1)}, u32[]{:S(2)}) copy-start(bf16[2,256,256]{2,1,0:T(8,128)(2,1)} %copy-done.1) | copy-start | bytes 786436

commit v6 on v5

--- a/solution.py
+++ b/solution.py
@@ -104,28 +104,28 @@
         return jnp.where(label >= high, label - size, jnp.where(label >= self.top, label + size, label))
 
 
+def widen(turned, block):
+    lane = lax.broadcasted_iota(jnp.int32, (128, 128), 1)
+    for to_bit in range(2):
+        kept = jnp.where((lane >= 64) == (to_bit == 1), turned, 0.0)
+        moved = pltpu.roll(kept, 64, 1)
+        first, second = (kept, moved) if to_bit == 0 else (moved, kept)
+        for from_bit in range(2):
+            part = slice(64 * from_bit, 64 * from_bit + 64)
+            both = jnp.concatenate([first[part], second[part]], axis=0)
+            block[128 * from_bit:128 * from_bit + 128, 128 * to_bit:128 * to_bit + 128] = both.astype(jnp.bfloat16)
+
+
 def tables_kernel(plan, rows, gates, pair_qubits, pair_angles, cut_qubits, cut_angle, path_index,
-                  near, far, phases, sizes, far_here, done):
+                  near, last, phases, sizes):
     device_part = lax.axis_index("hi") << plan.local_bits
-    lane = lax.broadcasted_iota(jnp.int32, (128, 128), 1)
-    for layer in range(plan.layers - 1, -1, -1):
+    for layer in range(plan.layers):
         for kind in range(2):
             turned = gates[layer, kind].astype(jnp.float32).T
-            for to_bit in range(2):
-                kept = jnp.where((lane >= 64) == (to_bit == 1), turned, 0.0)
-                moved = pltpu.roll(kept, 64, 1)
-                first, second = (kept, moved) if to_bit == 0 else (moved, kept)
-                for from_bit in range(2):
-                    part = slice(64 * from_bit, 64 * from_bit + 64)
-                    both = jnp.concatenate([first[part], second[part]], axis=0).astype(jnp.bfloat16)
-                    at_row, at_col = slice(128 * from_bit, 128 * from_bit + 128), slice(128 * to_bit, 128 * to_bit + 128)
-                    if layer == plan.layers - 1:
-                        far_here[kind, at_row, at_col] = both
-                    else:
-                        near[layer, kind, at_row, at_col] = both
-        if layer == plan.layers - 1:
-            copy = pltpu.make_async_copy(far_here, far, done)
-            copy.start()
+            if layer == plan.layers - 1:
+                last[kind] = turned.astype(jnp.bfloat16)
+            else:
+                widen(turned, near.at[layer, kind])
 
     block_rows = 64
     block_bits = block_rows.bit_length() - 1
@@ -175,8 +175,6 @@
             sine = jnp.round(sine * STEPS).astype(jnp.int32)
             phases[layer, at, :] = (cosine << 16) | (sine & 0xFFFF)
 
-    copy.wait()
-
 
 def offset_of(number, bits, order):
     return sum(((number >> k) & 1) << order.index(bit) for k, bit in enumerate(bits))
@@ -187,19 +185,23 @@
     return large, (values - large.astype(jnp.float32)).astype(jnp.bfloat16)
 
 
-def layers_kernel(plan, rows, state, near, far, phases, sizes, out, far_here, held, parts, done):
+def layers_kernel(plan, rows, state, near, last, phases, sizes, out, last_here, held, parts):
     layers = plan.layers
-    copy = pltpu.make_async_copy(far, far_here, done)
-    copy.start()
+    for kind in range(2):
+        widen(last[kind].astype(jnp.float32), last_here.at[kind])
 
     old_order = list(range(LANE_BITS, plan.local_bits))
     for layer in range(layers):
         order, step, target = plan.orders[layer], plan.steps[layer], plan.targets[layer]
         rest = [bit for bit in order if bit != target]
         pieces = []
-        for part in range(2):
-            for side in range(2):
-                if layer == 0 or step:
+        for part in range(3):
+            if layer == 0 or step:
+                if part == 2:
+                    pieces.append([-value for value in pieces[1]])
+                    continue
+                sides = []
+                for side in range(2):
                     tiles = []
                     for tile in range(rows // 16):
                         at = offset_of(tile, rest[3:], old_order) + (side << old_order.index(target))
@@ -207,36 +209,33 @@
                             tiles.append(state[pl.ds(2 * at + part, 8, 2 << step), :])
                         else:
                             tiles.append(held[part, pl.ds(at, 8, 1 << step), :])
-                    pieces.append(split(jnp.concatenate(tiles, axis=0)))
-                else:
-                    starts = [offset_of(tile, rest[4:], order) + (side << order.index(target))
-                              for tile in range(rows // 32)]
-                    pieces.append([
-                        jnp.concatenate([parts[layer % 2, size, part, at:at + 16, :] for at in starts], axis=0)
-                        for size in range(2)
-                    ])
-        joined = jnp.concatenate(
-            [jnp.concatenate([piece[size] for piece in pieces], axis=1) for size in range(2)], axis=0
-        )
-        if layer == layers - 1:
-            copy.wait()
-            weights = far_here
-        else:
-            weights = near.at[layer]
+                    sides.append(jnp.concatenate(tiles, axis=0))
+                pieces.append(split(jnp.concatenate(sides, axis=1)))
+            else:
+                starts = [[offset_of(tile, rest[4:], order) + (side << order.index(target))
+                           for tile in range(rows // 32)] for side in range(2)]
+                pieces.append([
+                    jnp.concatenate([
+                        jnp.concatenate([parts[layer % 2, size, part, at:at + 16, :] for at in side], axis=0)
+                        for side in starts
+                    ], axis=1)
+                    for size in range(2)
+                ])
+        weights = last_here if layer == layers - 1 else near.at[layer]
         real, imag = weights[0], weights[1]
-        weight = jnp.concatenate(
-            [jnp.concatenate([real, imag], axis=1), jnp.concatenate([-imag, real], axis=1)], axis=0
-        )
-        both = jnp.dot(joined, weight, preferred_element_type=jnp.float32)
-        result = both[:rows // 2] + both[rows // 2:]
+        results = []
+        for second, (upper, lower) in ((2, (real, imag)), (1, (imag, real))):
+            joined = jnp.concatenate([pieces[part][size] for size in range(2) for part in (0, second)], axis=1)
+            weight = jnp.concatenate([upper, lower, upper, lower], axis=0)
+            results.append(jnp.dot(joined, weight, preferred_element_type=jnp.float32))
         unit = jnp.full((16, 128), 1 / STEPS, jnp.float32)
         if layer == 0:
             unit = unit * sizes[0:1, :]
         for side in range(2):
             for tile in range(rows // 32):
                 at = offset_of(tile, rest[4:], order) + (side << order.index(target))
-                real = result[16 * tile:16 * tile + 16, 128 * side:128 * side + 128]
-                imag = result[16 * tile:16 * tile + 16, 256 + 128 * side:384 + 128 * side]
+                real = results[0][16 * tile:16 * tile + 16, 128 * side:128 * side + 128]
+                imag = results[1][16 * tile:16 * tile + 16, 128 * side:128 * side + 128]
                 word = phases[layer, at:at + 16, :]
                 cosine = (word >> 16).astype(jnp.float32) * unit
                 sine = ((word << 16) >> 16).astype(jnp.float32) * unit
@@ -249,6 +248,9 @@
                         large, small = split(value)
                         parts[(layer + 1) % 2, 0, part, at:at + 16, :] = large
                         parts[(layer + 1) % 2, 1, part, at:at + 16, :] = small
+                        if part == 1:
+                            parts[(layer + 1) % 2, 0, 2, at:at + 16, :] = -large
+                            parts[(layer + 1) % 2, 1, 2, at:at + 16, :] = -small
         old_order = order
 
 
@@ -267,19 +269,17 @@
     came = lax.all_to_all(sent, "hi", split_axis=0, concat_axis=0, tiled=True).reshape(2 * rows, 128)
 
     vmem, smem = pl.BlockSpec(memory_space=pltpu.VMEM), pl.BlockSpec(memory_space=pltpu.SMEM)
-    hbm = pl.BlockSpec(memory_space=pltpu.HBM)
     weights_shape = (2, 256, 256)
-    near, far, phases, sizes = pl.pallas_call(
+    near, last, phases, sizes = pl.pallas_call(
         functools.partial(tables_kernel, plan, rows),
         out_shape=(
             jax.ShapeDtypeStruct((layers - 1,) + weights_shape, jnp.bfloat16),
-            jax.ShapeDtypeStruct(weights_shape, jnp.bfloat16),
+            jax.ShapeDtypeStruct((2, 128, 128), jnp.bfloat16),
             jax.ShapeDtypeStruct((layers, rows, 128), jnp.int32),
             jax.ShapeDtypeStruct((8, 128), jnp.float32),
         ),
         in_specs=[vmem] + [smem] * 5,
-        out_specs=[vmem, hbm, vmem, vmem],
-        scratch_shapes=[pltpu.VMEM(weights_shape, jnp.bfloat16), pltpu.SemaphoreType.DMA],
+        out_specs=[vmem] * 4,
         cost_estimate=pl.CostEstimate(flops=100 * layers * amp_count, bytes_accessed=4 * layers * amp_count, transcendentals=0),
         compiler_params=pltpu.CompilerParams(vmem_limit_bytes=24 << 20),
         name="tables",
@@ -288,17 +288,16 @@
     result = pl.pallas_call(
         functools.partial(layers_kernel, plan, rows),
         out_shape=jax.ShapeDtypeStruct((2 * rows, 128), jnp.float32),
-        in_specs=[vmem, vmem, hbm, vmem, vmem],
+        in_specs=[vmem] * 5,
         out_specs=vmem,
         scratch_shapes=[
             pltpu.VMEM(weights_shape, jnp.bfloat16),
             pltpu.VMEM((2, rows, 128), jnp.float32),
-            pltpu.VMEM((2, 2, 2, rows, 128), jnp.bfloat16),
-            pltpu.SemaphoreType.DMA,
+            pltpu.VMEM((2, 2, 3, rows, 128), jnp.bfloat16),
         ],
         compiler_params=pltpu.CompilerParams(vmem_limit_bytes=24 << 20),
         name="layers",
-    )(came, near, far, phases, sizes)
+    )(came, near, last, phases, sizes)
 
     if plan.orders[-1] != plan.wanted:
         bits = len(plan.wanted)

time: 27 us -> 26 us (0.963)
  local copies, waits for them, and re-layouts: 6 us -> 4.36 us
  waiting for transfers between devices: 2.62 us -> 3.54 us
    unnamed x16 -> x12, local copies, waits for them, and re-layouts: 6 us -> 4.36 us
    all_to_all x1, waiting for transfers between devices: 2.62 us -> 3.54 us  [shards(): lax.all_to_all(sent, 'hi', split_axis=0, concat_axis=0, tiled=True)]
  transfers between devices with their start and end apart: 1 -> 1, of which waited for: 1 -> 1; matrix products, arithmetic and copies ran while one was open for 0% -> 0% of each run, Pallas kernels for 25% -> 26%
where the time goes in v6:
time: 26 us; the launch traced here: 25.7 us
  Pallas kernels  10.4 us (40%)
  starting transfers between devices  7.38 us (28%)
  local copies, waits for them, and re-layouts  4.36 us (17%)
  waiting for transfers between devices  3.54 us (14%)
    all_to_all x1, starting transfers between devices, shards(): lax.all_to_all(sent, 'hi', split_axis=0, concat_axis=0, tiled=True)  7.38 us
    pallas_call x1, Pallas kernels, shards(): pl.pallas_call(functools.partial(tables_kernel, plan, rows), out_shape=(j...  6.56 us
    unnamed x12, local copies, waits for them, and re-layouts  4.36 us
    pallas_call x1, Pallas kernels, shards(): pl.pallas_call(functools.partial(layers_kernel, plan, rows), out_shape=ja...  3.81 us
    all_to_all x1, waiting for transfers between devices, shards(): lax.all_to_all(sent, 'hi', split_axis=0, concat_axis=0, tiled=True)  3.54 us
  transfers between devices with their start and end apart: 1, of which 1 were waited for; matrix products, arithmetic and copies ran while one was open for 0% of the time, Pallas kernels for 26%

profile of v6, /device:TPU:0, one launch (start us, length us, event | category | flops | bytes accessed | tf_op | source)
XLA Modules:
  0.0 25.7 jit_solution(10970226196197386127)
XLA Ops:
  0.0 7.4 %all-to-all-start = ((f32[16,64,128]{2,1,0:T(8,128)}), f32[16,64,128]{2,1,0:T(8,128)S(1)}, u32[]{:S(2)}, u32[]{:S(2)}) async-start(f32[16,64,128]{2,1,0:T(8,128)} %bitcast.16), calls=%async_computation | async-start | bytes 1048576 | tf_op jit(solution)/shard_map/all_to_all | solution.py:269
  7.4 0.0 copy-start
  7.4 1.0 %copy-done = bf16[6,2,128,128]{3,2,1,0:T(8,128)(2,1)S(1)} copy-done((bf16[6,2,128,128]{3,2,1,0:T(8,128)(2,1)S(1)}, bf16[6,2,128,128]{3,2,1,0:T(8,128)(2,1)}, u32[]{:S(2)}) %copy-start) | copy-done | bytes 393240
  8.4 0.0 copy-start.1
  8.4 0.7 %copy-done.1 = s32[6,8,2]{1,2,0:T(2,128)S(1)} copy-done((s32[6,8,2]{1,2,0:T(2,128)S(1)}, s32[6,8,2]{1,2,0:T(2,128)}, u32[]{:S(2)}) %copy-start.1) | copy-done | bytes 408
  9.1 0.0 copy-start.2
  9.1 0.7 %copy-done.2 = f32[6,8]{1,0:T(8,128)S(1)} copy-done((f32[6,8]{1,0:T(8,128)S(1)}, f32[6,8]{1,0:T(8,128)}, u32[]{:S(2)}) %copy-start.2) | copy-done | bytes 216
  9.8 0.0 copy-start.3
  9.8 0.7 %copy-done.3 = s32[6,2]{0,1:T(2,128)S(1)} copy-done((s32[6,2]{0,1:T(2,128)S(1)}, s32[6,2]{0,1:T(2,128)}, u32[]{:S(2)}) %copy-start.3) | copy-done | bytes 72
  10.5 0.0 copy-start.4
  10.5 0.7 %copy-done.4 = f32[6]{0:T(128)S(1)} copy-done((f32[6]{0:T(128)S(1)}, f32[6]{0:T(128)}, u32[]{:S(2)}) %copy-start.4) | copy-done | bytes 48
  11.1 0.0 copy-start.5
  11.1 0.7 %copy-done.5 = s32[6]{0:T(128)S(1)} copy-done((s32[6]{0:T(128)S(1)}, s32[6]{0:T(128)}, u32[]{:S(2)}) %copy-start.5) | copy-done | bytes 48
  11.8 6.6 %tables.1 = (bf16[5,2,256,256]{3,2,1,0:T(8,128)(2,1)S(1)}, bf16[2,128,128]{2,1,0:T(8,128)(2,1)S(1)}, s32[6,512,128]{2,1,0:T(8,128)S(1)}, f32[8,128]{1,0:T(8,128)S(1)}) custom-call(bf16[6,2,128,128]{3,2,1,0:T(8,128)(2,1)S(1)} %copy-done, s32[6,2,8]{2,1,0:T(2,128)S(1)} %bitcast.14, f32[6,8]{1,0:T(8,128)S(1)} %copy-done.2, s32[2,6]{1,0:T(2,128)S(1)} %bitcast.15, ...), custom_call_target="tpu_custom_call" | custom-call | flops 39321600 | bytes 1572864 | tf_op jit(solution)/shard_map/tables/pallas_call | solution.py:273
  18.3 3.5 %all-to-all-done = f32[16,64,128]{2,1,0:T(8,128)S(1)} async-done(((f32[16,64,128]{2,1,0:T(8,128)}), f32[16,64,128]{2,1,0:T(8,128)S(1)}, u32[]{:S(2)}, u32[]{:S(2)}) %all-to-all-start) | async-done | bytes 524320 | tf_op jit(solution)/shard_map/all_to_all | solution.py:269
  21.9 3.8 %layers.1 = f32[1024,128]{1,0:T(8,128)} custom-call(f32[1024,128]{1,0:T(8,128)S(1)} %bitcast.13, bf16[5,2,256,256]{3,2,1,0:T(8,128)(2,1)S(1)} %get-tuple-element.9.near, bf16[2,128,128]{2,1,0:T(8,128)(2,1)S(1)} %get-tuple-element.10.last, s32[6,512,128]{2,1,0:T(8,128)S(1)} %get-tuple-element.11.phases, f32[8,128]{1,0:T(8,128)S(1)} %get-tuple-element.12.sizes), custom_call_target="tpu_custom_call" | custom-call | tf_op jit(solution)/shard_map/layers/pallas_call | solution.py:288
Async XLA Ops:
  0.0 21.9 %all-to-all-start = ((f32[16,64,128]{2,1,0:T(8,128)}), f32[16,64,128]{2,1,0:T(8,128)S(1)}, u32[]{:S(2)}, u32[]{:S(2)}) async-start(f32[16,64,128]{2,1,0:T(8,128)} %bitcast.16), calls=%async_computation | async-start | bytes 1048576 | tf_op jit(solution)/shard_map/all_to_all | solution.py:269
  7.4 1.0 %copy-start = (bf16[6,2,128,128]{3,2,1,0:T(8,128)(2,1)S(1)}, bf16[6,2,128,128]{3,2,1,0:T(8,128)(2,1)}, u32[]{:S(2)}) copy-start(bf16[6,2,128,128]{3,2,1,0:T(8,128)(2,1)} %gates.1) | copy-start | bytes 1179652
  8.4 0.7 %copy-start.1 = (s32[6,8,2]{1,2,0:T(2,128)S(1)}, s32[6,8,2]{1,2,0:T(2,128)}, u32[]{:S(2)}) copy-start(s32[6,8,2]{1,2,0:T(2,128)} %param.9) | copy-start | bytes 1156
  9.1 0.7 %copy-start.2 = (f32[6,8]{1,0:T(8,128)S(1)}, f32[6,8]{1,0:T(8,128)}, u32[]{:S(2)}) copy-start(f32[6,8]{1,0:T(8,128)} %pair_angles.1) | copy-start | bytes 580
  9.8 0.7 %copy-start.3 = (s32[6,2]{0,1:T(2,128)S(1)}, s32[6,2]{0,1:T(2,128)}, u32[]{:S(2)}) copy-start(s32[6,2]{0,1:T(2,128)} %param.11) | copy-start | bytes 148
  10.5 0.7 %copy-start.4 = (f32[6]{0:T(128)S(1)}, f32[6]{0:T(128)}, u32[]{:S(2)}) copy-start(f32[6]{0:T(128)} %cut_angle.1) | copy-start | bytes 76
  11.1 0.7 %copy-start.5 = (s32[6]{0:T(128)S(1)}, s32[6]{0:T(128)}, u32[]{:S(2)}) copy-start(s32[6]{0:T(128)} %path_index.1) | copy-start | bytes 76

commit v7 on v6

--- a/solution.py
+++ b/solution.py
@@ -88,6 +88,9 @@
             self.steps.append(step)
             self.orders.append(order)
 
+        self.halves = [bit for bit in order if bit not in self.targets
+                       and all(other.index(bit) >= 4 for other in self.orders)][:1]
+
     def lasts(self, bits, layer):
         uses = self.targets[layer:]
         count = next((k for k, bit in enumerate(uses) if bit in bits), len(uses))
@@ -190,34 +193,39 @@
     for kind in range(2):
         widen(last[kind].astype(jnp.float32), last_here.at[kind])
 
-    old_order = list(range(LANE_BITS, plan.local_bits))
-    for layer in range(layers):
-        order, step, target = plan.orders[layer], plan.steps[layer], plan.targets[layer]
-        rest = [bit for bit in order if bit != target]
+    def starts(layer, side, half, order, height):
+        fixed = [plan.targets[layer]] + plan.halves
+        rest = [bit for bit in plan.orders[layer] if bit not in fixed][height:]
+        base = side << order.index(plan.targets[layer])
+        if plan.halves:
+            base += half << order.index(plan.halves[0])
+        return [base + offset_of(number, rest, order) for number in range(1 << len(rest))]
+
+    def products(layer, half):
+        order, step = plan.orders[layer], plan.steps[layer]
         pieces = []
         for part in range(3):
             if layer == 0 or step:
                 if part == 2:
                     pieces.append([-value for value in pieces[1]])
                     continue
+                old_order = plan.orders[layer - 1] if layer else list(range(LANE_BITS, plan.local_bits))
                 sides = []
                 for side in range(2):
-                    tiles = []
-                    for tile in range(rows // 16):
-                        at = offset_of(tile, rest[3:], old_order) + (side << old_order.index(target))
-                        if layer == 0:
-                            tiles.append(state[pl.ds(2 * at + part, 8, 2 << step), :])
-                        else:
-                            tiles.append(held[part, pl.ds(at, 8, 1 << step), :])
+                    if layer == 0:
+                        tiles = [state[pl.ds(2 * at + part, 8, 2 << step), :]
+                                 for at in starts(layer, side, half, old_order, 3)]
+                    else:
+                        tiles = [held[part, pl.ds(at, 8, 1 << step), :]
+                                 for at in starts(layer, side, half, old_order, 3)]
                     sides.append(jnp.concatenate(tiles, axis=0))
                 pieces.append(split(jnp.concatenate(sides, axis=1)))
             else:
-                starts = [[offset_of(tile, rest[4:], order) + (side << order.index(target))
-                           for tile in range(rows // 32)] for side in range(2)]
                 pieces.append([
                     jnp.concatenate([
-                        jnp.concatenate([parts[layer % 2, size, part, at:at + 16, :] for at in side], axis=0)
-                        for side in starts
+                        jnp.concatenate([parts[layer % 2, size, part, at:at + 16, :]
+                                         for at in starts(layer, side, half, order, 4)], axis=0)
+                        for side in range(2)
                     ], axis=1)
                     for size in range(2)
                 ])
@@ -225,17 +233,21 @@
         real, imag = weights[0], weights[1]
         results = []
         for second, (upper, lower) in ((2, (real, imag)), (1, (imag, real))):
-            joined = jnp.concatenate([pieces[part][size] for size in range(2) for part in (0, second)], axis=1)
-            weight = jnp.concatenate([upper, lower, upper, lower], axis=0)
-            results.append(jnp.dot(joined, weight, preferred_element_type=jnp.float32))
+            joined = jnp.concatenate(
+                [jnp.concatenate([pieces[0][size], pieces[second][size]], axis=1) for size in range(2)], axis=0
+            )
+            both = jnp.dot(joined, jnp.concatenate([upper, lower], axis=0), preferred_element_type=jnp.float32)
+            results.append(both[:both.shape[0] // 2] + both[both.shape[0] // 2:])
+        return results
+
+    def turned(layer, half, results):
+        order = plan.orders[layer]
         unit = jnp.full((16, 128), 1 / STEPS, jnp.float32)
         if layer == 0:
             unit = unit * sizes[0:1, :]
         for side in range(2):
-            for tile in range(rows // 32):
-                at = offset_of(tile, rest[4:], order) + (side << order.index(target))
-                real = results[0][16 * tile:16 * tile + 16, 128 * side:128 * side + 128]
-                imag = results[1][16 * tile:16 * tile + 16, 128 * side:128 * side + 128]
+            for tile, at in enumerate(starts(layer, side, half, order, 4)):
+                real, imag = [result[16 * tile:16 * tile + 16, 128 * side:128 * side + 128] for result in results]
                 word = phases[layer, at:at + 16, :]
                 cosine = (word >> 16).astype(jnp.float32) * unit
                 sine = ((word << 16) >> 16).astype(jnp.float32) * unit
@@ -251,7 +263,20 @@
                         if part == 1:
                             parts[(layer + 1) % 2, 0, 2, at:at + 16, :] = -large
                             parts[(layer + 1) % 2, 1, 2, at:at + 16, :] = -small
-        old_order = order
+
+    waiting = None
+    for layer in range(layers):
+        for half in range(1 << len(plan.halves)):
+            results = products(layer, half)
+            if plan.halves and waiting:
+                turned(*waiting)
+                waiting = None
+            if plan.halves:
+                waiting = (layer, half, results)
+            else:
+                turned(layer, half, results)
+    if waiting:
+        turned(*waiting)
 
 
 def shards(

time: 26 us -> 25.2 us (0.969)
  Pallas kernels: 10.4 us -> 9.56 us
    pallas_call x1, Pallas kernels: 3.81 us -> 3 us  [shards(): pl.pallas_call(functools.partial(layers_kernel, plan, rows), out_shape=ja...]
where the time goes in v7:
time: 25.2 us; the launch traced here: 24.9 us
  Pallas kernels  9.56 us (38%)
  starting transfers between devices  7.38 us (29%)
  local copies, waits for them, and re-layouts  4.36 us (17%)
  waiting for transfers between devices  3.54 us (14%)
    all_to_all x1, starting transfers between devices, shards(): lax.all_to_all(sent, 'hi', split_axis=0, concat_axis=0, tiled=True)  7.38 us
    pallas_call x1, Pallas kernels, shards(): pl.pallas_call(functools.partial(tables_kernel, plan, rows), out_shape=(j...  6.56 us
    unnamed x12, local copies, waits for them, and re-layouts  4.36 us
    all_to_all x1, waiting for transfers between devices, shards(): lax.all_to_all(sent, 'hi', split_axis=0, concat_axis=0, tiled=True)  3.54 us
    pallas_call x1, Pallas kernels, shards(): pl.pallas_call(functools.partial(layers_kernel, plan, rows), out_shape=ja...  3 us
  transfers between devices with their start and end apart: 1, of which 1 were waited for; matrix products, arithmetic and copies ran while one was open for 0% of the time, Pallas kernels for 26%

profile of v7, /device:TPU:0, one launch (start us, length us, event | category | flops | bytes accessed | tf_op | source)
XLA Modules:
  0.0 24.9 jit_solution(11613785860621666407)
XLA Ops:
  0.0 7.4 %all-to-all-start = ((f32[16,64,128]{2,1,0:T(8,128)}), f32[16,64,128]{2,1,0:T(8,128)S(1)}, u32[]{:S(2)}, u32[]{:S(2)}) async-start(f32[16,64,128]{2,1,0:T(8,128)} %bitcast.16), calls=%async_computation | async-start | bytes 1048576 | tf_op jit(solution)/shard_map/all_to_all | solution.py:294
  7.4 0.0 copy-start
  7.4 1.0 %copy-done = bf16[6,2,128,128]{3,2,1,0:T(8,128)(2,1)S(1)} copy-done((bf16[6,2,128,128]{3,2,1,0:T(8,128)(2,1)S(1)}, bf16[6,2,128,128]{3,2,1,0:T(8,128)(2,1)}, u32[]{:S(2)}) %copy-start) | copy-done | bytes 393240
  8.4 0.0 copy-start.1
  8.4 0.7 %copy-done.1 = s32[6,8,2]{1,2,0:T(2,128)S(1)} copy-done((s32[6,8,2]{1,2,0:T(2,128)S(1)}, s32[6,8,2]{1,2,0:T(2,128)}, u32[]{:S(2)}) %copy-start.1) | copy-done | bytes 408
  9.1 0.0 copy-start.2
  9.1 0.7 %copy-done.2 = f32[6,8]{1,0:T(8,128)S(1)} copy-done((f32[6,8]{1,0:T(8,128)S(1)}, f32[6,8]{1,0:T(8,128)}, u32[]{:S(2)}) %copy-start.2) | copy-done | bytes 216
  9.8 0.0 copy-start.3
  9.8 0.7 %copy-done.3 = s32[6,2]{0,1:T(2,128)S(1)} copy-done((s32[6,2]{0,1:T(2,128)S(1)}, s32[6,2]{0,1:T(2,128)}, u32[]{:S(2)}) %copy-start.3) | copy-done | bytes 72
  10.5 0.0 copy-start.4
  10.5 0.7 %copy-done.4 = f32[6]{0:T(128)S(1)} copy-done((f32[6]{0:T(128)S(1)}, f32[6]{0:T(128)}, u32[]{:S(2)}) %copy-start.4) | copy-done | bytes 48
  11.1 0.0 copy-start.5
  11.1 0.7 %copy-done.5 = s32[6]{0:T(128)S(1)} copy-done((s32[6]{0:T(128)S(1)}, s32[6]{0:T(128)}, u32[]{:S(2)}) %copy-start.5) | copy-done | bytes 48
  11.8 6.6 %tables.1 = (bf16[5,2,256,256]{3,2,1,0:T(8,128)(2,1)S(1)}, bf16[2,128,128]{2,1,0:T(8,128)(2,1)S(1)}, s32[6,512,128]{2,1,0:T(8,128)S(1)}, f32[8,128]{1,0:T(8,128)S(1)}) custom-call(bf16[6,2,128,128]{3,2,1,0:T(8,128)(2,1)S(1)} %copy-done, s32[6,2,8]{2,1,0:T(2,128)S(1)} %bitcast.14, f32[6,8]{1,0:T(8,128)S(1)} %copy-done.2, s32[2,6]{1,0:T(2,128)S(1)} %bitcast.15, ...), custom_call_target="tpu_custom_call" | custom-call | flops 39321600 | bytes 1572864 | tf_op jit(solution)/shard_map/tables/pallas_call | solution.py:298
  18.3 3.5 %all-to-all-done = f32[16,64,128]{2,1,0:T(8,128)S(1)} async-done(((f32[16,64,128]{2,1,0:T(8,128)}), f32[16,64,128]{2,1,0:T(8,128)S(1)}, u32[]{:S(2)}, u32[]{:S(2)}) %all-to-all-start) | async-done | bytes 524320 | tf_op jit(solution)/shard_map/all_to_all | solution.py:294
  21.9 3.0 %layers.1 = f32[1024,128]{1,0:T(8,128)} custom-call(f32[1024,128]{1,0:T(8,128)S(1)} %bitcast.13, bf16[5,2,256,256]{3,2,1,0:T(8,128)(2,1)S(1)} %get-tuple-element.9.near, bf16[2,128,128]{2,1,0:T(8,128)(2,1)S(1)} %get-tuple-element.10.last, s32[6,512,128]{2,1,0:T(8,128)S(1)} %get-tuple-element.11.phases, f32[8,128]{1,0:T(8,128)S(1)} %get-tuple-element.12.sizes), custom_call_target="tpu_custom_call" | custom-call | tf_op jit(solution)/shard_map/layers/pallas_call | solution.py:313
Async XLA Ops:
  0.0 21.9 %all-to-all-start = ((f32[16,64,128]{2,1,0:T(8,128)}), f32[16,64,128]{2,1,0:T(8,128)S(1)}, u32[]{:S(2)}, u32[]{:S(2)}) async-start(f32[16,64,128]{2,1,0:T(8,128)} %bitcast.16), calls=%async_computation | async-start | bytes 1048576 | tf_op jit(solution)/shard_map/all_to_all | solution.py:294
  7.4 1.0 %copy-start = (bf16[6,2,128,128]{3,2,1,0:T(8,128)(2,1)S(1)}, bf16[6,2,128,128]{3,2,1,0:T(8,128)(2,1)}, u32[]{:S(2)}) copy-start(bf16[6,2,128,128]{3,2,1,0:T(8,128)(2,1)} %gates.1) | copy-start | bytes 1179652
  8.4 0.7 %copy-start.1 = (s32[6,8,2]{1,2,0:T(2,128)S(1)}, s32[6,8,2]{1,2,0:T(2,128)}, u32[]{:S(2)}) copy-start(s32[6,8,2]{1,2,0:T(2,128)} %param.9) | copy-start | bytes 1156
  9.1 0.7 %copy-start.2 = (f32[6,8]{1,0:T(8,128)S(1)}, f32[6,8]{1,0:T(8,128)}, u32[]{:S(2)}) copy-start(f32[6,8]{1,0:T(8,128)} %pair_angles.1) | copy-start | bytes 580
  9.8 0.7 %copy-start.3 = (s32[6,2]{0,1:T(2,128)S(1)}, s32[6,2]{0,1:T(2,128)}, u32[]{:S(2)}) copy-start(s32[6,2]{0,1:T(2,128)} %param.11) | copy-start | bytes 148
  10.5 0.7 %copy-start.4 = (f32[6]{0:T(128)S(1)}, f32[6]{0:T(128)}, u32[]{:S(2)}) copy-start(f32[6]{0:T(128)} %cut_angle.1) | copy-start | bytes 76
  11.1 0.7 %copy-start.5 = (s32[6]{0:T(128)S(1)}, s32[6]{0:T(128)}, u32[]{:S(2)}) copy-start(s32[6]{0:T(128)} %path_index.1) | copy-start | bytes 76

commit v8 on v7

--- a/solution.py
+++ b/solution.py
@@ -91,6 +91,16 @@
         self.halves = [bit for bit in order if bit not in self.targets
                        and all(other.index(bit) >= 4 for other in self.orders)][:1]
 
+        self.axes, shape = [], []
+        for bit in order[:3:-1]:
+            apart = bit in [self.targets[-1]] + self.halves
+            if not apart and self.axes and self.axes[-1] is None:
+                shape[-1] *= 2
+            else:
+                self.axes.append(bit if apart else None)
+                shape.append(2)
+        self.shape = tuple(shape)
+
     def lasts(self, bits, layer):
         uses = self.targets[layer:]
         count = next((k for k, bit in enumerate(uses) if bit in bits), len(uses))
@@ -188,10 +198,9 @@
     return large, (values - large.astype(jnp.float32)).astype(jnp.bfloat16)
 
 
-def layers_kernel(plan, rows, state, near, last, phases, sizes, out, last_here, held, parts):
+def layers_kernel(plan, rows, state, near, last, phases, sizes, result, last_here, held, parts, out, done):
     layers = plan.layers
-    for kind in range(2):
-        widen(last[kind].astype(jnp.float32), last_here.at[kind])
+    copies = []
 
     def starts(layer, side, half, order, height):
         fixed = [plan.targets[layer]] + plan.halves
@@ -253,7 +262,8 @@
                 sine = ((word << 16) >> 16).astype(jnp.float32) * unit
                 for part, value in enumerate((cosine * real - sine * imag, sine * real + cosine * imag)):
                     if layer == layers - 1:
-                        out[pl.ds(2 * at + part, 16, 2), :] = value
+                        block = tuple(int(k) for k in np.unravel_index(at // 16, plan.shape))
+                        out[block + (pl.ds(part, 16, 2), slice(None))] = value
                     elif plan.steps[layer + 1]:
                         held[part, at:at + 16, :] = value
                     else:
@@ -263,11 +273,21 @@
                         if part == 1:
                             parts[(layer + 1) % 2, 0, 2, at:at + 16, :] = -large
                             parts[(layer + 1) % 2, 1, 2, at:at + 16, :] = -small
+            if layer == layers - 1:
+                chosen = {plan.targets[layer]: side}
+                if plan.halves:
+                    chosen[plan.halves[0]] = half
+                here = tuple(chosen.get(bit, slice(None)) for bit in plan.axes)
+                copies.append(pltpu.make_async_copy(out.at[here], result.at[here], done.at[len(copies)]))
+                copies[-1].start()
 
     waiting = None
     for layer in range(layers):
         for half in range(1 << len(plan.halves)):
             results = products(layer, half)
+            if (layer, half) == (0, 0):
+                for kind in range(2):
+                    widen(last[kind].astype(jnp.float32), last_here.at[kind])
             if plan.halves and waiting:
                 turned(*waiting)
                 waiting = None
@@ -277,6 +297,8 @@
                 turned(layer, half, results)
     if waiting:
         turned(*waiting)
+    for copy in copies:
+        copy.wait()
 
 
 def shards(
@@ -312,17 +334,19 @@
 
     result = pl.pallas_call(
         functools.partial(layers_kernel, plan, rows),
-        out_shape=jax.ShapeDtypeStruct((2 * rows, 128), jnp.float32),
+        out_shape=jax.ShapeDtypeStruct(plan.shape + (32, 128), jnp.float32),
         in_specs=[vmem] * 5,
-        out_specs=vmem,
+        out_specs=pl.BlockSpec(memory_space=pltpu.HBM),
         scratch_shapes=[
             pltpu.VMEM(weights_shape, jnp.bfloat16),
             pltpu.VMEM((2, rows, 128), jnp.float32),
             pltpu.VMEM((2, 2, 3, rows, 128), jnp.bfloat16),
+            pltpu.VMEM(plan.shape + (32, 128), jnp.float32),
+            pltpu.SemaphoreType.DMA((2 << len(plan.halves),)),
         ],
         compiler_params=pltpu.CompilerParams(vmem_limit_bytes=24 << 20),
         name="layers",
-    )(came, near, last, phases, sizes)
+    )(came, near, last, phases, sizes).reshape(2 * rows, 128)
 
     if plan.orders[-1] != plan.wanted:
         bits = len(plan.wanted)

time: 25.2 us -> 25.2 us (level)
  no operation moved by 1% of the time
where the time goes in v8:
time: 25.2 us; the launch traced here: 24.8 us
  Pallas kernels  9.5 us (38%)
  starting transfers between devices  7.38 us (29%)
  local copies, waits for them, and re-layouts  4.36 us (17%)
  waiting for transfers between devices  3.54 us (14%)
    all_to_all x1, starting transfers between devices, shards(): lax.all_to_all(sent, 'hi', split_axis=0, concat_axis=0, tiled=True)  7.38 us
    pallas_call x1, Pallas kernels, shards(): pl.pallas_call(functools.partial(tables_kernel, plan, rows), out_shape=(j...  6.56 us
    unnamed x12, local copies, waits for them, and re-layouts  4.36 us
    all_to_all x1, waiting for transfers between devices, shards(): lax.all_to_all(sent, 'hi', split_axis=0, concat_axis=0, tiled=True)  3.54 us
    pallas_call x1, Pallas kernels, shards(): pl.pallas_call(functools.partial(layers_kernel, plan, rows), out_shape=ja...  2.94 us
  transfers between devices with their start and end apart: 1, of which 1 were waited for; matrix products, arithmetic and copies ran while one was open for 0% of the time, Pallas kernels for 26%

profile of v8, /device:TPU:0, one launch (start us, length us, event | category | flops | bytes accessed | tf_op | source)
XLA Modules:
  0.0 24.8 jit_solution(12286449873736478346)
XLA Ops:
  0.0 7.4 %all-to-all-start = ((f32[16,64,128]{2,1,0:T(8,128)}), f32[16,64,128]{2,1,0:T(8,128)S(1)}, u32[]{:S(2)}, u32[]{:S(2)}) async-start(f32[16,64,128]{2,1,0:T(8,128)} %bitcast.16), calls=%async_computation | async-start | bytes 1048576 | tf_op jit(solution)/shard_map/all_to_all | solution.py:316
  7.4 0.0 copy-start
  7.4 1.0 %copy-done = bf16[6,2,128,128]{3,2,1,0:T(8,128)(2,1)S(1)} copy-done((bf16[6,2,128,128]{3,2,1,0:T(8,128)(2,1)S(1)}, bf16[6,2,128,128]{3,2,1,0:T(8,128)(2,1)}, u32[]{:S(2)}) %copy-start) | copy-done | bytes 393240
  8.4 0.0 copy-start.1
  8.4 0.7 %copy-done.1 = s32[6,8,2]{1,2,0:T(2,128)S(1)} copy-done((s32[6,8,2]{1,2,0:T(2,128)S(1)}, s32[6,8,2]{1,2,0:T(2,128)}, u32[]{:S(2)}) %copy-start.1) | copy-done | bytes 408
  9.1 0.0 copy-start.2
  9.1 0.7 %copy-done.2 = f32[6,8]{1,0:T(8,128)S(1)} copy-done((f32[6,8]{1,0:T(8,128)S(1)}, f32[6,8]{1,0:T(8,128)}, u32[]{:S(2)}) %copy-start.2) | copy-done | bytes 216
  9.8 0.0 copy-start.3
  9.8 0.7 %copy-done.3 = s32[6,2]{0,1:T(2,128)S(1)} copy-done((s32[6,2]{0,1:T(2,128)S(1)}, s32[6,2]{0,1:T(2,128)}, u32[]{:S(2)}) %copy-start.3) | copy-done | bytes 72
  10.5 0.0 copy-start.4
  10.5 0.7 %copy-done.4 = f32[6]{0:T(128)S(1)} copy-done((f32[6]{0:T(128)S(1)}, f32[6]{0:T(128)}, u32[]{:S(2)}) %copy-start.4) | copy-done | bytes 48
  11.1 0.0 copy-start.5
  11.1 0.7 %copy-done.5 = s32[6]{0:T(128)S(1)} copy-done((s32[6]{0:T(128)S(1)}, s32[6]{0:T(128)}, u32[]{:S(2)}) %copy-start.5) | copy-done | bytes 48
  11.8 6.6 %tables.1 = (bf16[5,2,256,256]{3,2,1,0:T(8,128)(2,1)S(1)}, bf16[2,128,128]{2,1,0:T(8,128)(2,1)S(1)}, s32[6,512,128]{2,1,0:T(8,128)S(1)}, f32[8,128]{1,0:T(8,128)S(1)}) custom-call(bf16[6,2,128,128]{3,2,1,0:T(8,128)(2,1)S(1)} %copy-done, s32[6,2,8]{2,1,0:T(2,128)S(1)} %bitcast.14, f32[6,8]{1,0:T(8,128)S(1)} %copy-done.2, s32[2,6]{1,0:T(2,128)S(1)} %bitcast.15, ...), custom_call_target="tpu_custom_call" | custom-call | flops 39321600 | bytes 1572864 | tf_op jit(solution)/shard_map/tables/pallas_call | solution.py:320
  18.3 3.5 %all-to-all-done = f32[16,64,128]{2,1,0:T(8,128)S(1)} async-done(((f32[16,64,128]{2,1,0:T(8,128)}), f32[16,64,128]{2,1,0:T(8,128)S(1)}, u32[]{:S(2)}, u32[]{:S(2)}) %all-to-all-start) | async-done | bytes 524320 | tf_op jit(solution)/shard_map/all_to_all | solution.py:316
  21.9 2.9 %layers.1 = f32[4,2,2,2,32,128]{5,4,3,2,1,0:T(8,128)} custom-call(f32[1024,128]{1,0:T(8,128)S(1)} %bitcast.13, bf16[5,2,256,256]{3,2,1,0:T(8,128)(2,1)S(1)} %get-tuple-element.9.near, bf16[2,128,128]{2,1,0:T(8,128)(2,1)S(1)} %get-tuple-element.10.last, s32[6,512,128]{2,1,0:T(8,128)S(1)} %get-tuple-element.11.phases, f32[8,128]{1,0:T(8,128)S(1)} %get-tuple-element.12.sizes), custom_call_target="tpu_custom_call" | custom-call | tf_op jit(solution)/shard_map/layers/pallas_call | solution.py:335
Async XLA Ops:
  0.0 21.9 %all-to-all-start = ((f32[16,64,128]{2,1,0:T(8,128)}), f32[16,64,128]{2,1,0:T(8,128)S(1)}, u32[]{:S(2)}, u32[]{:S(2)}) async-start(f32[16,64,128]{2,1,0:T(8,128)} %bitcast.16), calls=%async_computation | async-start | bytes 1048576 | tf_op jit(solution)/shard_map/all_to_all | solution.py:316
  7.4 1.0 %copy-start = (bf16[6,2,128,128]{3,2,1,0:T(8,128)(2,1)S(1)}, bf16[6,2,128,128]{3,2,1,0:T(8,128)(2,1)}, u32[]{:S(2)}) copy-start(bf16[6,2,128,128]{3,2,1,0:T(8,128)(2,1)} %gates.1) | copy-start | bytes 1179652
  8.4 0.7 %copy-start.1 = (s32[6,8,2]{1,2,0:T(2,128)S(1)}, s32[6,8,2]{1,2,0:T(2,128)}, u32[]{:S(2)}) copy-start(s32[6,8,2]{1,2,0:T(2,128)} %param.9) | copy-start | bytes 1156
  9.1 0.7 %copy-start.2 = (f32[6,8]{1,0:T(8,128)S(1)}, f32[6,8]{1,0:T(8,128)}, u32[]{:S(2)}) copy-start(f32[6,8]{1,0:T(8,128)} %pair_angles.1) | copy-start | bytes 580
  9.8 0.7 %copy-start.3 = (s32[6,2]{0,1:T(2,128)S(1)}, s32[6,2]{0,1:T(2,128)}, u32[]{:S(2)}) copy-start(s32[6,2]{0,1:T(2,128)} %param.11) | copy-start | bytes 148
  10.5 0.7 %copy-start.4 = (f32[6]{0:T(128)S(1)}, f32[6]{0:T(128)}, u32[]{:S(2)}) copy-start(f32[6]{0:T(128)} %cut_angle.1) | copy-start | bytes 76
  11.1 0.7 %copy-start.5 = (s32[6]{0:T(128)S(1)}, s32[6]{0:T(128)}, u32[]{:S(2)}) copy-start(s32[6]{0:T(128)} %path_index.1) | copy-start | bytes 76

commit v9 on v8

--- a/solution.py
+++ b/solution.py
@@ -213,11 +213,8 @@
     def products(layer, half):
         order, step = plan.orders[layer], plan.steps[layer]
         pieces = []
-        for part in range(3):
+        for part in range(2):
             if layer == 0 or step:
-                if part == 2:
-                    pieces.append([-value for value in pieces[1]])
-                    continue
                 old_order = plan.orders[layer - 1] if layer else list(range(LANE_BITS, plan.local_bits))
                 sides = []
                 for side in range(2):
@@ -239,15 +236,14 @@
                     for size in range(2)
                 ])
         weights = last_here if layer == layers - 1 else near.at[layer]
-        real, imag = weights[0], weights[1]
-        results = []
-        for second, (upper, lower) in ((2, (real, imag)), (1, (imag, real))):
-            joined = jnp.concatenate(
-                [jnp.concatenate([pieces[0][size], pieces[second][size]], axis=1) for size in range(2)], axis=0
-            )
-            both = jnp.dot(joined, jnp.concatenate([upper, lower], axis=0), preferred_element_type=jnp.float32)
-            results.append(both[:both.shape[0] // 2] + both[both.shape[0] // 2:])
-        return results
+        joined = jnp.concatenate([pieces[part][size] for part in range(2) for size in range(2)], axis=0)
+        count = joined.shape[0] // 4
+        sums = []
+        for kind in range(2):
+            each = jnp.dot(joined, weights[kind], preferred_element_type=jnp.float32)
+            sums.append([each[2 * part * count:(2 * part + 1) * count] + each[(2 * part + 1) * count:(2 * part + 2) * count]
+                         for part in range(2)])
+        return [sums[0][0] - sums[1][1], sums[1][0] + sums[0][1]]
 
     def turned(layer, half, results):
         order = plan.orders[layer]
@@ -270,9 +266,6 @@
                         large, small = split(value)
                         parts[(layer + 1) % 2, 0, part, at:at + 16, :] = large
                         parts[(layer + 1) % 2, 1, part, at:at + 16, :] = small
-                        if part == 1:
-                            parts[(layer + 1) % 2, 0, 2, at:at + 16, :] = -large
-                            parts[(layer + 1) % 2, 1, 2, at:at + 16, :] = -small
             if layer == layers - 1:
                 chosen = {plan.targets[layer]: side}
                 if plan.halves:
@@ -340,7 +333,7 @@
         scratch_shapes=[
             pltpu.VMEM(weights_shape, jnp.bfloat16),
             pltpu.VMEM((2, rows, 128), jnp.float32),
-            pltpu.VMEM((2, 2, 3, rows, 128), jnp.bfloat16),
+            pltpu.VMEM((2, 2, 2, rows, 128), jnp.bfloat16),
             pltpu.VMEM(plan.shape + (32, 128), jnp.float32),
             pltpu.SemaphoreType.DMA((2 << len(plan.halves),)),
         ],

time: 25.2 us -> 26.2 us (1.040)
  Pallas kernels: 9.5 us -> 10.5 us
    pallas_call x1, Pallas kernels: 2.94 us -> 3.95 us  [shards(): pl.pallas_call(functools.partial(layers_kernel, plan, rows), out_shape=ja...]
  transfers between devices with their start and end apart: 1 -> 1, of which waited for: 1 -> 1; matrix products, arithmetic and copies ran while one was open for 0% -> 0% of each run, Pallas kernels for 26% -> 25%
where the time goes in v9:
time: 26.2 us; the launch traced here: 25.8 us
  Pallas kernels  10.5 us (40%)
  starting transfers between devices  7.38 us (28%)
  local copies, waits for them, and re-layouts  4.36 us (17%)
  waiting for transfers between devices  3.54 us (14%)
    all_to_all x1, starting transfers between devices, shards(): lax.all_to_all(sent, 'hi', split_axis=0, concat_axis=0, tiled=True)  7.38 us
    pallas_call x1, Pallas kernels, shards(): pl.pallas_call(functools.partial(tables_kernel, plan, rows), out_shape=(j...  6.56 us
    unnamed x12, local copies, waits for them, and re-layouts  4.36 us
    pallas_call x1, Pallas kernels, shards(): pl.pallas_call(functools.partial(layers_kernel, plan, rows), out_shape=ja...  3.95 us
    all_to_all x1, waiting for transfers between devices, shards(): lax.all_to_all(sent, 'hi', split_axis=0, concat_axis=0, tiled=True)  3.54 us
  transfers between devices with their start and end apart: 1, of which 1 were waited for; matrix products, arithmetic and copies ran while one was open for 0% of the time, Pallas kernels for 25%

profile of v9, /device:TPU:0, one launch (start us, length us, event | category | flops | bytes accessed | tf_op | source)
XLA Modules:
  0.0 25.8 jit_solution(373041200188257745)
XLA Ops:
  0.0 7.4 %all-to-all-start = ((f32[16,64,128]{2,1,0:T(8,128)}), f32[16,64,128]{2,1,0:T(8,128)S(1)}, u32[]{:S(2)}, u32[]{:S(2)}) async-start(f32[16,64,128]{2,1,0:T(8,128)} %bitcast.16), calls=%async_computation | async-start | bytes 1048576 | tf_op jit(solution)/shard_map/all_to_all | solution.py:309
  7.4 0.0 copy-start
  7.4 1.0 %copy-done = bf16[6,2,128,128]{3,2,1,0:T(8,128)(2,1)S(1)} copy-done((bf16[6,2,128,128]{3,2,1,0:T(8,128)(2,1)S(1)}, bf16[6,2,128,128]{3,2,1,0:T(8,128)(2,1)}, u32[]{:S(2)}) %copy-start) | copy-done | bytes 393240
  8.4 0.0 copy-start.1
  8.4 0.7 %copy-done.1 = s32[6,8,2]{1,2,0:T(2,128)S(1)} copy-done((s32[6,8,2]{1,2,0:T(2,128)S(1)}, s32[6,8,2]{1,2,0:T(2,128)}, u32[]{:S(2)}) %copy-start.1) | copy-done | bytes 408
  9.1 0.0 copy-start.2
  9.1 0.7 %copy-done.2 = f32[6,8]{1,0:T(8,128)S(1)} copy-done((f32[6,8]{1,0:T(8,128)S(1)}, f32[6,8]{1,0:T(8,128)}, u32[]{:S(2)}) %copy-start.2) | copy-done | bytes 216
  9.8 0.0 copy-start.3
  9.8 0.7 %copy-done.3 = s32[6,2]{0,1:T(2,128)S(1)} copy-done((s32[6,2]{0,1:T(2,128)S(1)}, s32[6,2]{0,1:T(2,128)}, u32[]{:S(2)}) %copy-start.3) | copy-done | bytes 72
  10.5 0.0 copy-start.4
  10.5 0.7 %copy-done.4 = f32[6]{0:T(128)S(1)} copy-done((f32[6]{0:T(128)S(1)}, f32[6]{0:T(128)}, u32[]{:S(2)}) %copy-start.4) | copy-done | bytes 48
  11.1 0.0 copy-start.5
  11.1 0.7 %copy-done.5 = s32[6]{0:T(128)S(1)} copy-done((s32[6]{0:T(128)S(1)}, s32[6]{0:T(128)}, u32[]{:S(2)}) %copy-start.5) | copy-done | bytes 48
  11.8 6.6 %tables.1 = (bf16[5,2,256,256]{3,2,1,0:T(8,128)(2,1)S(1)}, bf16[2,128,128]{2,1,0:T(8,128)(2,1)S(1)}, s32[6,512,128]{2,1,0:T(8,128)S(1)}, f32[8,128]{1,0:T(8,128)S(1)}) custom-call(bf16[6,2,128,128]{3,2,1,0:T(8,128)(2,1)S(1)} %copy-done, s32[6,2,8]{2,1,0:T(2,128)S(1)} %bitcast.14, f32[6,8]{1,0:T(8,128)S(1)} %copy-done.2, s32[2,6]{1,0:T(2,128)S(1)} %bitcast.15, ...), custom_call_target="tpu_custom_call" | custom-call | flops 39321600 | bytes 1572864 | tf_op jit(solution)/shard_map/tables/pallas_call | solution.py:313
  18.3 3.5 %all-to-all-done = f32[16,64,128]{2,1,0:T(8,128)S(1)} async-done(((f32[16,64,128]{2,1,0:T(8,128)}), f32[16,64,128]{2,1,0:T(8,128)S(1)}, u32[]{:S(2)}, u32[]{:S(2)}) %all-to-all-start) | async-done | bytes 524320 | tf_op jit(solution)/shard_map/all_to_all | solution.py:309
  21.9 4.0 %layers.1 = f32[4,2,2,2,32,128]{5,4,3,2,1,0:T(8,128)} custom-call(f32[1024,128]{1,0:T(8,128)S(1)} %bitcast.13, bf16[5,2,256,256]{3,2,1,0:T(8,128)(2,1)S(1)} %get-tuple-element.9.near, bf16[2,128,128]{2,1,0:T(8,128)(2,1)S(1)} %get-tuple-element.10.last, s32[6,512,128]{2,1,0:T(8,128)S(1)} %get-tuple-element.11.phases, f32[8,128]{1,0:T(8,128)S(1)} %get-tuple-element.12.sizes), custom_call_target="tpu_custom_call" | custom-call | tf_op jit(solution)/shard_map/layers/pallas_call | solution.py:328
Async XLA Ops:
  0.0 21.9 %all-to-all-start = ((f32[16,64,128]{2,1,0:T(8,128)}), f32[16,64,128]{2,1,0:T(8,128)S(1)}, u32[]{:S(2)}, u32[]{:S(2)}) async-start(f32[16,64,128]{2,1,0:T(8,128)} %bitcast.16), calls=%async_computation | async-start | bytes 1048576 | tf_op jit(solution)/shard_map/all_to_all | solution.py:309
  7.4 1.0 %copy-start = (bf16[6,2,128,128]{3,2,1,0:T(8,128)(2,1)S(1)}, bf16[6,2,128,128]{3,2,1,0:T(8,128)(2,1)}, u32[]{:S(2)}) copy-start(bf16[6,2,128,128]{3,2,1,0:T(8,128)(2,1)} %gates.1) | copy-start | bytes 1179652
  8.4 0.7 %copy-start.1 = (s32[6,8,2]{1,2,0:T(2,128)S(1)}, s32[6,8,2]{1,2,0:T(2,128)}, u32[]{:S(2)}) copy-start(s32[6,8,2]{1,2,0:T(2,128)} %param.9) | copy-start | bytes 1156
  9.1 0.7 %copy-start.2 = (f32[6,8]{1,0:T(8,128)S(1)}, f32[6,8]{1,0:T(8,128)}, u32[]{:S(2)}) copy-start(f32[6,8]{1,0:T(8,128)} %pair_angles.1) | copy-start | bytes 580
  9.8 0.7 %copy-start.3 = (s32[6,2]{0,1:T(2,128)S(1)}, s32[6,2]{0,1:T(2,128)}, u32[]{:S(2)}) copy-start(s32[6,2]{0,1:T(2,128)} %param.11) | copy-start | bytes 148
  10.5 0.7 %copy-start.4 = (f32[6]{0:T(128)S(1)}, f32[6]{0:T(128)}, u32[]{:S(2)}) copy-start(f32[6]{0:T(128)} %cut_angle.1) | copy-start | bytes 76
  11.1 0.7 %copy-start.5 = (s32[6]{0:T(128)S(1)}, s32[6]{0:T(128)}, u32[]{:S(2)}) copy-start(s32[6]{0:T(128)} %path_index.1) | copy-start | bytes 76

commit v10 on v8

--- a/solution.py
+++ b/solution.py
@@ -242,11 +242,9 @@
         real, imag = weights[0], weights[1]
         results = []
         for second, (upper, lower) in ((2, (real, imag)), (1, (imag, real))):
-            joined = jnp.concatenate(
-                [jnp.concatenate([pieces[0][size], pieces[second][size]], axis=1) for size in range(2)], axis=0
-            )
-            both = jnp.dot(joined, jnp.concatenate([upper, lower], axis=0), preferred_element_type=jnp.float32)
-            results.append(both[:both.shape[0] // 2] + both[both.shape[0] // 2:])
+            joined = jnp.concatenate([pieces[part][size] for size in range(2) for part in (0, second)], axis=1)
+            weight = jnp.concatenate([upper, lower, upper, lower], axis=0)
+            results.append(jnp.dot(joined, weight, preferred_element_type=jnp.float32))
         return results
 
     def turned(layer, half, results):

time: 25.2 us -> 25.3 us (level)
  no operation moved by 1% of the time
where the time goes in v10:
time: 25.3 us; the launch traced here: 24.9 us
  Pallas kernels  9.6 us (38%)
  starting transfers between devices  7.38 us (29%)
  local copies, waits for them, and re-layouts  4.36 us (17%)
  waiting for transfers between devices  3.54 us (14%)
    all_to_all x1, starting transfers between devices, shards(): lax.all_to_all(sent, 'hi', split_axis=0, concat_axis=0, tiled=True)  7.38 us
    pallas_call x1, Pallas kernels, shards(): pl.pallas_call(functools.partial(tables_kernel, plan, rows), out_shape=(j...  6.56 us
    unnamed x12, local copies, waits for them, and re-layouts  4.36 us
    all_to_all x1, waiting for transfers between devices, shards(): lax.all_to_all(sent, 'hi', split_axis=0, concat_axis=0, tiled=True)  3.54 us
    pallas_call x1, Pallas kernels, shards(): pl.pallas_call(functools.partial(layers_kernel, plan, rows), out_shape=ja...  3.04 us
  transfers between devices with their start and end apart: 1, of which 1 were waited for; matrix products, arithmetic and copies ran while one was open for 0% of the time, Pallas kernels for 26%

profile of v10, /device:TPU:0, one launch (start us, length us, event | category | flops | bytes accessed | tf_op | source)
XLA Modules:
  0.0 24.9 jit_solution(6075929369695013336)
XLA Ops:
  0.0 7.4 %all-to-all-start = ((f32[16,64,128]{2,1,0:T(8,128)}), f32[16,64,128]{2,1,0:T(8,128)S(1)}, u32[]{:S(2)}, u32[]{:S(2)}) async-start(f32[16,64,128]{2,1,0:T(8,128)} %bitcast.16), calls=%async_computation | async-start | bytes 1048576 | tf_op jit(solution)/shard_map/all_to_all | solution.py:314
  7.4 0.0 copy-start
  7.4 1.0 %copy-done = bf16[6,2,128,128]{3,2,1,0:T(8,128)(2,1)S(1)} copy-done((bf16[6,2,128,128]{3,2,1,0:T(8,128)(2,1)S(1)}, bf16[6,2,128,128]{3,2,1,0:T(8,128)(2,1)}, u32[]{:S(2)}) %copy-start) | copy-done | bytes 393240
  8.4 0.0 copy-start.1
  8.4 0.7 %copy-done.1 = s32[6,8,2]{1,2,0:T(2,128)S(1)} copy-done((s32[6,8,2]{1,2,0:T(2,128)S(1)}, s32[6,8,2]{1,2,0:T(2,128)}, u32[]{:S(2)}) %copy-start.1) | copy-done | bytes 408
  9.1 0.0 copy-start.2
  9.1 0.7 %copy-done.2 = f32[6,8]{1,0:T(8,128)S(1)} copy-done((f32[6,8]{1,0:T(8,128)S(1)}, f32[6,8]{1,0:T(8,128)}, u32[]{:S(2)}) %copy-start.2) | copy-done | bytes 216
  9.8 0.0 copy-start.3
  9.8 0.7 %copy-done.3 = s32[6,2]{0,1:T(2,128)S(1)} copy-done((s32[6,2]{0,1:T(2,128)S(1)}, s32[6,2]{0,1:T(2,128)}, u32[]{:S(2)}) %copy-start.3) | copy-done | bytes 72
  10.5 0.0 copy-start.4
  10.5 0.7 %copy-done.4 = f32[6]{0:T(128)S(1)} copy-done((f32[6]{0:T(128)S(1)}, f32[6]{0:T(128)}, u32[]{:S(2)}) %copy-start.4) | copy-done | bytes 48
  11.1 0.0 copy-start.5
  11.1 0.7 %copy-done.5 = s32[6]{0:T(128)S(1)} copy-done((s32[6]{0:T(128)S(1)}, s32[6]{0:T(128)}, u32[]{:S(2)}) %copy-start.5) | copy-done | bytes 48
  11.8 6.6 %tables.1 = (bf16[5,2,256,256]{3,2,1,0:T(8,128)(2,1)S(1)}, bf16[2,128,128]{2,1,0:T(8,128)(2,1)S(1)}, s32[6,512,128]{2,1,0:T(8,128)S(1)}, f32[8,128]{1,0:T(8,128)S(1)}) custom-call(bf16[6,2,128,128]{3,2,1,0:T(8,128)(2,1)S(1)} %copy-done, s32[6,2,8]{2,1,0:T(2,128)S(1)} %bitcast.14, f32[6,8]{1,0:T(8,128)S(1)} %copy-done.2, s32[2,6]{1,0:T(2,128)S(1)} %bitcast.15, ...), custom_call_target="tpu_custom_call" | custom-call | flops 39321600 | bytes 1572864 | tf_op jit(solution)/shard_map/tables/pallas_call | solution.py:318
  18.3 3.5 %all-to-all-done = f32[16,64,128]{2,1,0:T(8,128)S(1)} async-done(((f32[16,64,128]{2,1,0:T(8,128)}), f32[16,64,128]{2,1,0:T(8,128)S(1)}, u32[]{:S(2)}, u32[]{:S(2)}) %all-to-all-start) | async-done | bytes 524320 | tf_op jit(solution)/shard_map/all_to_all | solution.py:314
  21.9 3.0 %layers.1 = f32[4,2,2,2,32,128]{5,4,3,2,1,0:T(8,128)} custom-call(f32[1024,128]{1,0:T(8,128)S(1)} %bitcast.13, bf16[5,2,256,256]{3,2,1,0:T(8,128)(2,1)S(1)} %get-tuple-element.9.near, bf16[2,128,128]{2,1,0:T(8,128)(2,1)S(1)} %get-tuple-element.10.last, s32[6,512,128]{2,1,0:T(8,128)S(1)} %get-tuple-element.11.phases, f32[8,128]{1,0:T(8,128)S(1)} %get-tuple-element.12.sizes), custom_call_target="tpu_custom_call" | custom-call | tf_op jit(solution)/shard_map/layers/pallas_call | solution.py:333
Async XLA Ops:
  0.0 21.9 %all-to-all-start = ((f32[16,64,128]{2,1,0:T(8,128)}), f32[16,64,128]{2,1,0:T(8,128)S(1)}, u32[]{:S(2)}, u32[]{:S(2)}) async-start(f32[16,64,128]{2,1,0:T(8,128)} %bitcast.16), calls=%async_computation | async-start | bytes 1048576 | tf_op jit(solution)/shard_map/all_to_all | solution.py:314
  7.4 1.0 %copy-start = (bf16[6,2,128,128]{3,2,1,0:T(8,128)(2,1)S(1)}, bf16[6,2,128,128]{3,2,1,0:T(8,128)(2,1)}, u32[]{:S(2)}) copy-start(bf16[6,2,128,128]{3,2,1,0:T(8,128)(2,1)} %gates.1) | copy-start | bytes 1179652
  8.4 0.7 %copy-start.1 = (s32[6,8,2]{1,2,0:T(2,128)S(1)}, s32[6,8,2]{1,2,0:T(2,128)}, u32[]{:S(2)}) copy-start(s32[6,8,2]{1,2,0:T(2,128)} %param.9) | copy-start | bytes 1156
  9.1 0.7 %copy-start.2 = (f32[6,8]{1,0:T(8,128)S(1)}, f32[6,8]{1,0:T(8,128)}, u32[]{:S(2)}) copy-start(f32[6,8]{1,0:T(8,128)} %pair_angles.1) | copy-start | bytes 580
  9.8 0.7 %copy-start.3 = (s32[6,2]{0,1:T(2,128)S(1)}, s32[6,2]{0,1:T(2,128)}, u32[]{:S(2)}) copy-start(s32[6,2]{0,1:T(2,128)} %param.11) | copy-start | bytes 148
  10.5 0.7 %copy-start.4 = (f32[6]{0:T(128)S(1)}, f32[6]{0:T(128)}, u32[]{:S(2)}) copy-start(f32[6]{0:T(128)} %cut_angle.1) | copy-start | bytes 76
  11.1 0.7 %copy-start.5 = (s32[6]{0:T(128)S(1)}, s32[6]{0:T(128)}, u32[]{:S(2)}) copy-start(s32[6]{0:T(128)} %path_index.1) | copy-start | bytes 76

commit v11 on v8

--- a/solution.py
+++ b/solution.py
@@ -198,9 +198,15 @@
     return large, (values - large.astype(jnp.float32)).astype(jnp.bfloat16)
 
 
-def layers_kernel(plan, rows, state, near, last, phases, sizes, result, last_here, held, parts, out, done):
+def layers_kernel(plan, rows, came, taken, near, last, phases, sizes, result, last_here, held, parts, out, state, done):
     layers = plan.layers
     copies = []
+    near_bit = lax.axis_index("hi") & 1
+    size = taken.shape[1]
+    for chip in range(taken.shape[0]):
+        mine = pl.ds(pl.multiple_of(near_bit * size, size), size)
+        state[pl.ds(pl.multiple_of((2 * chip + near_bit) * size, size), size), :] = came[chip, mine, :]
+        state[pl.ds(pl.multiple_of((2 * chip + 1 - near_bit) * size, size), size), :] = taken[chip]
 
     def starts(layer, side, half, order, height):
         fixed = [plan.targets[layer]] + plan.halves
@@ -313,7 +319,13 @@
 
     shaped = with_layout_constraint(amplitudes.reshape(2, rows, 128), Layout(major_to_minor=(1, 0, 2)))
     sent = shaped.transpose(1, 0, 2).reshape(devices, -1, 128)
-    came = lax.all_to_all(sent, "hi", split_axis=0, concat_axis=0, tiled=True).reshape(2 * rows, 128)
+    near_bit = lax.axis_index("hi") & 1
+    groups = [list(range(first, devices, 2)) for first in range(2)]
+    came = lax.all_to_all(
+        sent.reshape(devices // 2, -1, 128), "hi", split_axis=0, concat_axis=0, axis_index_groups=groups, tiled=True,
+    )
+    given = lax.dynamic_index_in_dim(came.reshape(devices // 2, 2, -1, 128), 1 - near_bit, 1, keepdims=False)
+    taken = lax.ppermute(given, "hi", [(i, i ^ 1) for i in range(devices)])
 
     vmem, smem = pl.BlockSpec(memory_space=pltpu.VMEM), pl.BlockSpec(memory_space=pltpu.SMEM)
     weights_shape = (2, 256, 256)
@@ -335,18 +347,19 @@
     result = pl.pallas_call(
         functools.partial(layers_kernel, plan, rows),
         out_shape=jax.ShapeDtypeStruct(plan.shape + (32, 128), jnp.float32),
-        in_specs=[vmem] * 5,
+        in_specs=[vmem] * 6,
         out_specs=pl.BlockSpec(memory_space=pltpu.HBM),
         scratch_shapes=[
             pltpu.VMEM(weights_shape, jnp.bfloat16),
             pltpu.VMEM((2, rows, 128), jnp.float32),
             pltpu.VMEM((2, 2, 3, rows, 128), jnp.bfloat16),
             pltpu.VMEM(plan.shape + (32, 128), jnp.float32),
+            pltpu.VMEM((2 * rows, 128), jnp.float32),
             pltpu.SemaphoreType.DMA((2 << len(plan.halves),)),
         ],
         compiler_params=pltpu.CompilerParams(vmem_limit_bytes=24 << 20),
         name="layers",
-    )(came, near, last, phases, sizes).reshape(2 * rows, 128)
+    )(came, taken, near, last, phases, sizes).reshape(2 * rows, 128)
 
     if plan.orders[-1] != plan.wanted:
         bits = len(plan.wanted)

time: 25.2 us -> 32 us (1.27)
  waiting for transfers between devices: 3.54 us -> 14.5 us
  local copies, waits for them, and re-layouts: 4.36 us -> 0.04 us
    all_to_all x1, waiting for transfers between devices: 3.54 us -> 14.5 us  [shards(): lax.all_to_all(sent.reshape(devices // 2, -1, 128), 'hi', split_axis=0, c...]
    unnamed x12, local copies, waits for them, and re-layouts: 4.36 us -> 0.02 us
  transfers between devices with their start and end apart: 1 -> 2, of which waited for: 1 -> 1; matrix products, arithmetic and copies ran while one was open for 0% -> 0% of each run, Pallas kernels for 26% -> 21%
where the time goes in v11:
time: 32 us; the launch traced here: 31.7 us
  waiting for transfers between devices  14.5 us (45%)
  Pallas kernels  9.62 us (30%)
  starting transfers between devices  7.51 us (23%)
    all_to_all x1, waiting for transfers between devices, shards(): lax.all_to_all(sent.reshape(devices // 2, -1, 128), 'hi', split_axis=0, c...  14.5 us
    all_to_all x1, starting transfers between devices, shards(): lax.all_to_all(sent.reshape(devices // 2, -1, 128), 'hi', split_axis=0, c...  7.44 us
    pallas_call x1, Pallas kernels, shards(): pl.pallas_call(functools.partial(tables_kernel, plan, rows), out_shape=(j...  6.56 us
    pallas_call x1, Pallas kernels, shards(): pl.pallas_call(functools.partial(layers_kernel, plan, rows), out_shape=ja...  3.05 us
  transfers between devices with their start and end apart: 2, of which 1 were waited for; matrix products, arithmetic and copies ran while one was open for 0% of the time, Pallas kernels for 21%

profile of v11, /device:TPU:0, one launch (start us, length us, event | category | flops | bytes accessed | tf_op | source)
XLA Modules:
  0.0 31.7 jit_solution(8543406527134961393)
XLA Ops:
  0.0 0.0 copy-start.5
  0.0 0.0 copy-start.4
  0.0 0.0 copy-start.3
  0.0 0.0 copy-start.2
  0.0 0.0 copy-start.1
  0.0 0.0 copy-start
  0.0 7.4 %all-to-all-start = ((f32[8,128,128]{2,1,0:T(8,128)}), f32[8,128,128]{2,1,0:T(8,128)S(1)}, u32[]{:S(2)}, u32[]{:S(2)}) async-start(f32[8,128,128]{2,1,0:T(8,128)} %bitcast.20), calls=%async_computation | async-start | bytes 1048576 | tf_op jit(solution)/shard_map/all_to_all | solution.py:324
  7.5 14.5 %all-to-all-done.came = f32[8,128,128]{2,1,0:T(8,128)S(1)} async-done(((f32[8,128,128]{2,1,0:T(8,128)}), f32[8,128,128]{2,1,0:T(8,128)S(1)}, u32[]{:S(2)}, u32[]{:S(2)}) %all-to-all-start) | async-done | bytes 524320 | tf_op jit(solution)/shard_map/all_to_all | solution.py:324
  22.0 0.1 collective-permute-start
  22.1 0.0 copy-done.5
  22.1 0.0 copy-done.4
  22.1 0.0 copy-done.3
  22.1 0.0 copy-done.2
  22.1 0.0 copy-done.1
  22.1 0.0 copy-done
  22.1 6.6 %tables.1 = (bf16[5,2,256,256]{3,2,1,0:T(8,128)(2,1)S(1)}, bf16[2,128,128]{2,1,0:T(8,128)(2,1)S(1)}, s32[6,512,128]{2,1,0:T(8,128)S(1)}, f32[8,128]{1,0:T(8,128)S(1)}) custom-call(bf16[6,2,128,128]{3,2,1,0:T(8,128)(2,1)S(1)} %copy-done, s32[6,2,8]{2,1,0:T(2,128)S(1)} %bitcast.18, f32[6,8]{1,0:T(8,128)S(1)} %copy-done.2, s32[2,6]{1,0:T(2,128)S(1)} %bitcast.19, ...), custom_call_target="tpu_custom_call" | custom-call | flops 39321600 | bytes 1572864 | tf_op jit(solution)/shard_map/tables/pallas_call | solution.py:332
  28.7 0.0 collective-permute-done.taken
  28.7 3.1 %layers.1 = f32[4,2,2,2,32,128]{5,4,3,2,1,0:T(8,128)} custom-call(f32[8,128,128]{2,1,0:T(8,128)S(1)} %all-to-all-done.came, f32[8,64,128]{2,1,0:T(8,128)S(1)} %collective-permute-done.taken, bf16[5,2,256,256]{3,2,1,0:T(8,128)(2,1)S(1)} %get-tuple-element.9.near, bf16[2,128,128]{2,1,0:T(8,128)(2,1)S(1)} %get-tuple-element.10.last, ...), custom_call_target="tpu_custom_call" | custom-call | tf_op jit(solution)/shard_map/layers/pallas_call | solution.py:347
  (1 shorter events, 0.0 us)
Async XLA Ops:
  0.0 22.1 %copy-start.5 = (s32[6]{0:T(128)S(1)}, s32[6]{0:T(128)}, u32[]{:S(2)}) copy-start(s32[6]{0:T(128)} %path_index.1) | copy-start | bytes 76
  0.0 22.1 %copy-start.4 = (f32[6]{0:T(128)S(1)}, f32[6]{0:T(128)}, u32[]{:S(2)}) copy-start(f32[6]{0:T(128)} %cut_angle.1) | copy-start | bytes 76
  0.0 22.1 %copy-start.3 = (s32[6,2]{0,1:T(2,128)S(1)}, s32[6,2]{0,1:T(2,128)}, u32[]{:S(2)}) copy-start(s32[6,2]{0,1:T(2,128)} %param.11) | copy-start | bytes 148
  0.0 22.1 %copy-start.2 = (f32[6,8]{1,0:T(8,128)S(1)}, f32[6,8]{1,0:T(8,128)}, u32[]{:S(2)}) copy-start(f32[6,8]{1,0:T(8,128)} %pair_angles.1) | copy-start | bytes 580
  0.0 22.1 %copy-start.1 = (s32[6,8,2]{1,2,0:T(2,128)S(1)}, s32[6,8,2]{1,2,0:T(2,128)}, u32[]{:S(2)}) copy-start(s32[6,8,2]{1,2,0:T(2,128)} %param.9) | copy-start | bytes 1156
  0.0 22.1 %copy-start = (bf16[6,2,128,128]{3,2,1,0:T(8,128)(2,1)S(1)}, bf16[6,2,128,128]{3,2,1,0:T(8,128)(2,1)}, u32[]{:S(2)}) copy-start(bf16[6,2,128,128]{3,2,1,0:T(8,128)(2,1)} %gates.1) | copy-start | bytes 1179652
  0.0 21.9 %all-to-all-start = ((f32[8,128,128]{2,1,0:T(8,128)}), f32[8,128,128]{2,1,0:T(8,128)S(1)}, u32[]{:S(2)}, u32[]{:S(2)}) async-start(f32[8,128,128]{2,1,0:T(8,128)} %bitcast.20), calls=%async_computation | async-start | bytes 1048576 | tf_op jit(solution)/shard_map/all_to_all | solution.py:324
  22.0 6.7 %collective-permute-start = (f32[8,64,128]{2,1,0:T(8,128)S(1)}, f32[8,64,128]{2,1,0:T(8,128)S(1)}, u32[]{:S(2)}, u32[]{:S(2)}) collective-permute-start(f32[8,64,128]{2,1,0:T(8,128)S(1)} %dynamic-slice_bitcast_fusion), channel_id=1, source_target_pairs={{0,1},{1,0},{2,3},{3,2},{4,5},{5,4},{6,7},{7,6},{8,9},{9,8},{10,11... | collective-permute-start | bytes 786440 | tf_op jit(solution)/shard_map/ppermute | solution.py:328

commit v12 on v9

--- a/solution.py
+++ b/solution.py
@@ -236,14 +236,15 @@
                     for size in range(2)
                 ])
         weights = last_here if layer == layers - 1 else near.at[layer]
-        joined = jnp.concatenate([pieces[part][size] for part in range(2) for size in range(2)], axis=0)
-        count = joined.shape[0] // 4
-        sums = []
-        for kind in range(2):
-            each = jnp.dot(joined, weights[kind], preferred_element_type=jnp.float32)
-            sums.append([each[2 * part * count:(2 * part + 1) * count] + each[(2 * part + 1) * count:(2 * part + 2) * count]
-                         for part in range(2)])
-        return [sums[0][0] - sums[1][1], sums[1][0] + sums[0][1]]
+        real, imag = weights[0], weights[1]
+        results = []
+        joined = jnp.concatenate(
+            [jnp.concatenate([pieces[0][size], pieces[1][size]], axis=1) for size in range(2)], axis=0
+        )
+        for upper, lower in ((real, -imag), (imag, real)):
+            both = jnp.dot(joined, jnp.concatenate([upper, lower], axis=0), preferred_element_type=jnp.float32)
+            results.append(both[:both.shape[0] // 2] + both[both.shape[0] // 2:])
+        return results
 
     def turned(layer, half, results):
         order = plan.orders[layer]

time: 26.2 us -> 25.1 us (0.958)
  Pallas kernels: 10.5 us -> 9.41 us
    pallas_call x1, Pallas kernels: 3.95 us -> 2.85 us  [shards(): pl.pallas_call(functools.partial(layers_kernel, plan, rows), out_shape=ja...]
  transfers between devices with their start and end apart: 1 -> 1, of which waited for: 1 -> 1; matrix products, arithmetic and copies ran while one was open for 0% -> 0% of each run, Pallas kernels for 25% -> 27%
where the time goes in v12:
time: 25.1 us; the launch traced here: 24.7 us
  Pallas kernels  9.41 us (37%)
  starting transfers between devices  7.38 us (29%)
  local copies, waits for them, and re-layouts  4.36 us (17%)
  waiting for transfers between devices  3.54 us (14%)
    all_to_all x1, starting transfers between devices, shards(): lax.all_to_all(sent, 'hi', split_axis=0, concat_axis=0, tiled=True)  7.38 us
    pallas_call x1, Pallas kernels, shards(): pl.pallas_call(functools.partial(tables_kernel, plan, rows), out_shape=(j...  6.56 us
    unnamed x12, local copies, waits for them, and re-layouts  4.36 us
    all_to_all x1, waiting for transfers between devices, shards(): lax.all_to_all(sent, 'hi', split_axis=0, concat_axis=0, tiled=True)  3.54 us
    pallas_call x1, Pallas kernels, shards(): pl.pallas_call(functools.partial(layers_kernel, plan, rows), out_shape=ja...  2.85 us
  transfers between devices with their start and end apart: 1, of which 1 were waited for; matrix products, arithmetic and copies ran while one was open for 0% of the time, Pallas kernels for 27%

profile of v12, /device:TPU:0, one launch (start us, length us, event | category | flops | bytes accessed | tf_op | source)
XLA Modules:
  0.0 24.7 jit_solution(4097411301843220338)
XLA Ops:
  0.0 7.4 %all-to-all-start = ((f32[16,64,128]{2,1,0:T(8,128)}), f32[16,64,128]{2,1,0:T(8,128)S(1)}, u32[]{:S(2)}, u32[]{:S(2)}) async-start(f32[16,64,128]{2,1,0:T(8,128)} %bitcast.16), calls=%async_computation | async-start | bytes 1048576 | tf_op jit(solution)/shard_map/all_to_all | solution.py:310
  7.4 0.0 copy-start
  7.4 1.0 %copy-done = bf16[6,2,128,128]{3,2,1,0:T(8,128)(2,1)S(1)} copy-done((bf16[6,2,128,128]{3,2,1,0:T(8,128)(2,1)S(1)}, bf16[6,2,128,128]{3,2,1,0:T(8,128)(2,1)}, u32[]{:S(2)}) %copy-start) | copy-done | bytes 393240
  8.4 0.0 copy-start.1
  8.4 0.7 %copy-done.1 = s32[6,8,2]{1,2,0:T(2,128)S(1)} copy-done((s32[6,8,2]{1,2,0:T(2,128)S(1)}, s32[6,8,2]{1,2,0:T(2,128)}, u32[]{:S(2)}) %copy-start.1) | copy-done | bytes 408
  9.1 0.0 copy-start.2
  9.1 0.7 %copy-done.2 = f32[6,8]{1,0:T(8,128)S(1)} copy-done((f32[6,8]{1,0:T(8,128)S(1)}, f32[6,8]{1,0:T(8,128)}, u32[]{:S(2)}) %copy-start.2) | copy-done | bytes 216
  9.8 0.0 copy-start.3
  9.8 0.7 %copy-done.3 = s32[6,2]{0,1:T(2,128)S(1)} copy-done((s32[6,2]{0,1:T(2,128)S(1)}, s32[6,2]{0,1:T(2,128)}, u32[]{:S(2)}) %copy-start.3) | copy-done | bytes 72
  10.5 0.0 copy-start.4
  10.5 0.7 %copy-done.4 = f32[6]{0:T(128)S(1)} copy-done((f32[6]{0:T(128)S(1)}, f32[6]{0:T(128)}, u32[]{:S(2)}) %copy-start.4) | copy-done | bytes 48
  11.1 0.0 copy-start.5
  11.1 0.7 %copy-done.5 = s32[6]{0:T(128)S(1)} copy-done((s32[6]{0:T(128)S(1)}, s32[6]{0:T(128)}, u32[]{:S(2)}) %copy-start.5) | copy-done | bytes 48
  11.8 6.6 %tables.1 = (bf16[5,2,256,256]{3,2,1,0:T(8,128)(2,1)S(1)}, bf16[2,128,128]{2,1,0:T(8,128)(2,1)S(1)}, s32[6,512,128]{2,1,0:T(8,128)S(1)}, f32[8,128]{1,0:T(8,128)S(1)}) custom-call(bf16[6,2,128,128]{3,2,1,0:T(8,128)(2,1)S(1)} %copy-done, s32[6,2,8]{2,1,0:T(2,128)S(1)} %bitcast.14, f32[6,8]{1,0:T(8,128)S(1)} %copy-done.2, s32[2,6]{1,0:T(2,128)S(1)} %bitcast.15, ...), custom_call_target="tpu_custom_call" | custom-call | flops 39321600 | bytes 1572864 | tf_op jit(solution)/shard_map/tables/pallas_call | solution.py:314
  18.3 3.5 %all-to-all-done = f32[16,64,128]{2,1,0:T(8,128)S(1)} async-done(((f32[16,64,128]{2,1,0:T(8,128)}), f32[16,64,128]{2,1,0:T(8,128)S(1)}, u32[]{:S(2)}, u32[]{:S(2)}) %all-to-all-start) | async-done | bytes 524320 | tf_op jit(solution)/shard_map/all_to_all | solution.py:310
  21.9 2.9 %layers.1 = f32[4,2,2,2,32,128]{5,4,3,2,1,0:T(8,128)} custom-call(f32[1024,128]{1,0:T(8,128)S(1)} %bitcast.13, bf16[5,2,256,256]{3,2,1,0:T(8,128)(2,1)S(1)} %get-tuple-element.9.near, bf16[2,128,128]{2,1,0:T(8,128)(2,1)S(1)} %get-tuple-element.10.last, s32[6,512,128]{2,1,0:T(8,128)S(1)} %get-tuple-element.11.phases, f32[8,128]{1,0:T(8,128)S(1)} %get-tuple-element.12.sizes), custom_call_target="tpu_custom_call" | custom-call | tf_op jit(solution)/shard_map/layers/pallas_call | solution.py:329
Async XLA Ops:
  0.0 21.9 %all-to-all-start = ((f32[16,64,128]{2,1,0:T(8,128)}), f32[16,64,128]{2,1,0:T(8,128)S(1)}, u32[]{:S(2)}, u32[]{:S(2)}) async-start(f32[16,64,128]{2,1,0:T(8,128)} %bitcast.16), calls=%async_computation | async-start | bytes 1048576 | tf_op jit(solution)/shard_map/all_to_all | solution.py:310
  7.4 1.0 %copy-start = (bf16[6,2,128,128]{3,2,1,0:T(8,128)(2,1)S(1)}, bf16[6,2,128,128]{3,2,1,0:T(8,128)(2,1)}, u32[]{:S(2)}) copy-start(bf16[6,2,128,128]{3,2,1,0:T(8,128)(2,1)} %gates.1) | copy-start | bytes 1179652
  8.4 0.7 %copy-start.1 = (s32[6,8,2]{1,2,0:T(2,128)S(1)}, s32[6,8,2]{1,2,0:T(2,128)}, u32[]{:S(2)}) copy-start(s32[6,8,2]{1,2,0:T(2,128)} %param.9) | copy-start | bytes 1156
  9.1 0.7 %copy-start.2 = (f32[6,8]{1,0:T(8,128)S(1)}, f32[6,8]{1,0:T(8,128)}, u32[]{:S(2)}) copy-start(f32[6,8]{1,0:T(8,128)} %pair_angles.1) | copy-start | bytes 580
  9.8 0.7 %copy-start.3 = (s32[6,2]{0,1:T(2,128)S(1)}, s32[6,2]{0,1:T(2,128)}, u32[]{:S(2)}) copy-start(s32[6,2]{0,1:T(2,128)} %param.11) | copy-start | bytes 148
  10.5 0.7 %copy-start.4 = (f32[6]{0:T(128)S(1)}, f32[6]{0:T(128)}, u32[]{:S(2)}) copy-start(f32[6]{0:T(128)} %cut_angle.1) | copy-start | bytes 76
  11.1 0.7 %copy-start.5 = (s32[6]{0:T(128)S(1)}, s32[6]{0:T(128)}, u32[]{:S(2)}) copy-start(s32[6]{0:T(128)} %path_index.1) | copy-start | bytes 76

commit v13 on v12

--- a/solution.py
+++ b/solution.py
@@ -237,13 +237,15 @@
                 ])
         weights = last_here if layer == layers - 1 else near.at[layer]
         real, imag = weights[0], weights[1]
-        results = []
         joined = jnp.concatenate(
             [jnp.concatenate([pieces[0][size], pieces[1][size]], axis=1) for size in range(2)], axis=0
         )
-        for upper, lower in ((real, -imag), (imag, real)):
-            both = jnp.dot(joined, jnp.concatenate([upper, lower], axis=0), preferred_element_type=jnp.float32)
-            results.append(both[:both.shape[0] // 2] + both[both.shape[0] // 2:])
+        weight = jnp.concatenate(
+            [jnp.concatenate([real, imag], axis=1), jnp.concatenate([-imag, real], axis=1)], axis=0
+        )
+        both = jnp.dot(joined, weight, preferred_element_type=jnp.float32)
+        total = both[:both.shape[0] // 2] + both[both.shape[0] // 2:]
+        results = [total[:, :256], total[:, 256:]]
         return results
 
     def turned(layer, half, results):

time: 25.1 us -> 25.1 us (level)
  no operation moved by 1% of the time
where the time goes in v13:
time: 25.1 us; the launch traced here: 24.7 us
  Pallas kernels  9.41 us (37%)
  starting transfers between devices  7.38 us (29%)
  local copies, waits for them, and re-layouts  4.36 us (17%)
  waiting for transfers between devices  3.54 us (14%)
    all_to_all x1, starting transfers between devices, shards(): lax.all_to_all(sent, 'hi', split_axis=0, concat_axis=0, tiled=True)  7.38 us
    pallas_call x1, Pallas kernels, shards(): pl.pallas_call(functools.partial(tables_kernel, plan, rows), out_shape=(j...  6.56 us
    unnamed x12, local copies, waits for them, and re-layouts  4.36 us
    all_to_all x1, waiting for transfers between devices, shards(): lax.all_to_all(sent, 'hi', split_axis=0, concat_axis=0, tiled=True)  3.54 us
    pallas_call x1, Pallas kernels, shards(): pl.pallas_call(functools.partial(layers_kernel, plan, rows), out_shape=ja...  2.85 us
  transfers between devices with their start and end apart: 1, of which 1 were waited for; matrix products, arithmetic and copies ran while one was open for 0% of the time, Pallas kernels for 27%

profile of v13, /device:TPU:0, one launch (start us, length us, event | category | flops | bytes accessed | tf_op | source)
XLA Modules:
  0.0 24.7 jit_solution(4097411301843220338)
XLA Ops:
  0.0 7.4 %all-to-all-start = ((f32[16,64,128]{2,1,0:T(8,128)}), f32[16,64,128]{2,1,0:T(8,128)S(1)}, u32[]{:S(2)}, u32[]{:S(2)}) async-start(f32[16,64,128]{2,1,0:T(8,128)} %bitcast.16), calls=%async_computation | async-start | bytes 1048576 | tf_op jit(solution)/shard_map/all_to_all | solution.py:312
  7.4 0.0 copy-start
  7.4 1.0 %copy-done = bf16[6,2,128,128]{3,2,1,0:T(8,128)(2,1)S(1)} copy-done((bf16[6,2,128,128]{3,2,1,0:T(8,128)(2,1)S(1)}, bf16[6,2,128,128]{3,2,1,0:T(8,128)(2,1)}, u32[]{:S(2)}) %copy-start) | copy-done | bytes 393240
  8.4 0.0 copy-start.1
  8.4 0.7 %copy-done.1 = s32[6,8,2]{1,2,0:T(2,128)S(1)} copy-done((s32[6,8,2]{1,2,0:T(2,128)S(1)}, s32[6,8,2]{1,2,0:T(2,128)}, u32[]{:S(2)}) %copy-start.1) | copy-done | bytes 408
  9.1 0.0 copy-start.2
  9.1 0.7 %copy-done.2 = f32[6,8]{1,0:T(8,128)S(1)} copy-done((f32[6,8]{1,0:T(8,128)S(1)}, f32[6,8]{1,0:T(8,128)}, u32[]{:S(2)}) %copy-start.2) | copy-done | bytes 216
  9.8 0.0 copy-start.3
  9.8 0.7 %copy-done.3 = s32[6,2]{0,1:T(2,128)S(1)} copy-done((s32[6,2]{0,1:T(2,128)S(1)}, s32[6,2]{0,1:T(2,128)}, u32[]{:S(2)}) %copy-start.3) | copy-done | bytes 72
  10.5 0.0 copy-start.4
  10.5 0.7 %copy-done.4 = f32[6]{0:T(128)S(1)} copy-done((f32[6]{0:T(128)S(1)}, f32[6]{0:T(128)}, u32[]{:S(2)}) %copy-start.4) | copy-done | bytes 48
  11.1 0.0 copy-start.5
  11.1 0.7 %copy-done.5 = s32[6]{0:T(128)S(1)} copy-done((s32[6]{0:T(128)S(1)}, s32[6]{0:T(128)}, u32[]{:S(2)}) %copy-start.5) | copy-done | bytes 48
  11.8 6.6 %tables.1 = (bf16[5,2,256,256]{3,2,1,0:T(8,128)(2,1)S(1)}, bf16[2,128,128]{2,1,0:T(8,128)(2,1)S(1)}, s32[6,512,128]{2,1,0:T(8,128)S(1)}, f32[8,128]{1,0:T(8,128)S(1)}) custom-call(bf16[6,2,128,128]{3,2,1,0:T(8,128)(2,1)S(1)} %copy-done, s32[6,2,8]{2,1,0:T(2,128)S(1)} %bitcast.14, f32[6,8]{1,0:T(8,128)S(1)} %copy-done.2, s32[2,6]{1,0:T(2,128)S(1)} %bitcast.15, ...), custom_call_target="tpu_custom_call" | custom-call | flops 39321600 | bytes 1572864 | tf_op jit(solution)/shard_map/tables/pallas_call | solution.py:316
  18.3 3.5 %all-to-all-done = f32[16,64,128]{2,1,0:T(8,128)S(1)} async-done(((f32[16,64,128]{2,1,0:T(8,128)}), f32[16,64,128]{2,1,0:T(8,128)S(1)}, u32[]{:S(2)}, u32[]{:S(2)}) %all-to-all-start) | async-done | bytes 524320 | tf_op jit(solution)/shard_map/all_to_all | solution.py:312
  21.9 2.9 %layers.1 = f32[4,2,2,2,32,128]{5,4,3,2,1,0:T(8,128)} custom-call(f32[1024,128]{1,0:T(8,128)S(1)} %bitcast.13, bf16[5,2,256,256]{3,2,1,0:T(8,128)(2,1)S(1)} %get-tuple-element.9.near, bf16[2,128,128]{2,1,0:T(8,128)(2,1)S(1)} %get-tuple-element.10.last, s32[6,512,128]{2,1,0:T(8,128)S(1)} %get-tuple-element.11.phases, f32[8,128]{1,0:T(8,128)S(1)} %get-tuple-element.12.sizes), custom_call_target="tpu_custom_call" | custom-call | tf_op jit(solution)/shard_map/layers/pallas_call | solution.py:331
Async XLA Ops:
  0.0 21.9 %all-to-all-start = ((f32[16,64,128]{2,1,0:T(8,128)}), f32[16,64,128]{2,1,0:T(8,128)S(1)}, u32[]{:S(2)}, u32[]{:S(2)}) async-start(f32[16,64,128]{2,1,0:T(8,128)} %bitcast.16), calls=%async_computation | async-start | bytes 1048576 | tf_op jit(solution)/shard_map/all_to_all | solution.py:312
  7.4 1.0 %copy-start = (bf16[6,2,128,128]{3,2,1,0:T(8,128)(2,1)S(1)}, bf16[6,2,128,128]{3,2,1,0:T(8,128)(2,1)}, u32[]{:S(2)}) copy-start(bf16[6,2,128,128]{3,2,1,0:T(8,128)(2,1)} %gates.1) | copy-start | bytes 1179652
  8.4 0.7 %copy-start.1 = (s32[6,8,2]{1,2,0:T(2,128)S(1)}, s32[6,8,2]{1,2,0:T(2,128)}, u32[]{:S(2)}) copy-start(s32[6,8,2]{1,2,0:T(2,128)} %param.9) | copy-start | bytes 1156
  9.1 0.7 %copy-start.2 = (f32[6,8]{1,0:T(8,128)S(1)}, f32[6,8]{1,0:T(8,128)}, u32[]{:S(2)}) copy-start(f32[6,8]{1,0:T(8,128)} %pair_angles.1) | copy-start | bytes 580
  9.8 0.7 %copy-start.3 = (s32[6,2]{0,1:T(2,128)S(1)}, s32[6,2]{0,1:T(2,128)}, u32[]{:S(2)}) copy-start(s32[6,2]{0,1:T(2,128)} %param.11) | copy-start | bytes 148
  10.5 0.7 %copy-start.4 = (f32[6]{0:T(128)S(1)}, f32[6]{0:T(128)}, u32[]{:S(2)}) copy-start(f32[6]{0:T(128)} %cut_angle.1) | copy-start | bytes 76
  11.1 0.7 %copy-start.5 = (s32[6]{0:T(128)S(1)}, s32[6]{0:T(128)}, u32[]{:S(2)}) copy-start(s32[6]{0:T(128)} %path_index.1) | copy-start | bytes 76
